TPU v7x, 32 devices: a whole 2x2x4 slice. The times are simulated.
32 devices in a mesh: pipe: 4 (over y, core), dp: 4 (over z), tensor: 2 (over x).
Axes of the slice: x: 2, y: 2, z: 4, core: 2. Of those that a mesh axis runs over, the one named last changes fastest.
Arguments:
- activations: bfloat16 [4, 2, 512, 16384], P('pipe', None, 'dp', 'tensor'), may hold values from -6 to 6
- cotangent: bfloat16 [4, 2, 512, 1024], P('pipe', None, 'dp', 'tensor'), may hold values from -0.5 to 0.5
- error_tiles: bfloat16 [4, 4, 2, 2, 1, 128, 128], P('pipe', 'dp', 'tensor'), may hold values from -4 to 4
- tile_picks: int32 [4, 4, 2, 2, 1, 2], P('pipe', None, 'tensor'), may hold values from 0 to 63, as said below
- row_owners: int32 [4, 2, 64], P('pipe', 'tensor'), may hold values from 0 to 63, as said below
Outputs:
- grad_strips: bfloat16 [4, 2, 8192, 1024], P('pipe', 'tensor', 'dp')
Inputs may be any that keep to these rules, and one draw needn't show every extreme that they name: `tile_picks`: for each section, replica and row group, the 2 picked row blocks j have distinct owners row_owners[p, u, j] // 16; c is below 4. Each row_owners[p, u] is a permutation of 0 to 63.
All inputs are finite; a program needn't handle non-finite values.
Results may differ from a plain program's by a relative error of at most 0.001.
Values may be sent and summed in bfloat16 or wider, within the bound.
No kernel may reach another device: no remote copies, remote signals or barrier semaphores. Data moves between devices by JAX's collectives and lax.ppermute only.
A program may use at most 64 MiB of HBM per device.

v0:
```python
import functools

import jax
import jax.numpy as jnp
from jax import lax
from jax.experimental import pallas as pl
from jax.experimental.pallas import tpu as pltpu
from jax.sharding import PartitionSpec as P

VMEM = pl.BlockSpec(memory_space=pltpu.VMEM)
SMEM = pl.BlockSpec(memory_space=pltpu.SMEM)
ANY = pl.BlockSpec(memory_space=pl.ANY)
MOST_STEPS = 8
ROUNDS = {4: [(2, 3, 1, 0), (3, 2, 0, 1), (1, 0, 3, 2)]}
SMALL = pltpu.CompilerParams(vmem_limit_bytes=4 << 20)


def in_hbm(value):
    return pltpu.with_memory_space_constraint(value, pltpu.HBM)


def column(index, edge):
    return pl.ds(pl.multiple_of(index * edge, edge), edge)


def rounds(replicas):
    shifts = [
        tuple((one + step) % replicas for one in range(replicas)) for step in range(1, replicas)
    ]
    return ROUNDS.get(replicas, shifts)


def step_table(replicas):
    table = []
    for source in range(replicas):
        steps = [0] * replicas
        for step, targets in reversed(list(enumerate(rounds(replicas), 1))):
            steps[targets[source]] = step
        table.append(sum(step << 4 * target for target, step in enumerate(steps)))
    return table


def plan_sizes(tiles, steps):
    return 1, 1 + tiles, 1 + 2 * tiles, 1 + 2 * tiles + steps, 1 + 2 * tiles + 2 * steps


def pick(shifts, apart, columns, picks, owners, activations, errors, picked, plan, *refs):
    cuts, (read, seen, copied) = refs[:shifts], refs[shifts:]
    replica, group_at = lax.axis_index("dp"), lax.axis_index("tensor")
    groups, slots, replicas = picks.shape[2], picks.shape[3], picks.shape[-1]
    edge = picked.shape[1]
    tiles = [
        (lax.rem(group_at + shift, groups), slot) for shift in range(groups) for slot in range(slots)
    ]
    reads = []
    for at, (group, slot) in enumerate(tiles):
        block = picks[0, 0, group, slot, 0, replica]
        reads.append(
            pltpu.make_async_copy(
                activations.at[0, :, :, column(block, edge)], read.at[at], copied.at[at]
            )
        )
    for shift, cut in enumerate(cuts):
        other = lax.rem(group_at + groups - shift - 1, groups)
        reads.append(
            pltpu.make_async_copy(errors.at[0, 0, 0, other], cut, copied.at[len(tiles) + shift])
        )
    for copy in reads:
        copy.start()

    owned = owners.shape[-1] // replicas
    per_group = columns // groups
    steps = len(rounds(replicas)) + 1 if apart else replicas
    to_step, to_column, to_row, to_col, end = plan_sizes(len(tiles), steps)
    table = step_table(replicas) if apart else []
    mine = jnp.int32(0)
    for source, packed in enumerate(table):
        mine = jnp.where(replica == source, packed, mine)
    lane = lax.broadcasted_iota(jnp.int32, plan.shape, 1)
    planned = jnp.where((lane >= to_row) & (lane < end), -1, 0)

    for at, (group, slot) in enumerate(tiles):
        row = owners[0, 0, picks[0, 0, group, slot, 0, replica]]
        owner = jnp.int32(0)
        for one in range(1, replicas):
            owner += (row >= one * owned).astype(jnp.int32)
        step = (mine >> 4 * owner) & 15 if apart else owner
        planned = jnp.where(lane == to_step + at, step, planned)
        planned = jnp.where(lane == to_column + at, picks[0, 0, group, slot, 1, replica], planned)

    for origin in range(replicas):
        place_row, place_col = jnp.int32(-1), jnp.int32(0)
        for group, slot in tiles:
            row = owners[0, 0, picks[0, 0, group, slot, 0, origin]] - replica * owned
            here = (row >= 0) & (row < owned)
            place_row = jnp.where(here, row, place_row)
            place_col = jnp.where(
                here, picks[0, 0, group, slot, 1, origin] + group * per_group, place_col
            )
        step = (jnp.int32(table[origin]) >> 4 * replica) & 15 if apart else origin
        planned = jnp.where(lane == to_row + step, place_row, planned)
        planned = jnp.where(lane == to_col + step, place_col, planned)

    meets = jnp.int32(0)
    if apart:
        spots = [
            picks[0, 0, group, slot, 0, origin] * columns
            + picks[0, 0, group, slot, 1, origin]
            + group * per_group
            for group, slot in tiles
            for origin in range(replicas)
        ]
        for spot in spots:
            seen[spot] = 0
        for spot in spots:
            meets = meets | seen[spot]
            seen[spot] = 1
    plan[...] = jnp.where(lane == 0, meets, planned)

    for at, copy in enumerate(reads):
        copy.wait()
        if at < len(tiles):
            picked[at] = read[at].reshape(-1, edge).T


def clear(after, strip, zeros, cleared):
    zeros[...] = jnp.zeros_like(zeros)
    rows = zeros.shape[0]
    writes = [
        pltpu.make_async_copy(zeros, strip.at[0, 0, pl.ds(part * rows, rows)], cleared.at[part])
        for part in range(strip.shape[2] // rows)
    ]
    for write in writes:
        write.start()
    for write in writes:
        write.wait()


def multiply(groups, apart, to_step, to_column, plan, picked, error, *refs):
    returned, carried, outs = refs[:groups], refs[groups : 2 * groups - 1], refs[2 * groups - 1 :]
    mine = lax.axis_index("tensor")
    slots, (edge, tokens) = error.shape[4], picked.shape[1:]
    for shift in range(groups):
        for slot in range(slots):
            at = shift * slots + slot
            right = returned[shift][0, :, :, column(plan[0, to_column + at], edge)]
            extra = error[0, 0, 0, mine, slot] if shift == 0 else carried[shift - 1][slot]
            tile = jnp.dot(
                picked[at], right.reshape(tokens, edge), preferred_element_type=jnp.float32
            )
            tile = tile + extra.astype(jnp.float32)
            step = plan[0, to_step + at]
            if apart:
                outs[0][at] = tile
                store(tile.astype(jnp.bfloat16), step, outs[1:])
            else:
                outs[0][step] = tile


def store(tile, step, buffers):
    for at, buffer in enumerate(buffers):

        @pl.when(step == at)
        def _():
            buffer[...] = tile


def spread(to_step, plan, tiles, *buffers):
    for at in range(tiles.shape[0]):
        store(tiles[at], plan[0, to_step + at], buffers)


def place(count, alone, to_row, to_col, plan, *refs):
    blocks, strip, staged, sent = refs[:count], refs[-3], refs[-2], refs[-1]
    steps, edge = staged.shape[0], staged.shape[-1]

    rows = [plan[0, to_row + step] for step in range(steps)]
    cols = [plan[0, to_col + step] for step in range(steps)]

    def meets(one, other):
        return (rows[one] == rows[other]) & (cols[one] == cols[other])

    def block_of(step):
        return blocks[0][step] if count == 1 else blocks[step][...]

    def first_of(step):
        first = rows[step] >= 0
        for earlier in range(0 if alone else step):
            first = first & jnp.logical_not(meets(earlier, step))
        return first

    def write_of(step):
        return pltpu.make_async_copy(
            blocks[step] if alone else staged.at[step],
            strip.at[0, 0, column(rows[step], edge), column(cols[step], edge)],
            sent.at[step],
        )

    for step in range(steps):

        @pl.when(first_of(step))
        def _():
            if not alone:
                total = block_of(step)
                for later in range(step + 1, steps):
                    total = total + jnp.where(meets(step, later), block_of(later), 0.0)
                staged[step] = total.astype(staged.dtype)
            write_of(step).start()

    for step in range(steps):

        @pl.when(first_of(step))
        def _():
            write_of(step).wait()


def body(mesh, activations, cotangent, error_tiles, tile_picks, row_owners):
    sections, replicas, groups = mesh.shape["pipe"], mesh.shape["dp"], mesh.shape["tensor"]
    edge = error_tiles.shape[-1]
    slots = tile_picks.shape[4]
    micro, tokens = activations.shape[1:3]
    width = cotangent.shape[-1] * groups
    strip_rows = row_owners.shape[-1] // replicas * edge
    picks = jnp.transpose(tile_picks, (0, 2, 3, 4, 5, 1))

    returned = []
    for shift in range(groups):
        pairs = [
            (
                (section + 1) % sections * groups + (group + shift) % groups,
                section * groups + group,
            )
            for section in range(sections)
            for group in range(groups)
        ]
        returned.append(lax.ppermute(cotangent, ("pipe", "tensor"), pairs))
    apart = replicas <= MOST_STEPS
    tiles, shifts = groups * slots, groups - 1
    steps = len(rounds(replicas)) + 1 if apart else replicas
    picked, plan, *errors = pl.pallas_call(
        functools.partial(pick, shifts, apart, width // edge),
        out_shape=[
            pltpu.VMEM((tiles, edge, micro * tokens), activations.dtype),
            pltpu.VMEM((1, -(-plan_sizes(tiles, steps)[-1] // 128) * 128), jnp.int32),
        ]
        + [pltpu.VMEM((slots, edge, edge), error_tiles.dtype)] * shifts,
        in_specs=[SMEM, SMEM, ANY, ANY],
        out_specs=[VMEM] * (2 + shifts),
        scratch_shapes=[
            pltpu.VMEM((tiles, micro, tokens, edge), activations.dtype),
            pltpu.SMEM((row_owners.shape[-1] * (width // edge),), jnp.int32),
            pltpu.SemaphoreType.DMA((tiles + shifts,)),
        ],
        compiler_params=SMALL,
        name="pick",
    )(in_hbm(picks), in_hbm(row_owners), in_hbm(activations), in_hbm(error_tiles))
    carried = [
        lax.ppermute(
            error, "tensor", [((group + shift + 1) % groups, group) for group in range(groups)]
        )
        for shift, error in enumerate(errors)
    ]

    zero_rows = min(strip_rows, 256)
    strip_shape = (1, 1, strip_rows, width)
    cleared = pl.pallas_call(
        clear,
        out_shape=pltpu.HBM(strip_shape, jnp.bfloat16),
        in_specs=[ANY],
        out_specs=pl.BlockSpec(memory_space=pltpu.HBM),
        scratch_shapes=[
            pltpu.VMEM((zero_rows, width), jnp.bfloat16),
            pltpu.SemaphoreType.DMA((strip_rows // zero_rows,)),
        ],
        compiler_params=SMALL,
        cost_estimate=pl.CostEstimate(
            flops=0, bytes_accessed=2 * strip_rows * width, transcendentals=0
        ),
        name="clear",
    )(picked)

    to_step, to_column, to_row, to_col, _ = plan_sizes(tiles, steps)
    tile_shape = (edge, edge)
    if apart:
        out_shape = [jax.ShapeDtypeStruct((tiles,) + tile_shape, jnp.float32)]
        out_shape += [jax.ShapeDtypeStruct(tile_shape, jnp.bfloat16)] * steps
    else:
        out_shape = [jax.ShapeDtypeStruct((replicas,) + tile_shape, jnp.float32)]
    outgoing = pl.pallas_call(
        functools.partial(multiply, groups, apart, to_step, to_column),
        out_shape=out_shape,
        in_specs=[VMEM] * (2 * groups + 2),
        out_specs=[VMEM] * len(out_shape),
        compiler_params=SMALL,
        name="multiply",
    )(plan, picked, error_tiles, *returned, *carried)

    def placed(alone, incoming):
        return pl.pallas_call(
            functools.partial(place, len(incoming), alone, to_row, to_col),
            out_shape=jax.ShapeDtypeStruct(strip_shape, jnp.bfloat16),
            in_specs=[VMEM] * (1 + len(incoming)) + [ANY],
            out_specs=ANY,
            scratch_shapes=[
                pltpu.VMEM((steps,) + tile_shape, jnp.bfloat16),
                pltpu.SemaphoreType.DMA((steps,)),
            ],
            input_output_aliases={1 + len(incoming): 0},
            compiler_params=SMALL,
            name="place",
        )(plan, *incoming, cleared)

    def exchanged(blocks):
        moved = [
            lax.ppermute(block, "dp", list(enumerate(targets)))
            for block, targets in zip(blocks[1:], rounds(replicas))
        ]
        return [blocks[0], *moved]

    def in_full():
        blocks = pl.pallas_call(
            functools.partial(spread, to_step),
            out_shape=[jax.ShapeDtypeStruct(tile_shape, jnp.float32)] * steps,
            in_specs=[VMEM, VMEM],
            out_specs=[VMEM] * steps,
            compiler_params=SMALL,
            name="spread",
        )(plan, outgoing[0])
        return placed(False, exchanged(blocks))

    if not apart:
        swapped = lax.all_to_all(outgoing[0], "dp", split_axis=0, concat_axis=0, tiled=True)
        return placed(False, [swapped])
    return lax.cond(plan[0, 0] > 0, in_full, lambda: placed(True, exchanged(outgoing[1:])))


def solution(mesh):
    in_specs = (
        P("pipe", None, "dp", "tensor"),
        P("pipe", None, "dp", "tensor"),
        P("pipe", "dp", "tensor", None, None, None, None),
        P("pipe", None, "tensor", None, None, None),
        P("pipe", "tensor", None),
    )
    out_specs = P("pipe", "tensor", "dp", None)
    return jax.shard_map(
        functools.partial(body, mesh),
        mesh=mesh,
        in_specs=in_specs,
        out_specs=out_specs,
        check_vma=False,
    )
```

profile of v0, /device:TPU:0, one launch (start us, length us, event | category | flops | bytes accessed | tf_op | source)
XLA Modules:
  0.0 20.1 jit_solution(17534086924162466566)
XLA Ops:
  0.0 3.3 %collective-permute-start.7 = (bf16[1,2,128,512]{3,2,1,0:T(8,128)(2,1)}, bf16[1,2,128,512]{3,2,1,0:T(8,128)(2,1)S(1)}, u32[]{:S(2)}, u32[]{:S(2)}) collective-permute-start(bf16[1,2,128,512]{3,2,1,0:T(8,128)(2,1)} %param.8), channel_id=1, source_target_pairs={{9,0},{8,1},{17,8},{16,9},{25,16},{24,17},{1,24},{0,25},{11,2},{10... | collective-permute-start | bytes 786440 | tf_op jit(solution)/shard_map/ppermute | solution.py:236
  3.3 0.8 %collective-permute-start.6 = (bf16[1,2,128,512]{3,2,1,0:T(8,128)(2,1)}, bf16[1,2,128,512]{3,2,1,0:T(8,128)(2,1)S(1)}, u32[]{:S(2)}, u32[]{:S(2)}) collective-permute-start(bf16[1,2,128,512]{3,2,1,0:T(8,128)(2,1)} %param.8), channel_id=1, source_target_pairs={{8,0},{9,1},{16,8},{17,9},{24,16},{25,17},{0,24},{1,25},{10,2},{11... | collective-permute-start | bytes 786440 | tf_op jit(solution)/shard_map/ppermute | solution.py:236
  4.2 0.0 copy-start
  4.2 1.9 %pick.1 = (bf16[2,128,256]{2,1,0:T(8,128)(2,1)S(1)}, s32[1,128]{1,0:T(1,128)S(1)}, bf16[1,128,128]{2,1,0:T(8,128)(2,1)S(1)}) custom-call(s32[1,1,2,1,2,4]{5,4,3,2,1,0:T(2,128)} %bitcast.4, s32[1,1,64]{2,1,0:T(1,128)} %owners.1, bf16[1,2,128,8192]{3,2,1,0:T(8,128)(2,1)} %activations.1, bf16[1,1,1,2,1,128,128]{6,5,4,3,2,1,0:T(8,128)(2,1)} %error.1), custom_call_target="tpu_custom_call" | custom-call | tf_op jit(solution)/shard_map/pick/pallas_call | solution.py:240
  6.0 0.6 %collective-permute-start.8 = (bf16[1,128,128]{2,1,0:T(8,128)(2,1)S(1)}, bf16[1,128,128]{2,1,0:T(8,128)(2,1)S(1)}, u32[]{:S(2)}, u32[]{:S(2)}) collective-permute-start(bf16[1,128,128]{2,1,0:T(8,128)(2,1)S(1)} %get-tuple-element.49), channel_id=1, source_target_pairs={{1,0},{0,1},{3,2},{2,3},{5,4},{4,5},{7,6},{6,7},{9,8},{8,9},{11,10... | collective-permute-start | bytes 98312 | tf_op jit(solution)/shard_map/ppermute | solution.py:258
  6.7 2.1 %clear.1 = bf16[1,1,2048,1024]{3,2,1,0:T(8,128)(2,1)} custom-call(bf16[2,128,256]{2,1,0:T(8,128)(2,1)S(1)} %get-tuple-element.48.picked.after), custom_call_target="tpu_custom_call" | custom-call | bytes 4194304 | tf_op jit(solution)/shard_map/clear/pallas_call | solution.py:266
  8.8 1.4 %collective-permute-done.8.refs_2_ = bf16[1,128,128]{2,1,0:T(8,128)(2,1)S(1)} collective-permute-done((bf16[1,128,128]{2,1,0:T(8,128)(2,1)S(1)}, bf16[1,128,128]{2,1,0:T(8,128)(2,1)S(1)}, u32[]{:S(2)}, u32[]{:S(2)}) %collective-permute-start.8) | collective-permute-done | bytes 32800 | tf_op jit(solution)/shard_map/ppermute | solution.py:258
  10.2 0.0 collective-permute-done.7.refs_1_
  10.2 0.6 %collective-permute-done.6.refs_0_ = bf16[1,2,128,512]{3,2,1,0:T(8,128)(2,1)S(1)} collective-permute-done((bf16[1,2,128,512]{3,2,1,0:T(8,128)(2,1)}, bf16[1,2,128,512]{3,2,1,0:T(8,128)(2,1)S(1)}, u32[]{:S(2)}, u32[]{:S(2)}) %collective-permute-start.6) | collective-permute-done | bytes 262176 | tf_op jit(solution)/shard_map/ppermute | solution.py:236
  10.8 0.0 copy-done
  10.8 0.6 %multiply.1 = (f32[2,128,128]{2,1,0:T(8,128)S(1)}, bf16[128,128]{1,0:T(8,128)(2,1)S(1)}, bf16[128,128]{1,0:T(8,128)(2,1)S(1)}, bf16[128,128]{1,0:T(8,128)(2,1)S(1)}, bf16[128,128]{1,0:T(8,128)(2,1)S(1)}) custom-call(s32[1,128]{1,0:T(1,128)S(1)} %get-tuple-element.47.plan, bf16[2,128,256]{2,1,0:T(8,128)(2,1)S(1)} %get-tuple-element.48.picked.after, ...), custom_call_target="tpu_custom_call" | custom-call | tf_op jit(solution)/shard_map/multiply/pallas_call | solution.py:289
  11.4 8.8 %conditional.1 = (bf16[1,1,2048,1024]{3,2,1,0:T(8,128)(2,1)}) conditional(s32[]{:T(128)} %bitcast.1, (bf16[128,128]{1,0:T(8,128)(2,1)S(1)}, bf16[128,128]{1,0:T(8,128)(2,1)S(1)}, bf16[128,128]{1,0:T(8,128)(2,1)S(1)}, s32[1,128]{1,0:T(1,128)S(1)}, bf16[128,128]{1,0:T(8,128)(2,1)S(1)}, /*index=5*/bf16[1,1,2048,1024]{3,2,1,0:T(8,128)(2,1)}) %tuple.11, ...), branch_computations={%region_0.0_spmd, %region_1.0_spmd} | conditional | bytes 786560 | solution.py:334
  11.4 2.8 %collective-permute-start = (bf16[128,128]{1,0:T(8,128)(2,1)S(1)}, bf16[128,128]{1,0:T(8,128)(2,1)S(1)}, u32[]{:S(2)}, u32[]{:S(2)}) collective-permute-start(bf16[128,128]{1,0:T(8,128)(2,1)S(1)} %get-tuple-element.28), channel_id=1, source_target_pairs={{0,4},{2,6},{4,2},{6,0},{1,5},{3,7},{5,3},{7,1},{8,12},{10,14},{12... | collective-permute-start | bytes 98312 | tf_op jit(solution)/shard_map/cond/branch_0_fun/ppermute | solution.py:315
  14.2 1.1 %collective-permute-start.1 = (bf16[128,128]{1,0:T(8,128)(2,1)S(1)}, bf16[128,128]{1,0:T(8,128)(2,1)S(1)}, u32[]{:S(2)}, u32[]{:S(2)}) collective-permute-start(bf16[128,128]{1,0:T(8,128)(2,1)S(1)} %get-tuple-element.29), channel_id=1, source_target_pairs={{0,6},{2,4},{4,0},{6,2},{1,7},{3,5},{5,1},{7,3},{8,14},{10,12},{12... | collective-permute-start | bytes 98312 | tf_op jit(solution)/shard_map/cond/branch_0_fun/ppermute | solution.py:315
  15.3 0.5 %collective-permute-start.2 = (bf16[128,128]{1,0:T(8,128)(2,1)S(1)}, bf16[128,128]{1,0:T(8,128)(2,1)S(1)}, u32[]{:S(2)}, u32[]{:S(2)}) collective-permute-start(bf16[128,128]{1,0:T(8,128)(2,1)S(1)} %get-tuple-element.30), channel_id=1, source_target_pairs={{0,2},{2,0},{4,6},{6,4},{1,3},{3,1},{5,7},{7,5},{8,10},{10,8},{12,... | collective-permute-start | bytes 98312 | tf_op jit(solution)/shard_map/cond/branch_0_fun/ppermute | solution.py:315
  15.8 1.5 %collective-permute-done.refs_1_ = bf16[128,128]{1,0:T(8,128)(2,1)S(1)} collective-permute-done((bf16[128,128]{1,0:T(8,128)(2,1)S(1)}, bf16[128,128]{1,0:T(8,128)(2,1)S(1)}, u32[]{:S(2)}, u32[]{:S(2)}) %collective-permute-start) | collective-permute-done | bytes 32800 | tf_op jit(solution)/shard_map/cond/branch_0_fun/ppermute | solution.py:315
  17.3 1.8 %collective-permute-done.1.refs_2_ = bf16[128,128]{1,0:T(8,128)(2,1)S(1)} collective-permute-done((bf16[128,128]{1,0:T(8,128)(2,1)S(1)}, bf16[128,128]{1,0:T(8,128)(2,1)S(1)}, u32[]{:S(2)}, u32[]{:S(2)}) %collective-permute-start.1) | collective-permute-done | bytes 32800 | tf_op jit(solution)/shard_map/cond/branch_0_fun/ppermute | solution.py:315
  19.0 0.3 %collective-permute-done.2.refs_3_ = bf16[128,128]{1,0:T(8,128)(2,1)S(1)} collective-permute-done((bf16[128,128]{1,0:T(8,128)(2,1)S(1)}, bf16[128,128]{1,0:T(8,128)(2,1)S(1)}, u32[]{:S(2)}, u32[]{:S(2)}) %collective-permute-start.2) | collective-permute-done | bytes 32800 | tf_op jit(solution)/shard_map/cond/branch_0_fun/ppermute | solution.py:315
  19.4 0.8 %place.2 = bf16[1,1,2048,1024]{3,2,1,0:T(8,128)(2,1)} custom-call(s32[1,128]{1,0:T(1,128)S(1)} %get-tuple-element.26.plan, bf16[128,128]{1,0:T(8,128)(2,1)S(1)} %get-tuple-element.27.refs_0_, bf16[128,128]{1,0:T(8,128)(2,1)S(1)} %collective-permute-done.refs_1_, bf16[128,128]{1,0:T(8,128)(2,1)S(1)} %collective-permute-done.1.refs_2_, ...), custom_call_target="tpu_custom_call", output_to_operand_aliasing={{}: (5, {})} | custom-call | tf_op jit(solution)/shard_map/cond/branch_0_fun/place/pallas_call | solution.py:299
Async XLA Ops:
  0.0 10.2 %collective-permute-start.7 = (bf16[1,2,128,512]{3,2,1,0:T(8,128)(2,1)}, bf16[1,2,128,512]{3,2,1,0:T(8,128)(2,1)S(1)}, u32[]{:S(2)}, u32[]{:S(2)}) collective-permute-start(bf16[1,2,128,512]{3,2,1,0:T(8,128)(2,1)} %param.8), channel_id=1, source_target_pairs={{9,0},{8,1},{17,8},{16,9},{25,16},{24,17},{1,24},{0,25},{11,2},{10... | collective-permute-start | bytes 786440 | tf_op jit(solution)/shard_map/ppermute | solution.py:236
  3.3 7.5 %collective-permute-start.6 = (bf16[1,2,128,512]{3,2,1,0:T(8,128)(2,1)}, bf16[1,2,128,512]{3,2,1,0:T(8,128)(2,1)S(1)}, u32[]{:S(2)}, u32[]{:S(2)}) collective-permute-start(bf16[1,2,128,512]{3,2,1,0:T(8,128)(2,1)} %param.8), channel_id=1, source_target_pairs={{8,0},{9,1},{16,8},{17,9},{24,16},{25,17},{0,24},{1,25},{10,2},{11... | collective-permute-start | bytes 786440 | tf_op jit(solution)/shard_map/ppermute | solution.py:236
  4.2 6.6 %copy-start = (bf16[1,1,1,2,1,128,128]{6,5,4,3,2,1,0:T(8,128)(2,1)S(1)}, bf16[1,1,1,2,1,128,128]{6,5,4,3,2,1,0:T(8,128)(2,1)}, u32[]{:S(2)}) copy-start(bf16[1,1,1,2,1,128,128]{6,5,4,3,2,1,0:T(8,128)(2,1)} %error.1) | copy-start | bytes 196612
  6.0 4.1 %collective-permute-start.8 = (bf16[1,128,128]{2,1,0:T(8,128)(2,1)S(1)}, bf16[1,128,128]{2,1,0:T(8,128)(2,1)S(1)}, u32[]{:S(2)}, u32[]{:S(2)}) collective-permute-start(bf16[1,128,128]{2,1,0:T(8,128)(2,1)S(1)} %get-tuple-element.49), channel_id=1, source_target_pairs={{1,0},{0,1},{3,2},{2,3},{5,4},{4,5},{7,6},{6,7},{9,8},{8,9},{11,10... | collective-permute-start | bytes 98312 | tf_op jit(solution)/shard_map/ppermute | solution.py:258
  11.4 5.9 %collective-permute-start = (bf16[128,128]{1,0:T(8,128)(2,1)S(1)}, bf16[128,128]{1,0:T(8,128)(2,1)S(1)}, u32[]{:S(2)}, u32[]{:S(2)}) collective-permute-start(bf16[128,128]{1,0:T(8,128)(2,1)S(1)} %get-tuple-element.28), channel_id=1, source_target_pairs={{0,4},{2,6},{4,2},{6,0},{1,5},{3,7},{5,3},{7,1},{8,12},{10,14},{12... | collective-permute-start | bytes 98312 | tf_op jit(solution)/shard_map/cond/branch_0_fun/ppermute | solution.py:315
  14.2 4.8 %collective-permute-start.1 = (bf16[128,128]{1,0:T(8,128)(2,1)S(1)}, bf16[128,128]{1,0:T(8,128)(2,1)S(1)}, u32[]{:S(2)}, u32[]{:S(2)}) collective-permute-start(bf16[128,128]{1,0:T(8,128)(2,1)S(1)} %get-tuple-element.29), channel_id=1, source_target_pairs={{0,6},{2,4},{4,0},{6,2},{1,7},{3,5},{5,1},{7,3},{8,14},{10,12},{12... | collective-permute-start | bytes 98312 | tf_op jit(solution)/shard_map/cond/branch_0_fun/ppermute | solution.py:315
  15.3 4.1 %collective-permute-start.2 = (bf16[128,128]{1,0:T(8,128)(2,1)S(1)}, bf16[128,128]{1,0:T(8,128)(2,1)S(1)}, u32[]{:S(2)}, u32[]{:S(2)}) collective-permute-start(bf16[128,128]{1,0:T(8,128)(2,1)S(1)} %get-tuple-element.30), channel_id=1, source_target_pairs={{0,2},{2,0},{4,6},{6,4},{1,3},{3,1},{5,7},{7,5},{8,10},{10,8},{12,... | collective-permute-start | bytes 98312 | tf_op jit(solution)/shard_map/cond/branch_0_fun/ppermute | solution.py:315
where the time goes:
time: 20.3 us; the launch traced here: 20.1 us
  starting transfers between devices  9.18 us (45%)
  waiting for transfers between devices  5.58 us (27%)
  Pallas kernels  5.29 us (26%)
    ppermute x3, starting transfers between devices, exchanged(): lax.ppermute(block, 'dp', list(enumerate(targets)))  4.41 us
    ppermute x2, starting transfers between devices, body(): returned.append(lax.ppermute(cotangent, ('pipe', 'tensor'), pairs))  4.18 us
    ppermute x3, waiting for transfers between devices, exchanged(): lax.ppermute(block, 'dp', list(enumerate(targets)))  3.59 us
    pallas_call x1, Pallas kernels, body(): pl.pallas_call(clear, out_shape=pltpu.HBM(strip_shape, jnp.bfloat16), in_...  2.1 us
    pallas_call x1, Pallas kernels, body(): pl.pallas_call(functools.partial(pick, shifts, apart, width // edge), out...  1.86 us
    ppermute x1, waiting for transfers between devices, body(): lax.ppermute(error, 'tensor', [((group + shift + 1) % groups, group) for...  1.35 us
    pallas_call x1, Pallas kernels, placed(): pl.pallas_call(functools.partial(place, len(incoming), alone, to_row, to_...  0.77 us
    ppermute x2, waiting for transfers between devices, body(): returned.append(lax.ppermute(cotangent, ('pipe', 'tensor'), pairs))  0.64 us
  transfers between devices with their start and end apart: 6, of which 5 were waited for; matrix products, arithmetic and copies ran while one was open for 0% of the time, Pallas kernels for 20%

commit v1 on v0

--- a/solution.py
+++ b/solution.py
@@ -140,34 +140,38 @@
     returned, carried, outs = refs[:groups], refs[groups : 2 * groups - 1], refs[2 * groups - 1 :]
     mine = lax.axis_index("tensor")
     slots, (edge, tokens) = error.shape[4], picked.shape[1:]
+    count = groups * slots
+    meet = plan[0, 0] > 0
+    columns = [plan[0, to_column + at] for at in range(count)]
+    steps = [plan[0, to_step + at] for at in range(count)]
+    tiles = []
     for shift in range(groups):
         for slot in range(slots):
             at = shift * slots + slot
-            right = returned[shift][0, :, :, column(plan[0, to_column + at], edge)]
+            right = returned[shift][0, :, :, column(columns[at], edge)].reshape(tokens, edge)
             extra = error[0, 0, 0, mine, slot] if shift == 0 else carried[shift - 1][slot]
-            tile = jnp.dot(
-                picked[at], right.reshape(tokens, edge), preferred_element_type=jnp.float32
-            )
-            tile = tile + extra.astype(jnp.float32)
-            step = plan[0, to_step + at]
-            if apart:
-                outs[0][at] = tile
-                store(tile.astype(jnp.bfloat16), step, outs[1:])
-            else:
-                outs[0][step] = tile
-
-
-def store(tile, step, buffers):
-    for at, buffer in enumerate(buffers):
-
-        @pl.when(step == at)
-        def _():
-            buffer[...] = tile
-
-
-def spread(to_step, plan, tiles, *buffers):
-    for at in range(tiles.shape[0]):
-        store(tiles[at], plan[0, to_step + at], buffers)
+            tile = jnp.dot(picked[at], right, preferred_element_type=jnp.float32)
+            tiles.append(tile + extra.astype(jnp.float32))
+    if not apart:
+        for step, tile in zip(steps, tiles):
+            outs[0][step] = tile
+        return
+
+    def store(buffers):
+        for step, tile in zip(steps, tiles):
+            for at, buffer in enumerate(buffers):
+
+                @pl.when(step == at)
+                def _():
+                    buffer[...] = tile.astype(buffer.dtype)
+
+    @pl.when(meet)
+    def _():
+        store(outs[: len(outs) // 2])
+
+    @pl.when(jnp.logical_not(meet))
+    def _():
+        store(outs[len(outs) // 2 :])
 
 
 def place(count, alone, to_row, to_col, plan, *refs):
@@ -282,8 +286,11 @@
     to_step, to_column, to_row, to_col, _ = plan_sizes(tiles, steps)
     tile_shape = (edge, edge)
     if apart:
-        out_shape = [jax.ShapeDtypeStruct((tiles,) + tile_shape, jnp.float32)]
-        out_shape += [jax.ShapeDtypeStruct(tile_shape, jnp.bfloat16)] * steps
+        out_shape = [
+            jax.ShapeDtypeStruct(tile_shape, dtype)
+            for dtype in (jnp.float32, jnp.bfloat16)
+            for step in range(steps)
+        ]
     else:
         out_shape = [jax.ShapeDtypeStruct((replicas,) + tile_shape, jnp.float32)]
     outgoing = pl.pallas_call(
@@ -317,21 +324,14 @@
         ]
         return [blocks[0], *moved]
 
-    def in_full():
-        blocks = pl.pallas_call(
-            functools.partial(spread, to_step),
-            out_shape=[jax.ShapeDtypeStruct(tile_shape, jnp.float32)] * steps,
-            in_specs=[VMEM, VMEM],
-            out_specs=[VMEM] * steps,
-            compiler_params=SMALL,
-            name="spread",
-        )(plan, outgoing[0])
-        return placed(False, exchanged(blocks))
-
     if not apart:
         swapped = lax.all_to_all(outgoing[0], "dp", split_axis=0, concat_axis=0, tiled=True)
         return placed(False, [swapped])
-    return lax.cond(plan[0, 0] > 0, in_full, lambda: placed(True, exchanged(outgoing[1:])))
+    return lax.cond(
+        plan[0, 0] > 0,
+        lambda: placed(False, exchanged(outgoing[:steps])),
+        lambda: placed(True, exchanged(outgoing[steps:])),
+    )
 
 
 def solution(mesh):

time: 20.3 us -> 20.1 us (level)
  Pallas kernels: 5.29 us -> 5.05 us
    pallas_call x1, Pallas kernels: 0.55 us -> 0.31 us  [body(): pl.pallas_call(functools.partial(multiply, groups, apart, to_step, to_col...]
where the time goes in v1:
time: 20.1 us; the launch traced here: 19.9 us
  starting transfers between devices  9.18 us (46%)
  waiting for transfers between devices  5.57 us (28%)
  Pallas kernels  5.05 us (25%)
    ppermute x3, starting transfers between devices, exchanged(): lax.ppermute(block, 'dp', list(enumerate(targets)))  4.41 us
    ppermute x2, starting transfers between devices, body(): returned.append(lax.ppermute(cotangent, ('pipe', 'tensor'), pairs))  4.18 us
    ppermute x3, waiting for transfers between devices, exchanged(): lax.ppermute(block, 'dp', list(enumerate(targets)))  3.58 us
    pallas_call x1, Pallas kernels, body(): pl.pallas_call(clear, out_shape=pltpu.HBM(strip_shape, jnp.bfloat16), in_...  2.1 us
    pallas_call x1, Pallas kernels, body(): pl.pallas_call(functools.partial(pick, shifts, apart, width // edge), out...  1.86 us
    ppermute x1, waiting for transfers between devices, body(): lax.ppermute(error, 'tensor', [((group + shift + 1) % groups, group) for...  1.35 us
    pallas_call x1, Pallas kernels, placed(): pl.pallas_call(functools.partial(place, len(incoming), alone, to_row, to_...  0.77 us
    ppermute x2, waiting for transfers between devices, body(): returned.append(lax.ppermute(cotangent, ('pipe', 'tensor'), pairs))  0.64 us
  transfers between devices with their start and end apart: 6, of which 5 were waited for; matrix products, arithmetic and copies ran while one was open for 0% of the time, Pallas kernels for 20%

profile of v1, /device:TPU:0, one launch (start us, length us, event | category | flops | bytes accessed | tf_op | source)
XLA Modules:
  0.0 19.9 jit_solution(13124818076406343884)
XLA Ops:
  0.0 3.3 %collective-permute-start.7 = (bf16[1,2,128,512]{3,2,1,0:T(8,128)(2,1)}, bf16[1,2,128,512]{3,2,1,0:T(8,128)(2,1)S(1)}, u32[]{:S(2)}, u32[]{:S(2)}) collective-permute-start(bf16[1,2,128,512]{3,2,1,0:T(8,128)(2,1)} %param.8), channel_id=1, source_target_pairs={{9,0},{8,1},{17,8},{16,9},{25,16},{24,17},{1,24},{0,25},{11,2},{10... | collective-permute-start | bytes 786440 | tf_op jit(solution)/shard_map/ppermute | solution.py:240
  3.3 0.8 %collective-permute-start.6 = (bf16[1,2,128,512]{3,2,1,0:T(8,128)(2,1)}, bf16[1,2,128,512]{3,2,1,0:T(8,128)(2,1)S(1)}, u32[]{:S(2)}, u32[]{:S(2)}) collective-permute-start(bf16[1,2,128,512]{3,2,1,0:T(8,128)(2,1)} %param.8), channel_id=1, source_target_pairs={{8,0},{9,1},{16,8},{17,9},{24,16},{25,17},{0,24},{1,25},{10,2},{11... | collective-permute-start | bytes 786440 | tf_op jit(solution)/shard_map/ppermute | solution.py:240
  4.2 0.0 copy-start
  4.2 1.9 %pick.1 = (bf16[2,128,256]{2,1,0:T(8,128)(2,1)S(1)}, s32[1,128]{1,0:T(1,128)S(1)}, bf16[1,128,128]{2,1,0:T(8,128)(2,1)S(1)}) custom-call(s32[1,1,2,1,2,4]{5,4,3,2,1,0:T(2,128)} %bitcast.4, s32[1,1,64]{2,1,0:T(1,128)} %owners.1, bf16[1,2,128,8192]{3,2,1,0:T(8,128)(2,1)} %activations.1, bf16[1,1,1,2,1,128,128]{6,5,4,3,2,1,0:T(8,128)(2,1)} %error.1), custom_call_target="tpu_custom_call" | custom-call | tf_op jit(solution)/shard_map/pick/pallas_call | solution.py:244
  6.0 0.6 %collective-permute-start.8 = (bf16[1,128,128]{2,1,0:T(8,128)(2,1)S(1)}, bf16[1,128,128]{2,1,0:T(8,128)(2,1)S(1)}, u32[]{:S(2)}, u32[]{:S(2)}) collective-permute-start(bf16[1,128,128]{2,1,0:T(8,128)(2,1)S(1)} %get-tuple-element.57), channel_id=1, source_target_pairs={{1,0},{0,1},{3,2},{2,3},{5,4},{4,5},{7,6},{6,7},{9,8},{8,9},{11,10... | collective-permute-start | bytes 98312 | tf_op jit(solution)/shard_map/ppermute | solution.py:262
  6.7 2.1 %clear.1 = bf16[1,1,2048,1024]{3,2,1,0:T(8,128)(2,1)} custom-call(bf16[2,128,256]{2,1,0:T(8,128)(2,1)S(1)} %get-tuple-element.56.picked.after), custom_call_target="tpu_custom_call" | custom-call | bytes 4194304 | tf_op jit(solution)/shard_map/clear/pallas_call | solution.py:270
  8.8 1.4 %collective-permute-done.8.refs_2_ = bf16[1,128,128]{2,1,0:T(8,128)(2,1)S(1)} collective-permute-done((bf16[1,128,128]{2,1,0:T(8,128)(2,1)S(1)}, bf16[1,128,128]{2,1,0:T(8,128)(2,1)S(1)}, u32[]{:S(2)}, u32[]{:S(2)}) %collective-permute-start.8) | collective-permute-done | bytes 32800 | tf_op jit(solution)/shard_map/ppermute | solution.py:262
  10.2 0.0 collective-permute-done.7.refs_1_
  10.2 0.6 %collective-permute-done.6.refs_0_ = bf16[1,2,128,512]{3,2,1,0:T(8,128)(2,1)S(1)} collective-permute-done((bf16[1,2,128,512]{3,2,1,0:T(8,128)(2,1)}, bf16[1,2,128,512]{3,2,1,0:T(8,128)(2,1)S(1)}, u32[]{:S(2)}, u32[]{:S(2)}) %collective-permute-start.6) | collective-permute-done | bytes 262176 | tf_op jit(solution)/shard_map/ppermute | solution.py:240
  10.8 0.0 copy-done
  10.8 0.3 %multiply.1 = (f32[128,128]{1,0:T(8,128)S(1)}, f32[128,128]{1,0:T(8,128)S(1)}, f32[128,128]{1,0:T(8,128)S(1)}, f32[128,128]{1,0:T(8,128)S(1)}, bf16[128,128]{1,0...) custom-call(s32[1,128]{1,0:T(1,128)S(1)} %get-tuple-element.55.plan, ...), custom_call_target="tpu_custom_call" | custom-call | tf_op jit(solution)/shard_map/multiply/pallas_call | solution.py:296
  11.1 8.8 %conditional.1 = (bf16[1,1,2048,1024]{3,2,1,0:T(8,128)(2,1)}) conditional(s32[]{:T(128)} %bitcast.1, (bf16[128,128]{1,0:T(8,128)(2,1)S(1)}, bf16[128,128]{1,0:T(8,128)(2,1)S(1)}, bf16[128,128]{1,0:T(8,128)(2,1)S(1)}, s32[1,128]{1,0:T(1,128)S(1)}, bf16[128,128]{1,0:T(8,128)(2,1)S(1)}, /*index=5*/bf16[1,1,2048,1024]{3,2,1,0:T(8,128)(2,1)}) %tuple.11, ...), branch_computations={%region_0.0_spmd, %region_1.0_spmd} | conditional | bytes 786560 | solution.py:330
  11.1 2.8 %collective-permute-start = (bf16[128,128]{1,0:T(8,128)(2,1)S(1)}, bf16[128,128]{1,0:T(8,128)(2,1)S(1)}, u32[]{:S(2)}, u32[]{:S(2)}) collective-permute-start(bf16[128,128]{1,0:T(8,128)(2,1)S(1)} %get-tuple-element.34), channel_id=1, source_target_pairs={{0,4},{2,6},{4,2},{6,0},{1,5},{3,7},{5,3},{7,1},{8,12},{10,14},{12... | collective-permute-start | bytes 98312 | tf_op jit(solution)/shard_map/cond/branch_0_fun/ppermute | solution.py:322
  14.0 1.1 %collective-permute-start.1 = (bf16[128,128]{1,0:T(8,128)(2,1)S(1)}, bf16[128,128]{1,0:T(8,128)(2,1)S(1)}, u32[]{:S(2)}, u32[]{:S(2)}) collective-permute-start(bf16[128,128]{1,0:T(8,128)(2,1)S(1)} %get-tuple-element.35), channel_id=1, source_target_pairs={{0,6},{2,4},{4,0},{6,2},{1,7},{3,5},{5,1},{7,3},{8,14},{10,12},{12... | collective-permute-start | bytes 98312 | tf_op jit(solution)/shard_map/cond/branch_0_fun/ppermute | solution.py:322
  15.0 0.5 %collective-permute-start.2 = (bf16[128,128]{1,0:T(8,128)(2,1)S(1)}, bf16[128,128]{1,0:T(8,128)(2,1)S(1)}, u32[]{:S(2)}, u32[]{:S(2)}) collective-permute-start(bf16[128,128]{1,0:T(8,128)(2,1)S(1)} %get-tuple-element.36), channel_id=1, source_target_pairs={{0,2},{2,0},{4,6},{6,4},{1,3},{3,1},{5,7},{7,5},{8,10},{10,8},{12,... | collective-permute-start | bytes 98312 | tf_op jit(solution)/shard_map/cond/branch_0_fun/ppermute | solution.py:322
  15.5 1.5 %collective-permute-done.refs_1_ = bf16[128,128]{1,0:T(8,128)(2,1)S(1)} collective-permute-done((bf16[128,128]{1,0:T(8,128)(2,1)S(1)}, bf16[128,128]{1,0:T(8,128)(2,1)S(1)}, u32[]{:S(2)}, u32[]{:S(2)}) %collective-permute-start) | collective-permute-done | bytes 32800 | tf_op jit(solution)/shard_map/cond/branch_0_fun/ppermute | solution.py:322
  17.0 1.8 %collective-permute-done.1.refs_2_ = bf16[128,128]{1,0:T(8,128)(2,1)S(1)} collective-permute-done((bf16[128,128]{1,0:T(8,128)(2,1)S(1)}, bf16[128,128]{1,0:T(8,128)(2,1)S(1)}, u32[]{:S(2)}, u32[]{:S(2)}) %collective-permute-start.1) | collective-permute-done | bytes 32800 | tf_op jit(solution)/shard_map/cond/branch_0_fun/ppermute | solution.py:322
  18.8 0.3 %collective-permute-done.2.refs_3_ = bf16[128,128]{1,0:T(8,128)(2,1)S(1)} collective-permute-done((bf16[128,128]{1,0:T(8,128)(2,1)S(1)}, bf16[128,128]{1,0:T(8,128)(2,1)S(1)}, u32[]{:S(2)}, u32[]{:S(2)}) %collective-permute-start.2) | collective-permute-done | bytes 32800 | tf_op jit(solution)/shard_map/cond/branch_0_fun/ppermute | solution.py:322
  19.1 0.8 %place.2 = bf16[1,1,2048,1024]{3,2,1,0:T(8,128)(2,1)} custom-call(s32[1,128]{1,0:T(1,128)S(1)} %get-tuple-element.32.plan, bf16[128,128]{1,0:T(8,128)(2,1)S(1)} %get-tuple-element.33.refs_0_, bf16[128,128]{1,0:T(8,128)(2,1)S(1)} %collective-permute-done.refs_1_, bf16[128,128]{1,0:T(8,128)(2,1)S(1)} %collective-permute-done.1.refs_2_, ...), custom_call_target="tpu_custom_call", output_to_operand_aliasing={{}: (5, {})} | custom-call | tf_op jit(solution)/shard_map/cond/branch_0_fun/place/pallas_call | solution.py:306
Async XLA Ops:
  0.0 10.2 %collective-permute-start.7 = (bf16[1,2,128,512]{3,2,1,0:T(8,128)(2,1)}, bf16[1,2,128,512]{3,2,1,0:T(8,128)(2,1)S(1)}, u32[]{:S(2)}, u32[]{:S(2)}) collective-permute-start(bf16[1,2,128,512]{3,2,1,0:T(8,128)(2,1)} %param.8), channel_id=1, source_target_pairs={{9,0},{8,1},{17,8},{16,9},{25,16},{24,17},{1,24},{0,25},{11,2},{10... | collective-permute-start | bytes 786440 | tf_op jit(solution)/shard_map/ppermute | solution.py:240
  3.3 7.5 %collective-permute-start.6 = (bf16[1,2,128,512]{3,2,1,0:T(8,128)(2,1)}, bf16[1,2,128,512]{3,2,1,0:T(8,128)(2,1)S(1)}, u32[]{:S(2)}, u32[]{:S(2)}) collective-permute-start(bf16[1,2,128,512]{3,2,1,0:T(8,128)(2,1)} %param.8), channel_id=1, source_target_pairs={{8,0},{9,1},{16,8},{17,9},{24,16},{25,17},{0,24},{1,25},{10,2},{11... | collective-permute-start | bytes 786440 | tf_op jit(solution)/shard_map/ppermute | solution.py:240
  4.2 6.6 %copy-start = (bf16[1,1,1,2,1,128,128]{6,5,4,3,2,1,0:T(8,128)(2,1)S(1)}, bf16[1,1,1,2,1,128,128]{6,5,4,3,2,1,0:T(8,128)(2,1)}, u32[]{:S(2)}) copy-start(bf16[1,1,1,2,1,128,128]{6,5,4,3,2,1,0:T(8,128)(2,1)} %error.1) | copy-start | bytes 196612
  6.0 4.1 %collective-permute-start.8 = (bf16[1,128,128]{2,1,0:T(8,128)(2,1)S(1)}, bf16[1,128,128]{2,1,0:T(8,128)(2,1)S(1)}, u32[]{:S(2)}, u32[]{:S(2)}) collective-permute-start(bf16[1,128,128]{2,1,0:T(8,128)(2,1)S(1)} %get-tuple-element.57), channel_id=1, source_target_pairs={{1,0},{0,1},{3,2},{2,3},{5,4},{4,5},{7,6},{6,7},{9,8},{8,9},{11,10... | collective-permute-start | bytes 98312 | tf_op jit(solution)/shard_map/ppermute | solution.py:262
  11.1 5.9 %collective-permute-start = (bf16[128,128]{1,0:T(8,128)(2,1)S(1)}, bf16[128,128]{1,0:T(8,128)(2,1)S(1)}, u32[]{:S(2)}, u32[]{:S(2)}) collective-permute-start(bf16[128,128]{1,0:T(8,128)(2,1)S(1)} %get-tuple-element.34), channel_id=1, source_target_pairs={{0,4},{2,6},{4,2},{6,0},{1,5},{3,7},{5,3},{7,1},{8,12},{10,14},{12... | collective-permute-start | bytes 98312 | tf_op jit(solution)/shard_map/cond/branch_0_fun/ppermute | solution.py:322
  14.0 4.8 %collective-permute-start.1 = (bf16[128,128]{1,0:T(8,128)(2,1)S(1)}, bf16[128,128]{1,0:T(8,128)(2,1)S(1)}, u32[]{:S(2)}, u32[]{:S(2)}) collective-permute-start(bf16[128,128]{1,0:T(8,128)(2,1)S(1)} %get-tuple-element.35), channel_id=1, source_target_pairs={{0,6},{2,4},{4,0},{6,2},{1,7},{3,5},{5,1},{7,3},{8,14},{10,12},{12... | collective-permute-start | bytes 98312 | tf_op jit(solution)/shard_map/cond/branch_0_fun/ppermute | solution.py:322
  15.0 4.1 %collective-permute-start.2 = (bf16[128,128]{1,0:T(8,128)(2,1)S(1)}, bf16[128,128]{1,0:T(8,128)(2,1)S(1)}, u32[]{:S(2)}, u32[]{:S(2)}) collective-permute-start(bf16[128,128]{1,0:T(8,128)(2,1)S(1)} %get-tuple-element.36), channel_id=1, source_target_pairs={{0,2},{2,0},{4,6},{6,4},{1,3},{3,1},{5,7},{7,5},{8,10},{10,8},{12,... | collective-permute-start | bytes 98312 | tf_op jit(solution)/shard_map/cond/branch_0_fun/ppermute | solution.py:322

commit v2 on v1

--- a/solution.py
+++ b/solution.py
@@ -38,6 +38,10 @@
             steps[targets[source]] = step
         table.append(sum(step << 4 * target for target, step in enumerate(steps)))
     return table
+
+
+def wide_bit(step, count):
+    return step - 1 if count <= 4 else 0
 
 
 def plan_sizes(tiles, steps):
@@ -72,6 +76,13 @@
     per_group = columns // groups
     steps = len(rounds(replicas)) + 1 if apart else replicas
     to_step, to_column, to_row, to_col, end = plan_sizes(len(tiles), steps)
+
+    def owner_of(row):
+        owner = jnp.int32(0)
+        for one in range(1, replicas):
+            owner += (row >= one * owned).astype(jnp.int32)
+        return owner
+
     table = step_table(replicas) if apart else []
     mine = jnp.int32(0)
     for source, packed in enumerate(table):
@@ -80,10 +91,7 @@
     planned = jnp.where((lane >= to_row) & (lane < end), -1, 0)
 
     for at, (group, slot) in enumerate(tiles):
-        row = owners[0, 0, picks[0, 0, group, slot, 0, replica]]
-        owner = jnp.int32(0)
-        for one in range(1, replicas):
-            owner += (row >= one * owned).astype(jnp.int32)
+        owner = owner_of(owners[0, 0, picks[0, 0, group, slot, 0, replica]])
         step = (mine >> 4 * owner) & 15 if apart else owner
         planned = jnp.where(lane == to_step + at, step, planned)
         planned = jnp.where(lane == to_column + at, picks[0, 0, group, slot, 1, replica], planned)
@@ -101,21 +109,26 @@
         planned = jnp.where(lane == to_row + step, place_row, planned)
         planned = jnp.where(lane == to_col + step, place_col, planned)
 
-    meets = jnp.int32(0)
+    wide = jnp.int32(0)
     if apart:
         spots = [
             picks[0, 0, group, slot, 0, origin] * columns
             + picks[0, 0, group, slot, 1, origin]
             + group * per_group
+            for origin in range(replicas)
             for group, slot in tiles
-            for origin in range(replicas)
         ]
         for spot in spots:
             seen[spot] = 0
         for spot in spots:
-            meets = meets | seen[spot]
-            seen[spot] = 1
-    plan[...] = jnp.where(lane == 0, meets, planned)
+            seen[spot] = seen[spot] + 1
+        for at, spot in enumerate(spots):
+            origin, (group, slot) = at // len(tiles), tiles[at % len(tiles)]
+            owner = owner_of(owners[0, 0, picks[0, 0, group, slot, 0, origin]])
+            step = (jnp.int32(table[origin]) >> 4 * owner) & 15
+            bit = jnp.int32(1) << wide_bit(jnp.maximum(step, 1), steps)
+            wide = jnp.where((seen[spot] > 1) & (step > 0), wide | bit, wide)
+    plan[...] = jnp.where(lane == 0, wide, planned)
 
     for at, copy in enumerate(reads):
         copy.wait()
@@ -141,7 +154,7 @@
     mine = lax.axis_index("tensor")
     slots, (edge, tokens) = error.shape[4], picked.shape[1:]
     count = groups * slots
-    meet = plan[0, 0] > 0
+    wide = plan[0, 0]
     columns = [plan[0, to_column + at] for at in range(count)]
     steps = [plan[0, to_step + at] for at in range(count)]
     tiles = []
@@ -157,21 +170,26 @@
             outs[0][step] = tile
         return
 
-    def store(buffers):
-        for step, tile in zip(steps, tiles):
-            for at, buffer in enumerate(buffers):
-
-                @pl.when(step == at)
-                def _():
-                    buffer[...] = tile.astype(buffer.dtype)
-
-    @pl.when(meet)
-    def _():
-        store(outs[: len(outs) // 2])
-
-    @pl.when(jnp.logical_not(meet))
-    def _():
-        store(outs[len(outs) // 2 :])
+    buffers = len(outs) // 2
+
+    def store(step, tile, buffers):
+        for at, buffer in enumerate(buffers):
+
+            @pl.when(step == at)
+            def _():
+                buffer[...] = tile.astype(buffer.dtype)
+
+    for step, tile in zip(steps, tiles):
+        bit = (wide >> wide_bit(jnp.maximum(step, 1), buffers)) & 1
+        full = jnp.where(step == 0, wide, bit) > 0
+
+        @pl.when(full)
+        def _():
+            store(step, tile, outs[:buffers])
+
+        @pl.when(jnp.logical_not(full))
+        def _():
+            store(step, tile, outs[buffers:])
 
 
 def place(count, alone, to_row, to_col, plan, *refs):
@@ -205,9 +223,10 @@
         @pl.when(first_of(step))
         def _():
             if not alone:
-                total = block_of(step)
+                total = block_of(step).astype(jnp.float32)
                 for later in range(step + 1, steps):
-                    total = total + jnp.where(meets(step, later), block_of(later), 0.0)
+                    block = block_of(later).astype(jnp.float32)
+                    total = total + jnp.where(meets(step, later), block, 0.0)
                 staged[step] = total.astype(staged.dtype)
             write_of(step).start()
 
@@ -327,11 +346,15 @@
     if not apart:
         swapped = lax.all_to_all(outgoing[0], "dp", split_axis=0, concat_axis=0, tiled=True)
         return placed(False, [swapped])
-    return lax.cond(
-        plan[0, 0] > 0,
-        lambda: placed(False, exchanged(outgoing[:steps])),
-        lambda: placed(True, exchanged(outgoing[steps:])),
-    )
+    def branch(wide):
+        blocks = [
+            outgoing[at if (wide >> wide_bit(at, steps) & 1 if at else wide) else steps + at]
+            for at in range(steps)
+        ]
+        return lambda: placed(not wide, exchanged(blocks))
+
+    sets = 1 << (wide_bit(steps - 1, steps) + 1)
+    return lax.switch(plan[0, 0], [branch(wide) for wide in range(sets)])
 
 
 def solution(mesh):

time: 20.1 us -> 20.1 us (level)
  no operation moved by 1% of the time
where the time goes in v2:
time: 20.1 us; the launch traced here: 19.9 us
  starting transfers between devices  9.19 us (46%)
  waiting for transfers between devices  5.58 us (28%)
  Pallas kernels  5.05 us (25%)
    ppermute x3, starting transfers between devices, exchanged(): lax.ppermute(block, 'dp', list(enumerate(targets)))  4.41 us
    ppermute x2, starting transfers between devices, body(): returned.append(lax.ppermute(cotangent, ('pipe', 'tensor'), pairs))  4.18 us
    ppermute x3, waiting for transfers between devices, exchanged(): lax.ppermute(block, 'dp', list(enumerate(targets)))  3.58 us
    pallas_call x1, Pallas kernels, body(): pl.pallas_call(clear, out_shape=pltpu.HBM(strip_shape, jnp.bfloat16), in_...  2.1 us
    pallas_call x1, Pallas kernels, body(): pl.pallas_call(functools.partial(pick, shifts, apart, width // edge), out...  1.86 us
    ppermute x1, waiting for transfers between devices, body(): lax.ppermute(error, 'tensor', [((group + shift + 1) % groups, group) for...  1.36 us
    pallas_call x1, Pallas kernels, placed(): pl.pallas_call(functools.partial(place, len(incoming), alone, to_row, to_...  0.77 us
    ppermute x2, waiting for transfers between devices, body(): returned.append(lax.ppermute(cotangent, ('pipe', 'tensor'), pairs))  0.64 us
  transfers between devices with their start and end apart: 6, of which 5 were waited for; matrix products, arithmetic and copies ran while one was open for 0% of the time, Pallas kernels for 20%

profile of v2, /device:TPU:0, one launch (start us, length us, event | category | flops | bytes accessed | tf_op | source)
XLA Modules:
  0.0 19.9 jit_solution(16913752003844665603)
XLA Ops:
  0.0 3.3 %collective-permute-start.25 = (bf16[1,2,128,512]{3,2,1,0:T(8,128)(2,1)}, bf16[1,2,128,512]{3,2,1,0:T(8,128)(2,1)S(1)}, u32[]{:S(2)}, u32[]{:S(2)}) collective-permute-start(bf16[1,2,128,512]{3,2,1,0:T(8,128)(2,1)} %param.14), channel_id=1, source_target_pairs={{9,0},{8,1},{17,8},{16,9},{25,16},{24,17},{1,24},{0,25},{11,2},{10... | collective-permute-start | bytes 786440 | tf_op jit(solution)/shard_map/ppermute | solution.py:259
  3.3 0.8 %collective-permute-start.24 = (bf16[1,2,128,512]{3,2,1,0:T(8,128)(2,1)}, bf16[1,2,128,512]{3,2,1,0:T(8,128)(2,1)S(1)}, u32[]{:S(2)}, u32[]{:S(2)}) collective-permute-start(bf16[1,2,128,512]{3,2,1,0:T(8,128)(2,1)} %param.14), channel_id=1, source_target_pairs={{8,0},{9,1},{16,8},{17,9},{24,16},{25,17},{0,24},{1,25},{10,2},{11... | collective-permute-start | bytes 786440 | tf_op jit(solution)/shard_map/ppermute | solution.py:259
  4.2 0.0 copy-start
  4.2 1.9 %pick.1 = (bf16[2,128,256]{2,1,0:T(8,128)(2,1)S(1)}, s32[1,128]{1,0:T(1,128)S(1)}, bf16[1,128,128]{2,1,0:T(8,128)(2,1)S(1)}) custom-call(s32[1,1,2,1,2,4]{5,4,3,2,1,0:T(2,128)} %bitcast.4, s32[1,1,64]{2,1,0:T(1,128)} %owners.1, bf16[1,2,128,8192]{3,2,1,0:T(8,128)(2,1)} %activations.1, bf16[1,1,1,2,1,128,128]{6,5,4,3,2,1,0:T(8,128)(2,1)} %error.1), custom_call_target="tpu_custom_call" | custom-call | tf_op jit(solution)/shard_map/pick/pallas_call | solution.py:263
  6.0 0.6 %collective-permute-start.26 = (bf16[1,128,128]{2,1,0:T(8,128)(2,1)S(1)}, bf16[1,128,128]{2,1,0:T(8,128)(2,1)S(1)}, u32[]{:S(2)}, u32[]{:S(2)}) collective-permute-start(bf16[1,128,128]{2,1,0:T(8,128)(2,1)S(1)} %get-tuple-element.171), channel_id=1, source_target_pairs={{1,0},{0,1},{3,2},{2,3},{5,4},{4,5},{7,6},{6,7},{9,8},{8,9},{11,10... | collective-permute-start | bytes 98312 | tf_op jit(solution)/shard_map/ppermute | solution.py:281
  6.6 2.1 %clear.1 = bf16[1,1,2048,1024]{3,2,1,0:T(8,128)(2,1)} custom-call(bf16[2,128,256]{2,1,0:T(8,128)(2,1)S(1)} %get-tuple-element.170.picked.after), custom_call_target="tpu_custom_call" | custom-call | bytes 4194304 | tf_op jit(solution)/shard_map/clear/pallas_call | solution.py:289
  8.8 1.4 %collective-permute-done.26.refs_2_ = bf16[1,128,128]{2,1,0:T(8,128)(2,1)S(1)} collective-permute-done((bf16[1,128,128]{2,1,0:T(8,128)(2,1)S(1)}, bf16[1,128,128]{2,1,0:T(8,128)(2,1)S(1)}, u32[]{:S(2)}, u32[]{:S(2)}) %collective-permute-start.26) | collective-permute-done | bytes 32800 | tf_op jit(solution)/shard_map/ppermute | solution.py:281
  10.2 0.0 collective-permute-done.25.refs_1_
  10.2 0.6 %collective-permute-done.24.refs_0_ = bf16[1,2,128,512]{3,2,1,0:T(8,128)(2,1)S(1)} collective-permute-done((bf16[1,2,128,512]{3,2,1,0:T(8,128)(2,1)}, bf16[1,2,128,512]{3,2,1,0:T(8,128)(2,1)S(1)}, u32[]{:S(2)}, u32[]{:S(2)}) %collective-permute-start.24) | collective-permute-done | bytes 262176 | tf_op jit(solution)/shard_map/ppermute | solution.py:259
  10.8 0.0 copy-done
  10.8 0.3 %multiply.1 = (f32[128,128]{1,0:T(8,128)S(1)}, f32[128,128]{1,0:T(8,128)S(1)}, f32[128,128]{1,0:T(8,128)S(1)}, f32[128,128]{1,0:T(8,128)S(1)}, bf16[128,128]{1,0...) custom-call(s32[1,128]{1,0:T(1,128)S(1)} %get-tuple-element.169.plan, ...), custom_call_target="tpu_custom_call" | custom-call | tf_op jit(solution)/shard_map/multiply/pallas_call | solution.py:315
  11.1 8.8 %conditional.1 = (bf16[1,1,2048,1024]{3,2,1,0:T(8,128)(2,1)}) conditional(s32[]{:T(128)} %bitcast.1, (bf16[128,128]{1,0:T(8,128)(2,1)S(1)}, bf16[128,128]{1,0:T(8,128)(2,1)S(1)}, bf16[128,128]{1,0:T(8,128)(2,1)S(1)}, s32[1,128]{1,0:T(1,128)S(1)}, bf16[128,128]{1,0:T(8,128)(2,1)S(1)}, ...), branch_computations={%region_0.0_spmd, %region_1.0_spmd, %region_2.0_spmd, %region_3.0_... | conditional | bytes 786560 | solution.py:357
  11.2 2.8 %collective-permute-start = (bf16[128,128]{1,0:T(8,128)(2,1)S(1)}, bf16[128,128]{1,0:T(8,128)(2,1)S(1)}, u32[]{:S(2)}, u32[]{:S(2)}) collective-permute-start(bf16[128,128]{1,0:T(8,128)(2,1)S(1)} %get-tuple-element.103), channel_id=1, source_target_pairs={{0,4},{2,6},{4,2},{6,0},{1,5},{3,7},{5,3},{7,1},{8,12},{10,14},{12... | collective-permute-start | bytes 98312 | tf_op jit(solution)/shard_map/cond/branch_0_fun/ppermute | solution.py:341
  14.0 1.1 %collective-permute-start.1 = (bf16[128,128]{1,0:T(8,128)(2,1)S(1)}, bf16[128,128]{1,0:T(8,128)(2,1)S(1)}, u32[]{:S(2)}, u32[]{:S(2)}) collective-permute-start(bf16[128,128]{1,0:T(8,128)(2,1)S(1)} %get-tuple-element.104), channel_id=1, source_target_pairs={{0,6},{2,4},{4,0},{6,2},{1,7},{3,5},{5,1},{7,3},{8,14},{10,12},{12... | collective-permute-start | bytes 98312 | tf_op jit(solution)/shard_map/cond/branch_0_fun/ppermute | solution.py:341
  15.1 0.5 %collective-permute-start.2 = (bf16[128,128]{1,0:T(8,128)(2,1)S(1)}, bf16[128,128]{1,0:T(8,128)(2,1)S(1)}, u32[]{:S(2)}, u32[]{:S(2)}) collective-permute-start(bf16[128,128]{1,0:T(8,128)(2,1)S(1)} %get-tuple-element.112), channel_id=1, source_target_pairs={{0,2},{2,0},{4,6},{6,4},{1,3},{3,1},{5,7},{7,5},{8,10},{10,8},{12,... | collective-permute-start | bytes 98312 | tf_op jit(solution)/shard_map/cond/branch_0_fun/ppermute | solution.py:341
  15.6 1.5 %collective-permute-done.refs_1_ = bf16[128,128]{1,0:T(8,128)(2,1)S(1)} collective-permute-done((bf16[128,128]{1,0:T(8,128)(2,1)S(1)}, bf16[128,128]{1,0:T(8,128)(2,1)S(1)}, u32[]{:S(2)}, u32[]{:S(2)}) %collective-permute-start) | collective-permute-done | bytes 32800 | tf_op jit(solution)/shard_map/cond/branch_0_fun/ppermute | solution.py:341
  17.0 1.8 %collective-permute-done.1.refs_2_ = bf16[128,128]{1,0:T(8,128)(2,1)S(1)} collective-permute-done((bf16[128,128]{1,0:T(8,128)(2,1)S(1)}, bf16[128,128]{1,0:T(8,128)(2,1)S(1)}, u32[]{:S(2)}, u32[]{:S(2)}) %collective-permute-start.1) | collective-permute-done | bytes 32800 | tf_op jit(solution)/shard_map/cond/branch_0_fun/ppermute | solution.py:341
  18.8 0.3 %collective-permute-done.2.refs_3_ = bf16[128,128]{1,0:T(8,128)(2,1)S(1)} collective-permute-done((bf16[128,128]{1,0:T(8,128)(2,1)S(1)}, bf16[128,128]{1,0:T(8,128)(2,1)S(1)}, u32[]{:S(2)}, u32[]{:S(2)}) %collective-permute-start.2) | collective-permute-done | bytes 32800 | tf_op jit(solution)/shard_map/cond/branch_0_fun/ppermute | solution.py:341
  19.1 0.8 %place.8 = bf16[1,1,2048,1024]{3,2,1,0:T(8,128)(2,1)} custom-call(s32[1,128]{1,0:T(1,128)S(1)} %get-tuple-element.101.plan, bf16[128,128]{1,0:T(8,128)(2,1)S(1)} %get-tuple-element.102.refs_0_, bf16[128,128]{1,0:T(8,128)(2,1)S(1)} %collective-permute-done.refs_1_, ...), custom_call_target="tpu_custom_call", output_to_operand_aliasing={{}: (5, {})} | custom-call | tf_op jit(solution)/shard_map/cond/branch_0_fun/place/pallas_call | solution.py:325
Async XLA Ops:
  0.0 10.2 %collective-permute-start.25 = (bf16[1,2,128,512]{3,2,1,0:T(8,128)(2,1)}, bf16[1,2,128,512]{3,2,1,0:T(8,128)(2,1)S(1)}, u32[]{:S(2)}, u32[]{:S(2)}) collective-permute-start(bf16[1,2,128,512]{3,2,1,0:T(8,128)(2,1)} %param.14), channel_id=1, source_target_pairs={{9,0},{8,1},{17,8},{16,9},{25,16},{24,17},{1,24},{0,25},{11,2},{10... | collective-permute-start | bytes 786440 | tf_op jit(solution)/shard_map/ppermute | solution.py:259
  3.3 7.5 %collective-permute-start.24 = (bf16[1,2,128,512]{3,2,1,0:T(8,128)(2,1)}, bf16[1,2,128,512]{3,2,1,0:T(8,128)(2,1)S(1)}, u32[]{:S(2)}, u32[]{:S(2)}) collective-permute-start(bf16[1,2,128,512]{3,2,1,0:T(8,128)(2,1)} %param.14), channel_id=1, source_target_pairs={{8,0},{9,1},{16,8},{17,9},{24,16},{25,17},{0,24},{1,25},{10,2},{11... | collective-permute-start | bytes 786440 | tf_op jit(solution)/shard_map/ppermute | solution.py:259
  4.2 6.6 %copy-start = (bf16[1,1,1,2,1,128,128]{6,5,4,3,2,1,0:T(8,128)(2,1)S(1)}, bf16[1,1,1,2,1,128,128]{6,5,4,3,2,1,0:T(8,128)(2,1)}, u32[]{:S(2)}) copy-start(bf16[1,1,1,2,1,128,128]{6,5,4,3,2,1,0:T(8,128)(2,1)} %error.1) | copy-start | bytes 196612
  6.0 4.1 %collective-permute-start.26 = (bf16[1,128,128]{2,1,0:T(8,128)(2,1)S(1)}, bf16[1,128,128]{2,1,0:T(8,128)(2,1)S(1)}, u32[]{:S(2)}, u32[]{:S(2)}) collective-permute-start(bf16[1,128,128]{2,1,0:T(8,128)(2,1)S(1)} %get-tuple-element.171), channel_id=1, source_target_pairs={{1,0},{0,1},{3,2},{2,3},{5,4},{4,5},{7,6},{6,7},{9,8},{8,9},{11,10... | collective-permute-start | bytes 98312 | tf_op jit(solution)/shard_map/ppermute | solution.py:281
  11.2 5.9 %collective-permute-start = (bf16[128,128]{1,0:T(8,128)(2,1)S(1)}, bf16[128,128]{1,0:T(8,128)(2,1)S(1)}, u32[]{:S(2)}, u32[]{:S(2)}) collective-permute-start(bf16[128,128]{1,0:T(8,128)(2,1)S(1)} %get-tuple-element.103), channel_id=1, source_target_pairs={{0,4},{2,6},{4,2},{6,0},{1,5},{3,7},{5,3},{7,1},{8,12},{10,14},{12... | collective-permute-start | bytes 98312 | tf_op jit(solution)/shard_map/cond/branch_0_fun/ppermute | solution.py:341
  14.0 4.8 %collective-permute-start.1 = (bf16[128,128]{1,0:T(8,128)(2,1)S(1)}, bf16[128,128]{1,0:T(8,128)(2,1)S(1)}, u32[]{:S(2)}, u32[]{:S(2)}) collective-permute-start(bf16[128,128]{1,0:T(8,128)(2,1)S(1)} %get-tuple-element.104), channel_id=1, source_target_pairs={{0,6},{2,4},{4,0},{6,2},{1,7},{3,5},{5,1},{7,3},{8,14},{10,12},{12... | collective-permute-start | bytes 98312 | tf_op jit(solution)/shard_map/cond/branch_0_fun/ppermute | solution.py:341
  15.1 4.1 %collective-permute-start.2 = (bf16[128,128]{1,0:T(8,128)(2,1)S(1)}, bf16[128,128]{1,0:T(8,128)(2,1)S(1)}, u32[]{:S(2)}, u32[]{:S(2)}) collective-permute-start(bf16[128,128]{1,0:T(8,128)(2,1)S(1)} %get-tuple-element.112), channel_id=1, source_target_pairs={{0,2},{2,0},{4,6},{6,4},{1,3},{3,1},{5,7},{7,5},{8,10},{10,8},{12,... | collective-permute-start | bytes 98312 | tf_op jit(solution)/shard_map/cond/branch_0_fun/ppermute | solution.py:341

commit v3 on v2

--- a/solution.py
+++ b/solution.py
@@ -211,12 +211,23 @@
             first = first & jnp.logical_not(meets(earlier, step))
         return first
 
-    def write_of(step):
-        return pltpu.make_async_copy(
-            blocks[step] if alone else staged.at[step],
-            strip.at[0, 0, column(rows[step], edge), column(cols[step], edge)],
-            sent.at[step],
-        )
+    half = edge // 2
+
+    def writes_of(step):
+        source = blocks[step] if alone else staged.at[step]
+        return [
+            pltpu.make_async_copy(
+                source.at[pl.ds(part * half, half)],
+                strip.at[
+                    0,
+                    0,
+                    pl.ds(pl.multiple_of(rows[step] * edge + part * half, half), half),
+                    column(cols[step], edge),
+                ],
+                sent.at[step, part],
+            )
+            for part in range(2)
+        ]
 
     for step in range(steps):
 
@@ -228,13 +239,15 @@
                     block = block_of(later).astype(jnp.float32)
                     total = total + jnp.where(meets(step, later), block, 0.0)
                 staged[step] = total.astype(staged.dtype)
-            write_of(step).start()
+            for write in writes_of(step):
+                write.start()
 
     for step in range(steps):
 
         @pl.when(first_of(step))
         def _():
-            write_of(step).wait()
+            for write in writes_of(step):
+                write.wait()
 
 
 def body(mesh, activations, cotangent, error_tiles, tile_picks, row_owners):
@@ -329,7 +342,7 @@
             out_specs=ANY,
             scratch_shapes=[
                 pltpu.VMEM((steps,) + tile_shape, jnp.bfloat16),
-                pltpu.SemaphoreType.DMA((steps,)),
+                pltpu.SemaphoreType.DMA((steps, 2)),
             ],
             input_output_aliases={1 + len(incoming): 0},
             compiler_params=SMALL,

time: 20.1 us -> 20.2 us (level)
  no operation moved by 1% of the time
where the time goes in v3:
time: 20.2 us; the launch traced here: 20 us
  starting transfers between devices  9.19 us (45%)
  waiting for transfers between devices  5.58 us (28%)
  Pallas kernels  5.08 us (25%)
    ppermute x3, starting transfers between devices, exchanged(): lax.ppermute(block, 'dp', list(enumerate(targets)))  4.41 us
    ppermute x2, starting transfers between devices, body(): returned.append(lax.ppermute(cotangent, ('pipe', 'tensor'), pairs))  4.18 us
    ppermute x3, waiting for transfers between devices, exchanged(): lax.ppermute(block, 'dp', list(enumerate(targets)))  3.58 us
    pallas_call x1, Pallas kernels, body(): pl.pallas_call(clear, out_shape=pltpu.HBM(strip_shape, jnp.bfloat16), in_...  2.1 us
    pallas_call x1, Pallas kernels, body(): pl.pallas_call(functools.partial(pick, shifts, apart, width // edge), out...  1.86 us
    ppermute x1, waiting for transfers between devices, body(): lax.ppermute(error, 'tensor', [((group + shift + 1) % groups, group) for...  1.36 us
    pallas_call x1, Pallas kernels, placed(): pl.pallas_call(functools.partial(place, len(incoming), alone, to_row, to_...  0.8 us
    ppermute x2, waiting for transfers between devices, body(): returned.append(lax.ppermute(cotangent, ('pipe', 'tensor'), pairs))  0.64 us
  transfers between devices with their start and end apart: 6, of which 5 were waited for; matrix products, arithmetic and copies ran while one was open for 0% of the time, Pallas kernels for 20%

profile of v3, /device:TPU:0, one launch (start us, length us, event | category | flops | bytes accessed | tf_op | source)
XLA Modules:
  0.0 20.0 jit_solution(9216101628316496328)
XLA Ops:
  0.0 3.3 %collective-permute-start.25 = (bf16[1,2,128,512]{3,2,1,0:T(8,128)(2,1)}, bf16[1,2,128,512]{3,2,1,0:T(8,128)(2,1)S(1)}, u32[]{:S(2)}, u32[]{:S(2)}) collective-permute-start(bf16[1,2,128,512]{3,2,1,0:T(8,128)(2,1)} %param.14), channel_id=1, source_target_pairs={{9,0},{8,1},{17,8},{16,9},{25,16},{24,17},{1,24},{0,25},{11,2},{10... | collective-permute-start | bytes 786440 | tf_op jit(solution)/shard_map/ppermute | solution.py:272
  3.3 0.8 %collective-permute-start.24 = (bf16[1,2,128,512]{3,2,1,0:T(8,128)(2,1)}, bf16[1,2,128,512]{3,2,1,0:T(8,128)(2,1)S(1)}, u32[]{:S(2)}, u32[]{:S(2)}) collective-permute-start(bf16[1,2,128,512]{3,2,1,0:T(8,128)(2,1)} %param.14), channel_id=1, source_target_pairs={{8,0},{9,1},{16,8},{17,9},{24,16},{25,17},{0,24},{1,25},{10,2},{11... | collective-permute-start | bytes 786440 | tf_op jit(solution)/shard_map/ppermute | solution.py:272
  4.2 0.0 copy-start
  4.2 1.9 %pick.1 = (bf16[2,128,256]{2,1,0:T(8,128)(2,1)S(1)}, s32[1,128]{1,0:T(1,128)S(1)}, bf16[1,128,128]{2,1,0:T(8,128)(2,1)S(1)}) custom-call(s32[1,1,2,1,2,4]{5,4,3,2,1,0:T(2,128)} %bitcast.4, s32[1,1,64]{2,1,0:T(1,128)} %owners.1, bf16[1,2,128,8192]{3,2,1,0:T(8,128)(2,1)} %activations.1, bf16[1,1,1,2,1,128,128]{6,5,4,3,2,1,0:T(8,128)(2,1)} %error.1), custom_call_target="tpu_custom_call" | custom-call | tf_op jit(solution)/shard_map/pick/pallas_call | solution.py:276
  6.0 0.6 %collective-permute-start.26 = (bf16[1,128,128]{2,1,0:T(8,128)(2,1)S(1)}, bf16[1,128,128]{2,1,0:T(8,128)(2,1)S(1)}, u32[]{:S(2)}, u32[]{:S(2)}) collective-permute-start(bf16[1,128,128]{2,1,0:T(8,128)(2,1)S(1)} %get-tuple-element.171), channel_id=1, source_target_pairs={{1,0},{0,1},{3,2},{2,3},{5,4},{4,5},{7,6},{6,7},{9,8},{8,9},{11,10... | collective-permute-start | bytes 98312 | tf_op jit(solution)/shard_map/ppermute | solution.py:294
  6.6 2.1 %clear.1 = bf16[1,1,2048,1024]{3,2,1,0:T(8,128)(2,1)} custom-call(bf16[2,128,256]{2,1,0:T(8,128)(2,1)S(1)} %get-tuple-element.170.picked.after), custom_call_target="tpu_custom_call" | custom-call | bytes 4194304 | tf_op jit(solution)/shard_map/clear/pallas_call | solution.py:302
  8.8 1.4 %collective-permute-done.26.refs_2_ = bf16[1,128,128]{2,1,0:T(8,128)(2,1)S(1)} collective-permute-done((bf16[1,128,128]{2,1,0:T(8,128)(2,1)S(1)}, bf16[1,128,128]{2,1,0:T(8,128)(2,1)S(1)}, u32[]{:S(2)}, u32[]{:S(2)}) %collective-permute-start.26) | collective-permute-done | bytes 32800 | tf_op jit(solution)/shard_map/ppermute | solution.py:294
  10.2 0.0 collective-permute-done.25.refs_1_
  10.2 0.6 %collective-permute-done.24.refs_0_ = bf16[1,2,128,512]{3,2,1,0:T(8,128)(2,1)S(1)} collective-permute-done((bf16[1,2,128,512]{3,2,1,0:T(8,128)(2,1)}, bf16[1,2,128,512]{3,2,1,0:T(8,128)(2,1)S(1)}, u32[]{:S(2)}, u32[]{:S(2)}) %collective-permute-start.24) | collective-permute-done | bytes 262176 | tf_op jit(solution)/shard_map/ppermute | solution.py:272
  10.8 0.0 copy-done
  10.8 0.3 %multiply.1 = (f32[128,128]{1,0:T(8,128)S(1)}, f32[128,128]{1,0:T(8,128)S(1)}, f32[128,128]{1,0:T(8,128)S(1)}, f32[128,128]{1,0:T(8,128)S(1)}, bf16[128,128]{1,0...) custom-call(s32[1,128]{1,0:T(1,128)S(1)} %get-tuple-element.169.plan, ...), custom_call_target="tpu_custom_call" | custom-call | tf_op jit(solution)/shard_map/multiply/pallas_call | solution.py:328
  11.1 8.8 %conditional.1 = (bf16[1,1,2048,1024]{3,2,1,0:T(8,128)(2,1)}) conditional(s32[]{:T(128)} %bitcast.1, (bf16[128,128]{1,0:T(8,128)(2,1)S(1)}, bf16[128,128]{1,0:T(8,128)(2,1)S(1)}, bf16[128,128]{1,0:T(8,128)(2,1)S(1)}, s32[1,128]{1,0:T(1,128)S(1)}, bf16[128,128]{1,0:T(8,128)(2,1)S(1)}, ...), branch_computations={%region_0.0_spmd, %region_1.0_spmd, %region_2.0_spmd, %region_3.0_... | conditional | bytes 786560 | solution.py:370
  11.2 2.8 %collective-permute-start = (bf16[128,128]{1,0:T(8,128)(2,1)S(1)}, bf16[128,128]{1,0:T(8,128)(2,1)S(1)}, u32[]{:S(2)}, u32[]{:S(2)}) collective-permute-start(bf16[128,128]{1,0:T(8,128)(2,1)S(1)} %get-tuple-element.103), channel_id=1, source_target_pairs={{0,4},{2,6},{4,2},{6,0},{1,5},{3,7},{5,3},{7,1},{8,12},{10,14},{12... | collective-permute-start | bytes 98312 | tf_op jit(solution)/shard_map/cond/branch_0_fun/ppermute | solution.py:354
  14.0 1.1 %collective-permute-start.1 = (bf16[128,128]{1,0:T(8,128)(2,1)S(1)}, bf16[128,128]{1,0:T(8,128)(2,1)S(1)}, u32[]{:S(2)}, u32[]{:S(2)}) collective-permute-start(bf16[128,128]{1,0:T(8,128)(2,1)S(1)} %get-tuple-element.104), channel_id=1, source_target_pairs={{0,6},{2,4},{4,0},{6,2},{1,7},{3,5},{5,1},{7,3},{8,14},{10,12},{12... | collective-permute-start | bytes 98312 | tf_op jit(solution)/shard_map/cond/branch_0_fun/ppermute | solution.py:354
  15.1 0.5 %collective-permute-start.2 = (bf16[128,128]{1,0:T(8,128)(2,1)S(1)}, bf16[128,128]{1,0:T(8,128)(2,1)S(1)}, u32[]{:S(2)}, u32[]{:S(2)}) collective-permute-start(bf16[128,128]{1,0:T(8,128)(2,1)S(1)} %get-tuple-element.112), channel_id=1, source_target_pairs={{0,2},{2,0},{4,6},{6,4},{1,3},{3,1},{5,7},{7,5},{8,10},{10,8},{12,... | collective-permute-start | bytes 98312 | tf_op jit(solution)/shard_map/cond/branch_0_fun/ppermute | solution.py:354
  15.6 1.5 %collective-permute-done.refs_1_ = bf16[128,128]{1,0:T(8,128)(2,1)S(1)} collective-permute-done((bf16[128,128]{1,0:T(8,128)(2,1)S(1)}, bf16[128,128]{1,0:T(8,128)(2,1)S(1)}, u32[]{:S(2)}, u32[]{:S(2)}) %collective-permute-start) | collective-permute-done | bytes 32800 | tf_op jit(solution)/shard_map/cond/branch_0_fun/ppermute | solution.py:354
  17.0 1.8 %collective-permute-done.1.refs_2_ = bf16[128,128]{1,0:T(8,128)(2,1)S(1)} collective-permute-done((bf16[128,128]{1,0:T(8,128)(2,1)S(1)}, bf16[128,128]{1,0:T(8,128)(2,1)S(1)}, u32[]{:S(2)}, u32[]{:S(2)}) %collective-permute-start.1) | collective-permute-done | bytes 32800 | tf_op jit(solution)/shard_map/cond/branch_0_fun/ppermute | solution.py:354
  18.8 0.3 %collective-permute-done.2.refs_3_ = bf16[128,128]{1,0:T(8,128)(2,1)S(1)} collective-permute-done((bf16[128,128]{1,0:T(8,128)(2,1)S(1)}, bf16[128,128]{1,0:T(8,128)(2,1)S(1)}, u32[]{:S(2)}, u32[]{:S(2)}) %collective-permute-start.2) | collective-permute-done | bytes 32800 | tf_op jit(solution)/shard_map/cond/branch_0_fun/ppermute | solution.py:354
  19.1 0.8 %place.8 = bf16[1,1,2048,1024]{3,2,1,0:T(8,128)(2,1)} custom-call(s32[1,128]{1,0:T(1,128)S(1)} %get-tuple-element.101.plan, bf16[128,128]{1,0:T(8,128)(2,1)S(1)} %get-tuple-element.102.refs_0_, bf16[128,128]{1,0:T(8,128)(2,1)S(1)} %collective-permute-done.refs_1_, ...), custom_call_target="tpu_custom_call", output_to_operand_aliasing={{}: (5, {})} | custom-call | tf_op jit(solution)/shard_map/cond/branch_0_fun/place/pallas_call | solution.py:338
Async XLA Ops:
  0.0 10.2 %collective-permute-start.25 = (bf16[1,2,128,512]{3,2,1,0:T(8,128)(2,1)}, bf16[1,2,128,512]{3,2,1,0:T(8,128)(2,1)S(1)}, u32[]{:S(2)}, u32[]{:S(2)}) collective-permute-start(bf16[1,2,128,512]{3,2,1,0:T(8,128)(2,1)} %param.14), channel_id=1, source_target_pairs={{9,0},{8,1},{17,8},{16,9},{25,16},{24,17},{1,24},{0,25},{11,2},{10... | collective-permute-start | bytes 786440 | tf_op jit(solution)/shard_map/ppermute | solution.py:272
  3.3 7.5 %collective-permute-start.24 = (bf16[1,2,128,512]{3,2,1,0:T(8,128)(2,1)}, bf16[1,2,128,512]{3,2,1,0:T(8,128)(2,1)S(1)}, u32[]{:S(2)}, u32[]{:S(2)}) collective-permute-start(bf16[1,2,128,512]{3,2,1,0:T(8,128)(2,1)} %param.14), channel_id=1, source_target_pairs={{8,0},{9,1},{16,8},{17,9},{24,16},{25,17},{0,24},{1,25},{10,2},{11... | collective-permute-start | bytes 786440 | tf_op jit(solution)/shard_map/ppermute | solution.py:272
  4.2 6.6 %copy-start = (bf16[1,1,1,2,1,128,128]{6,5,4,3,2,1,0:T(8,128)(2,1)S(1)}, bf16[1,1,1,2,1,128,128]{6,5,4,3,2,1,0:T(8,128)(2,1)}, u32[]{:S(2)}) copy-start(bf16[1,1,1,2,1,128,128]{6,5,4,3,2,1,0:T(8,128)(2,1)} %error.1) | copy-start | bytes 196612
  6.0 4.1 %collective-permute-start.26 = (bf16[1,128,128]{2,1,0:T(8,128)(2,1)S(1)}, bf16[1,128,128]{2,1,0:T(8,128)(2,1)S(1)}, u32[]{:S(2)}, u32[]{:S(2)}) collective-permute-start(bf16[1,128,128]{2,1,0:T(8,128)(2,1)S(1)} %get-tuple-element.171), channel_id=1, source_target_pairs={{1,0},{0,1},{3,2},{2,3},{5,4},{4,5},{7,6},{6,7},{9,8},{8,9},{11,10... | collective-permute-start | bytes 98312 | tf_op jit(solution)/shard_map/ppermute | solution.py:294
  11.2 5.9 %collective-permute-start = (bf16[128,128]{1,0:T(8,128)(2,1)S(1)}, bf16[128,128]{1,0:T(8,128)(2,1)S(1)}, u32[]{:S(2)}, u32[]{:S(2)}) collective-permute-start(bf16[128,128]{1,0:T(8,128)(2,1)S(1)} %get-tuple-element.103), channel_id=1, source_target_pairs={{0,4},{2,6},{4,2},{6,0},{1,5},{3,7},{5,3},{7,1},{8,12},{10,14},{12... | collective-permute-start | bytes 98312 | tf_op jit(solution)/shard_map/cond/branch_0_fun/ppermute | solution.py:354
  14.0 4.8 %collective-permute-start.1 = (bf16[128,128]{1,0:T(8,128)(2,1)S(1)}, bf16[128,128]{1,0:T(8,128)(2,1)S(1)}, u32[]{:S(2)}, u32[]{:S(2)}) collective-permute-start(bf16[128,128]{1,0:T(8,128)(2,1)S(1)} %get-tuple-element.104), channel_id=1, source_target_pairs={{0,6},{2,4},{4,0},{6,2},{1,7},{3,5},{5,1},{7,3},{8,14},{10,12},{12... | collective-permute-start | bytes 98312 | tf_op jit(solution)/shard_map/cond/branch_0_fun/ppermute | solution.py:354
  15.1 4.1 %collective-permute-start.2 = (bf16[128,128]{1,0:T(8,128)(2,1)S(1)}, bf16[128,128]{1,0:T(8,128)(2,1)S(1)}, u32[]{:S(2)}, u32[]{:S(2)}) collective-permute-start(bf16[128,128]{1,0:T(8,128)(2,1)S(1)} %get-tuple-element.112), channel_id=1, source_target_pairs={{0,2},{2,0},{4,6},{6,4},{1,3},{3,1},{5,7},{7,5},{8,10},{10,8},{12,... | collective-permute-start | bytes 98312 | tf_op jit(solution)/shard_map/cond/branch_0_fun/ppermute | solution.py:354

commit v4 on v2

--- a/solution.py
+++ b/solution.py
@@ -321,20 +321,21 @@
         name="multiply",
     )(plan, picked, error_tiles, *returned, *carried)
 
-    def placed(alone, incoming):
+    def placed(alone, incoming, strip, first=0):
+        count = len(incoming) if apart else replicas
         return pl.pallas_call(
-            functools.partial(place, len(incoming), alone, to_row, to_col),
+            functools.partial(place, len(incoming), alone, to_row + first, to_col + first),
             out_shape=jax.ShapeDtypeStruct(strip_shape, jnp.bfloat16),
             in_specs=[VMEM] * (1 + len(incoming)) + [ANY],
             out_specs=ANY,
             scratch_shapes=[
-                pltpu.VMEM((steps,) + tile_shape, jnp.bfloat16),
-                pltpu.SemaphoreType.DMA((steps,)),
+                pltpu.VMEM((count,) + tile_shape, jnp.bfloat16),
+                pltpu.SemaphoreType.DMA((count,)),
             ],
             input_output_aliases={1 + len(incoming): 0},
             compiler_params=SMALL,
             name="place",
-        )(plan, *incoming, cleared)
+        )(plan, *incoming, strip)
 
     def exchanged(blocks):
         moved = [
@@ -345,13 +346,19 @@
 
     if not apart:
         swapped = lax.all_to_all(outgoing[0], "dp", split_axis=0, concat_axis=0, tiled=True)
-        return placed(False, [swapped])
+        return placed(False, [swapped], cleared)
     def branch(wide):
         blocks = [
             outgoing[at if (wide >> wide_bit(at, steps) & 1 if at else wide) else steps + at]
             for at in range(steps)
         ]
-        return lambda: placed(not wide, exchanged(blocks))
+        def run():
+            arrived = exchanged(blocks)
+            if wide:
+                return placed(False, arrived, cleared)
+            return placed(True, arrived[2:], placed(True, arrived[:2], cleared), 2)
+
+        return run
 
     sets = 1 << (wide_bit(steps - 1, steps) + 1)
     return lax.switch(plan[0, 0], [branch(wide) for wide in range(sets)])

time: 20.1 us -> 20.1 us (level)
    pallas_call x1 -> x2, Pallas kernels: 0.77 us -> 0.88 us  [placed(): pl.pallas_call(functools.partial(place, len(incoming), alone, to_row + fi...]
  transfers between devices with their start and end apart: 6 -> 6, of which waited for: 5 -> 5; matrix products, arithmetic and copies ran while one was open for 0% -> 0% of each run, Pallas kernels for 20% -> 21%
where the time goes in v4:
time: 20.1 us; the launch traced here: 19.9 us
  starting transfers between devices  9.19 us (46%)
  waiting for transfers between devices  5.45 us (27%)
  Pallas kernels  5.16 us (26%)
    ppermute x3, starting transfers between devices, exchanged(): lax.ppermute(block, 'dp', list(enumerate(targets)))  4.41 us
    ppermute x2, starting transfers between devices, body(): returned.append(lax.ppermute(cotangent, ('pipe', 'tensor'), pairs))  4.18 us
    ppermute x3, waiting for transfers between devices, exchanged(): lax.ppermute(block, 'dp', list(enumerate(targets)))  3.45 us
    pallas_call x1, Pallas kernels, body(): pl.pallas_call(clear, out_shape=pltpu.HBM(strip_shape, jnp.bfloat16), in_...  2.1 us
    pallas_call x1, Pallas kernels, body(): pl.pallas_call(functools.partial(pick, shifts, apart, width // edge), out...  1.86 us
    ppermute x1, waiting for transfers between devices, body(): lax.ppermute(error, 'tensor', [((group + shift + 1) % groups, group) for...  1.36 us
    pallas_call x2, Pallas kernels, placed(): pl.pallas_call(functools.partial(place, len(incoming), alone, to_row + fi...  0.88 us
    ppermute x2, waiting for transfers between devices, body(): returned.append(lax.ppermute(cotangent, ('pipe', 'tensor'), pairs))  0.64 us
  transfers between devices with their start and end apart: 6, of which 5 were waited for; matrix products, arithmetic and copies ran while one was open for 0% of the time, Pallas kernels for 21%

profile of v4, /device:TPU:0, one launch (start us, length us, event | category | flops | bytes accessed | tf_op | source)
XLA Modules:
  0.0 19.9 jit_solution(13851697333779011494)
XLA Ops:
  0.0 3.3 %collective-permute-start.25 = (bf16[1,2,128,512]{3,2,1,0:T(8,128)(2,1)}, bf16[1,2,128,512]{3,2,1,0:T(8,128)(2,1)S(1)}, u32[]{:S(2)}, u32[]{:S(2)}) collective-permute-start(bf16[1,2,128,512]{3,2,1,0:T(8,128)(2,1)} %param.14), channel_id=1, source_target_pairs={{9,0},{8,1},{17,8},{16,9},{25,16},{24,17},{1,24},{0,25},{11,2},{10... | collective-permute-start | bytes 786440 | tf_op jit(solution)/shard_map/ppermute | solution.py:259
  3.3 0.8 %collective-permute-start.24 = (bf16[1,2,128,512]{3,2,1,0:T(8,128)(2,1)}, bf16[1,2,128,512]{3,2,1,0:T(8,128)(2,1)S(1)}, u32[]{:S(2)}, u32[]{:S(2)}) collective-permute-start(bf16[1,2,128,512]{3,2,1,0:T(8,128)(2,1)} %param.14), channel_id=1, source_target_pairs={{8,0},{9,1},{16,8},{17,9},{24,16},{25,17},{0,24},{1,25},{10,2},{11... | collective-permute-start | bytes 786440 | tf_op jit(solution)/shard_map/ppermute | solution.py:259
  4.2 0.0 copy-start
  4.2 1.9 %pick.1 = (bf16[2,128,256]{2,1,0:T(8,128)(2,1)S(1)}, s32[1,128]{1,0:T(1,128)S(1)}, bf16[1,128,128]{2,1,0:T(8,128)(2,1)S(1)}) custom-call(s32[1,1,2,1,2,4]{5,4,3,2,1,0:T(2,128)} %bitcast.4, s32[1,1,64]{2,1,0:T(1,128)} %owners.1, bf16[1,2,128,8192]{3,2,1,0:T(8,128)(2,1)} %activations.1, bf16[1,1,1,2,1,128,128]{6,5,4,3,2,1,0:T(8,128)(2,1)} %error.1), custom_call_target="tpu_custom_call" | custom-call | tf_op jit(solution)/shard_map/pick/pallas_call | solution.py:263
  6.0 0.6 %collective-permute-start.26 = (bf16[1,128,128]{2,1,0:T(8,128)(2,1)S(1)}, bf16[1,128,128]{2,1,0:T(8,128)(2,1)S(1)}, u32[]{:S(2)}, u32[]{:S(2)}) collective-permute-start(bf16[1,128,128]{2,1,0:T(8,128)(2,1)S(1)} %get-tuple-element.171), channel_id=1, source_target_pairs={{1,0},{0,1},{3,2},{2,3},{5,4},{4,5},{7,6},{6,7},{9,8},{8,9},{11,10... | collective-permute-start | bytes 98312 | tf_op jit(solution)/shard_map/ppermute | solution.py:281
  6.6 2.1 %clear.1 = bf16[1,1,2048,1024]{3,2,1,0:T(8,128)(2,1)} custom-call(bf16[2,128,256]{2,1,0:T(8,128)(2,1)S(1)} %get-tuple-element.170.picked.after), custom_call_target="tpu_custom_call" | custom-call | bytes 4194304 | tf_op jit(solution)/shard_map/clear/pallas_call | solution.py:289
  8.8 1.4 %collective-permute-done.26.refs_2_ = bf16[1,128,128]{2,1,0:T(8,128)(2,1)S(1)} collective-permute-done((bf16[1,128,128]{2,1,0:T(8,128)(2,1)S(1)}, bf16[1,128,128]{2,1,0:T(8,128)(2,1)S(1)}, u32[]{:S(2)}, u32[]{:S(2)}) %collective-permute-start.26) | collective-permute-done | bytes 32800 | tf_op jit(solution)/shard_map/ppermute | solution.py:281
  10.2 0.0 collective-permute-done.25.refs_1_
  10.2 0.6 %collective-permute-done.24.refs_0_ = bf16[1,2,128,512]{3,2,1,0:T(8,128)(2,1)S(1)} collective-permute-done((bf16[1,2,128,512]{3,2,1,0:T(8,128)(2,1)}, bf16[1,2,128,512]{3,2,1,0:T(8,128)(2,1)S(1)}, u32[]{:S(2)}, u32[]{:S(2)}) %collective-permute-start.24) | collective-permute-done | bytes 262176 | tf_op jit(solution)/shard_map/ppermute | solution.py:259
  10.8 0.0 copy-done
  10.8 0.3 %multiply.1 = (f32[128,128]{1,0:T(8,128)S(1)}, f32[128,128]{1,0:T(8,128)S(1)}, f32[128,128]{1,0:T(8,128)S(1)}, f32[128,128]{1,0:T(8,128)S(1)}, bf16[128,128]{1,0...) custom-call(s32[1,128]{1,0:T(1,128)S(1)} %get-tuple-element.169.plan, ...), custom_call_target="tpu_custom_call" | custom-call | tf_op jit(solution)/shard_map/multiply/pallas_call | solution.py:315
  11.1 8.8 %conditional.1 = (bf16[1,1,2048,1024]{3,2,1,0:T(8,128)(2,1)}) conditional(s32[]{:T(128)} %bitcast.1, (bf16[128,128]{1,0:T(8,128)(2,1)S(1)}, bf16[128,128]{1,0:T(8,128)(2,1)S(1)}, bf16[128,128]{1,0:T(8,128)(2,1)S(1)}, s32[1,128]{1,0:T(1,128)S(1)}, bf16[128,128]{1,0:T(8,128)(2,1)S(1)}, ...), branch_computations={%region_0.0_spmd, %region_1.0_spmd, %region_2.0_spmd, %region_3.0_... | conditional | bytes 786560 | solution.py:364
  11.2 2.8 %collective-permute-start.2 = (bf16[128,128]{1,0:T(8,128)(2,1)S(1)}, bf16[128,128]{1,0:T(8,128)(2,1)S(1)}, u32[]{:S(2)}, u32[]{:S(2)}) collective-permute-start(bf16[128,128]{1,0:T(8,128)(2,1)S(1)} %get-tuple-element.112), channel_id=1, source_target_pairs={{0,4},{2,6},{4,2},{6,0},{1,5},{3,7},{5,3},{7,1},{8,12},{10,14},{12... | collective-permute-start | bytes 98312 | tf_op jit(solution)/shard_map/cond/branch_0_fun/ppermute | solution.py:342
  14.0 1.1 %collective-permute-start = (bf16[128,128]{1,0:T(8,128)(2,1)S(1)}, bf16[128,128]{1,0:T(8,128)(2,1)S(1)}, u32[]{:S(2)}, u32[]{:S(2)}) collective-permute-start(bf16[128,128]{1,0:T(8,128)(2,1)S(1)} %get-tuple-element.102), channel_id=1, source_target_pairs={{0,6},{2,4},{4,0},{6,2},{1,7},{3,5},{5,1},{7,3},{8,14},{10,12},{12... | collective-permute-start | bytes 98312 | tf_op jit(solution)/shard_map/cond/branch_0_fun/ppermute | solution.py:342
  15.1 0.5 %collective-permute-start.1 = (bf16[128,128]{1,0:T(8,128)(2,1)S(1)}, bf16[128,128]{1,0:T(8,128)(2,1)S(1)}, u32[]{:S(2)}, u32[]{:S(2)}) collective-permute-start(bf16[128,128]{1,0:T(8,128)(2,1)S(1)} %get-tuple-element.103), channel_id=1, source_target_pairs={{0,2},{2,0},{4,6},{6,4},{1,3},{3,1},{5,7},{7,5},{8,10},{10,8},{12,... | collective-permute-start | bytes 98312 | tf_op jit(solution)/shard_map/cond/branch_0_fun/ppermute | solution.py:342
  15.6 1.5 %collective-permute-done.2.refs_1_ = bf16[128,128]{1,0:T(8,128)(2,1)S(1)} collective-permute-done((bf16[128,128]{1,0:T(8,128)(2,1)S(1)}, bf16[128,128]{1,0:T(8,128)(2,1)S(1)}, u32[]{:S(2)}, u32[]{:S(2)}) %collective-permute-start.2) | collective-permute-done | bytes 32800 | tf_op jit(solution)/shard_map/cond/branch_0_fun/ppermute | solution.py:342
  17.0 0.1 place.9.refs_2_
  17.2 1.6 %collective-permute-done.refs_0_ = bf16[128,128]{1,0:T(8,128)(2,1)S(1)} collective-permute-done((bf16[128,128]{1,0:T(8,128)(2,1)S(1)}, bf16[128,128]{1,0:T(8,128)(2,1)S(1)}, u32[]{:S(2)}, u32[]{:S(2)}) %collective-permute-start) | collective-permute-done | bytes 32800 | tf_op jit(solution)/shard_map/cond/branch_0_fun/ppermute | solution.py:342
  18.8 0.3 %collective-permute-done.1.refs_1_ = bf16[128,128]{1,0:T(8,128)(2,1)S(1)} collective-permute-done((bf16[128,128]{1,0:T(8,128)(2,1)S(1)}, bf16[128,128]{1,0:T(8,128)(2,1)S(1)}, u32[]{:S(2)}, u32[]{:S(2)}) %collective-permute-start.1) | collective-permute-done | bytes 32800 | tf_op jit(solution)/shard_map/cond/branch_0_fun/ppermute | solution.py:342
  19.1 0.7 %place.10 = bf16[1,1,2048,1024]{3,2,1,0:T(8,128)(2,1)} custom-call(s32[1,128]{1,0:T(1,128)S(1)} %get-tuple-element.101.plan, bf16[128,128]{1,0:T(8,128)(2,1)S(1)} %collective-permute-done.refs_0_, bf16[128,128]{1,0:T(8,128)(2,1)S(1)} %collective-permute-done.1.refs_1_, bf16[1,1,2048,1024]{3,2,1,0:T(8,128)(2,1)} %place.9.refs_2_), custom_call_target="tpu_custom_call", output_to_operand_aliasing={{}: (3, {})} | custom-call | tf_op jit(solution)/shard_map/cond/branch_0_fun/place/pallas_call | solution.py:326
Async XLA Ops:
  0.0 10.2 %collective-permute-start.25 = (bf16[1,2,128,512]{3,2,1,0:T(8,128)(2,1)}, bf16[1,2,128,512]{3,2,1,0:T(8,128)(2,1)S(1)}, u32[]{:S(2)}, u32[]{:S(2)}) collective-permute-start(bf16[1,2,128,512]{3,2,1,0:T(8,128)(2,1)} %param.14), channel_id=1, source_target_pairs={{9,0},{8,1},{17,8},{16,9},{25,16},{24,17},{1,24},{0,25},{11,2},{10... | collective-permute-start | bytes 786440 | tf_op jit(solution)/shard_map/ppermute | solution.py:259
  3.3 7.5 %collective-permute-start.24 = (bf16[1,2,128,512]{3,2,1,0:T(8,128)(2,1)}, bf16[1,2,128,512]{3,2,1,0:T(8,128)(2,1)S(1)}, u32[]{:S(2)}, u32[]{:S(2)}) collective-permute-start(bf16[1,2,128,512]{3,2,1,0:T(8,128)(2,1)} %param.14), channel_id=1, source_target_pairs={{8,0},{9,1},{16,8},{17,9},{24,16},{25,17},{0,24},{1,25},{10,2},{11... | collective-permute-start | bytes 786440 | tf_op jit(solution)/shard_map/ppermute | solution.py:259
  4.2 6.6 %copy-start = (bf16[1,1,1,2,1,128,128]{6,5,4,3,2,1,0:T(8,128)(2,1)S(1)}, bf16[1,1,1,2,1,128,128]{6,5,4,3,2,1,0:T(8,128)(2,1)}, u32[]{:S(2)}) copy-start(bf16[1,1,1,2,1,128,128]{6,5,4,3,2,1,0:T(8,128)(2,1)} %error.1) | copy-start | bytes 196612
  6.0 4.1 %collective-permute-start.26 = (bf16[1,128,128]{2,1,0:T(8,128)(2,1)S(1)}, bf16[1,128,128]{2,1,0:T(8,128)(2,1)S(1)}, u32[]{:S(2)}, u32[]{:S(2)}) collective-permute-start(bf16[1,128,128]{2,1,0:T(8,128)(2,1)S(1)} %get-tuple-element.171), channel_id=1, source_target_pairs={{1,0},{0,1},{3,2},{2,3},{5,4},{4,5},{7,6},{6,7},{9,8},{8,9},{11,10... | collective-permute-start | bytes 98312 | tf_op jit(solution)/shard_map/ppermute | solution.py:281
  11.2 5.9 %collective-permute-start.2 = (bf16[128,128]{1,0:T(8,128)(2,1)S(1)}, bf16[128,128]{1,0:T(8,128)(2,1)S(1)}, u32[]{:S(2)}, u32[]{:S(2)}) collective-permute-start(bf16[128,128]{1,0:T(8,128)(2,1)S(1)} %get-tuple-element.112), channel_id=1, source_target_pairs={{0,4},{2,6},{4,2},{6,0},{1,5},{3,7},{5,3},{7,1},{8,12},{10,14},{12... | collective-permute-start | bytes 98312 | tf_op jit(solution)/shard_map/cond/branch_0_fun/ppermute | solution.py:342
  14.0 4.8 %collective-permute-start = (bf16[128,128]{1,0:T(8,128)(2,1)S(1)}, bf16[128,128]{1,0:T(8,128)(2,1)S(1)}, u32[]{:S(2)}, u32[]{:S(2)}) collective-permute-start(bf16[128,128]{1,0:T(8,128)(2,1)S(1)} %get-tuple-element.102), channel_id=1, source_target_pairs={{0,6},{2,4},{4,0},{6,2},{1,7},{3,5},{5,1},{7,3},{8,14},{10,12},{12... | collective-permute-start | bytes 98312 | tf_op jit(solution)/shard_map/cond/branch_0_fun/ppermute | solution.py:342
  15.1 4.1 %collective-permute-start.1 = (bf16[128,128]{1,0:T(8,128)(2,1)S(1)}, bf16[128,128]{1,0:T(8,128)(2,1)S(1)}, u32[]{:S(2)}, u32[]{:S(2)}) collective-permute-start(bf16[128,128]{1,0:T(8,128)(2,1)S(1)} %get-tuple-element.103), channel_id=1, source_target_pairs={{0,2},{2,0},{4,6},{6,4},{1,3},{3,1},{5,7},{7,5},{8,10},{10,8},{12,... | collective-permute-start | bytes 98312 | tf_op jit(solution)/shard_map/cond/branch_0_fun/ppermute | solution.py:342

commit v5 on v4

--- a/solution.py
+++ b/solution.py
@@ -23,18 +23,18 @@
     return pl.ds(pl.multiple_of(index * edge, edge), edge)
 
 
-def rounds(replicas):
+def rounds(replicas, odd=0):
     shifts = [
         tuple((one + step) % replicas for one in range(replicas)) for step in range(1, replicas)
     ]
-    return ROUNDS.get(replicas, shifts)
-
-
-def step_table(replicas):
+    return shifts if odd else ROUNDS.get(replicas, shifts)
+
+
+def step_table(replicas, odd):
     table = []
     for source in range(replicas):
         steps = [0] * replicas
-        for step, targets in reversed(list(enumerate(rounds(replicas), 1))):
+        for step, targets in reversed(list(enumerate(rounds(replicas, odd), 1))):
             steps[targets[source]] = step
         table.append(sum(step << 4 * target for target, step in enumerate(steps)))
     return table
@@ -83,7 +83,11 @@
             owner += (row >= one * owned).astype(jnp.int32)
         return owner
 
-    table = step_table(replicas) if apart else []
+    odd = lax.rem(lax.axis_index("pipe"), 2) > 0
+    table = [
+        jnp.where(odd, other, packed)
+        for packed, other in zip(step_table(replicas, 0), step_table(replicas, 1))
+    ] if apart else []
     mine = jnp.int32(0)
     for source, packed in enumerate(table):
         mine = jnp.where(replica == source, packed, mine)
@@ -105,7 +109,7 @@
             place_col = jnp.where(
                 here, picks[0, 0, group, slot, 1, origin] + group * per_group, place_col
             )
-        step = (jnp.int32(table[origin]) >> 4 * replica) & 15 if apart else origin
+        step = (table[origin] >> 4 * replica) & 15 if apart else origin
         planned = jnp.where(lane == to_row + step, place_row, planned)
         planned = jnp.where(lane == to_col + step, place_col, planned)
 
@@ -125,7 +129,7 @@
         for at, spot in enumerate(spots):
             origin, (group, slot) = at // len(tiles), tiles[at % len(tiles)]
             owner = owner_of(owners[0, 0, picks[0, 0, group, slot, 0, origin]])
-            step = (jnp.int32(table[origin]) >> 4 * owner) & 15
+            step = (table[origin] >> 4 * owner) & 15
             bit = jnp.int32(1) << wide_bit(jnp.maximum(step, 1), steps)
             wide = jnp.where((seen[spot] > 1) & (step > 0), wide | bit, wide)
     plan[...] = jnp.where(lane == 0, wide, planned)
@@ -338,10 +342,14 @@
         )(plan, *incoming, strip)
 
     def exchanged(blocks):
-        moved = [
-            lax.ppermute(block, "dp", list(enumerate(targets)))
-            for block, targets in zip(blocks[1:], rounds(replicas))
-        ]
+        moved = []
+        for at, block in enumerate(blocks[1:]):
+            pairs = [
+                (section * replicas + source, section * replicas + target)
+                for section in range(sections)
+                for source, target in enumerate(rounds(replicas, section % 2)[at])
+            ]
+            moved.append(lax.ppermute(block, ("pipe", "dp"), pairs))
         return [blocks[0], *moved]
 
     if not apart:

time: 20.1 us -> 20.1 us (level)
  waiting for transfers between devices: 5.45 us -> 4.84 us
  Pallas kernels: 5.16 us -> 5.76 us
    ppermute x3, waiting for transfers between devices: 3.45 us -> 2.84 us  [exchanged(): moved.append(lax.ppermute(block, ('pipe', 'dp'), pairs))]
    pallas_call x2, Pallas kernels: 0.88 us -> 1.48 us  [placed(): pl.pallas_call(functools.partial(place, len(incoming), alone, to_row + fi...]
  transfers between devices with their start and end apart: 6 -> 6, of which waited for: 5 -> 5; matrix products, arithmetic and copies ran while one was open for 0% -> 0% of each run, Pallas kernels for 21% -> 24%
where the time goes in v5:
time: 20.1 us; the launch traced here: 19.9 us
  starting transfers between devices  9.18 us (46%)
  Pallas kernels  5.76 us (29%)
  waiting for transfers between devices  4.84 us (24%)
    ppermute x3, starting transfers between devices, exchanged(): moved.append(lax.ppermute(block, ('pipe', 'dp'), pairs))  4.41 us
    ppermute x2, starting transfers between devices, body(): returned.append(lax.ppermute(cotangent, ('pipe', 'tensor'), pairs))  4.18 us
    ppermute x3, waiting for transfers between devices, exchanged(): moved.append(lax.ppermute(block, ('pipe', 'dp'), pairs))  2.84 us
    pallas_call x1, Pallas kernels, body(): pl.pallas_call(clear, out_shape=pltpu.HBM(strip_shape, jnp.bfloat16), in_...  2.1 us
    pallas_call x1, Pallas kernels, body(): pl.pallas_call(functools.partial(pick, shifts, apart, width // edge), out...  1.86 us
    pallas_call x2, Pallas kernels, placed(): pl.pallas_call(functools.partial(place, len(incoming), alone, to_row + fi...  1.48 us
    ppermute x1, waiting for transfers between devices, body(): lax.ppermute(error, 'tensor', [((group + shift + 1) % groups, group) for...  1.36 us
    ppermute x2, waiting for transfers between devices, body(): returned.append(lax.ppermute(cotangent, ('pipe', 'tensor'), pairs))  0.64 us
  transfers between devices with their start and end apart: 6, of which 5 were waited for; matrix products, arithmetic and copies ran while one was open for 0% of the time, Pallas kernels for 24%

profile of v5, /device:TPU:0, one launch (start us, length us, event | category | flops | bytes accessed | tf_op | source)
XLA Modules:
  0.0 19.9 jit_solution(8346826279131713601)
XLA Ops:
  0.0 3.3 %collective-permute-start.25 = (bf16[1,2,128,512]{3,2,1,0:T(8,128)(2,1)}, bf16[1,2,128,512]{3,2,1,0:T(8,128)(2,1)S(1)}, u32[]{:S(2)}, u32[]{:S(2)}) collective-permute-start(bf16[1,2,128,512]{3,2,1,0:T(8,128)(2,1)} %param.14), channel_id=1, source_target_pairs={{9,0},{8,1},{17,8},{16,9},{25,16},{24,17},{1,24},{0,25},{11,2},{10... | collective-permute-start | bytes 786440 | tf_op jit(solution)/shard_map/ppermute | solution.py:263
  3.3 0.8 %collective-permute-start.24 = (bf16[1,2,128,512]{3,2,1,0:T(8,128)(2,1)}, bf16[1,2,128,512]{3,2,1,0:T(8,128)(2,1)S(1)}, u32[]{:S(2)}, u32[]{:S(2)}) collective-permute-start(bf16[1,2,128,512]{3,2,1,0:T(8,128)(2,1)} %param.14), channel_id=1, source_target_pairs={{8,0},{9,1},{16,8},{17,9},{24,16},{25,17},{0,24},{1,25},{10,2},{11... | collective-permute-start | bytes 786440 | tf_op jit(solution)/shard_map/ppermute | solution.py:263
  4.2 0.0 copy-start
  4.2 1.9 %pick.1 = (bf16[2,128,256]{2,1,0:T(8,128)(2,1)S(1)}, s32[1,128]{1,0:T(1,128)S(1)}, bf16[1,128,128]{2,1,0:T(8,128)(2,1)S(1)}) custom-call(s32[1,1,2,1,2,4]{5,4,3,2,1,0:T(2,128)} %bitcast.4, s32[1,1,64]{2,1,0:T(1,128)} %owners.1, bf16[1,2,128,8192]{3,2,1,0:T(8,128)(2,1)} %activations.1, bf16[1,1,1,2,1,128,128]{6,5,4,3,2,1,0:T(8,128)(2,1)} %error.1), custom_call_target="tpu_custom_call" | custom-call | tf_op jit(solution)/shard_map/pick/pallas_call | solution.py:267
  6.0 0.6 %collective-permute-start.26 = (bf16[1,128,128]{2,1,0:T(8,128)(2,1)S(1)}, bf16[1,128,128]{2,1,0:T(8,128)(2,1)S(1)}, u32[]{:S(2)}, u32[]{:S(2)}) collective-permute-start(bf16[1,128,128]{2,1,0:T(8,128)(2,1)S(1)} %get-tuple-element.171), channel_id=1, source_target_pairs={{1,0},{0,1},{3,2},{2,3},{5,4},{4,5},{7,6},{6,7},{9,8},{8,9},{11,10... | collective-permute-start | bytes 98312 | tf_op jit(solution)/shard_map/ppermute | solution.py:285
  6.6 2.1 %clear.1 = bf16[1,1,2048,1024]{3,2,1,0:T(8,128)(2,1)} custom-call(bf16[2,128,256]{2,1,0:T(8,128)(2,1)S(1)} %get-tuple-element.170.picked.after), custom_call_target="tpu_custom_call" | custom-call | bytes 4194304 | tf_op jit(solution)/shard_map/clear/pallas_call | solution.py:293
  8.8 1.4 %collective-permute-done.26.refs_2_ = bf16[1,128,128]{2,1,0:T(8,128)(2,1)S(1)} collective-permute-done((bf16[1,128,128]{2,1,0:T(8,128)(2,1)S(1)}, bf16[1,128,128]{2,1,0:T(8,128)(2,1)S(1)}, u32[]{:S(2)}, u32[]{:S(2)}) %collective-permute-start.26) | collective-permute-done | bytes 32800 | tf_op jit(solution)/shard_map/ppermute | solution.py:285
  10.2 0.0 collective-permute-done.25.refs_1_
  10.2 0.6 %collective-permute-done.24.refs_0_ = bf16[1,2,128,512]{3,2,1,0:T(8,128)(2,1)S(1)} collective-permute-done((bf16[1,2,128,512]{3,2,1,0:T(8,128)(2,1)}, bf16[1,2,128,512]{3,2,1,0:T(8,128)(2,1)S(1)}, u32[]{:S(2)}, u32[]{:S(2)}) %collective-permute-start.24) | collective-permute-done | bytes 262176 | tf_op jit(solution)/shard_map/ppermute | solution.py:263
  10.8 0.0 copy-done
  10.8 0.3 %multiply.1 = (f32[128,128]{1,0:T(8,128)S(1)}, f32[128,128]{1,0:T(8,128)S(1)}, f32[128,128]{1,0:T(8,128)S(1)}, f32[128,128]{1,0:T(8,128)S(1)}, bf16[128,128]{1,0...) custom-call(s32[1,128]{1,0:T(1,128)S(1)} %get-tuple-element.169.plan, ...), custom_call_target="tpu_custom_call" | custom-call | tf_op jit(solution)/shard_map/multiply/pallas_call | solution.py:319
  11.1 8.8 %conditional.1 = (bf16[1,1,2048,1024]{3,2,1,0:T(8,128)(2,1)}) conditional(s32[]{:T(128)} %bitcast.1, (bf16[128,128]{1,0:T(8,128)(2,1)S(1)}, bf16[128,128]{1,0:T(8,128)(2,1)S(1)}, bf16[128,128]{1,0:T(8,128)(2,1)S(1)}, s32[1,128]{1,0:T(1,128)S(1)}, bf16[128,128]{1,0:T(8,128)(2,1)S(1)}, ...), branch_computations={%region_0.0_spmd, %region_1.0_spmd, %region_2.0_spmd, %region_3.0_... | conditional | bytes 786560 | solution.py:372
  11.2 2.8 %collective-permute-start.2 = (bf16[128,128]{1,0:T(8,128)(2,1)S(1)}, bf16[128,128]{1,0:T(8,128)(2,1)S(1)}, u32[]{:S(2)}, u32[]{:S(2)}) collective-permute-start(bf16[128,128]{1,0:T(8,128)(2,1)S(1)} %get-tuple-element.112), channel_id=1, source_target_pairs={{0,4},{2,6},{4,2},{6,0},{8,10},{10,12},{12,14},{14,8},{16,20},{18,... | collective-permute-start | bytes 98312 | tf_op jit(solution)/shard_map/cond/branch_0_fun/ppermute | solution.py:352
  14.0 1.1 %collective-permute-start = (bf16[128,128]{1,0:T(8,128)(2,1)S(1)}, bf16[128,128]{1,0:T(8,128)(2,1)S(1)}, u32[]{:S(2)}, u32[]{:S(2)}) collective-permute-start(bf16[128,128]{1,0:T(8,128)(2,1)S(1)} %get-tuple-element.102), channel_id=1, source_target_pairs={{0,6},{2,4},{4,0},{6,2},{8,12},{10,14},{12,8},{14,10},{16,22},{18,... | collective-permute-start | bytes 98312 | tf_op jit(solution)/shard_map/cond/branch_0_fun/ppermute | solution.py:352
  15.1 0.5 %collective-permute-start.1 = (bf16[128,128]{1,0:T(8,128)(2,1)S(1)}, bf16[128,128]{1,0:T(8,128)(2,1)S(1)}, u32[]{:S(2)}, u32[]{:S(2)}) collective-permute-start(bf16[128,128]{1,0:T(8,128)(2,1)S(1)} %get-tuple-element.103), channel_id=1, source_target_pairs={{0,2},{2,0},{4,6},{6,4},{8,14},{10,8},{12,10},{14,12},{16,18},{18,... | collective-permute-start | bytes 98312 | tf_op jit(solution)/shard_map/cond/branch_0_fun/ppermute | solution.py:352
  15.6 1.5 %collective-permute-done.2.refs_1_ = bf16[128,128]{1,0:T(8,128)(2,1)S(1)} collective-permute-done((bf16[128,128]{1,0:T(8,128)(2,1)S(1)}, bf16[128,128]{1,0:T(8,128)(2,1)S(1)}, u32[]{:S(2)}, u32[]{:S(2)}) %collective-permute-start.2) | collective-permute-done | bytes 32800 | tf_op jit(solution)/shard_map/cond/branch_0_fun/ppermute | solution.py:352
  17.1 0.7 %place.9.refs_2_ = bf16[1,1,2048,1024]{3,2,1,0:T(8,128)(2,1)} custom-call(s32[1,128]{1,0:T(1,128)S(1)} %get-tuple-element.101.plan, bf16[128,128]{1,0:T(8,128)(2,1)S(1)} %get-tuple-element.104.refs_0_, bf16[128,128]{1,0:T(8,128)(2,1)S(1)} %collective-permute-done.2.refs_1_, ...), custom_call_target="tpu_custom_call", output_to_operand_aliasing={{}: (3, {})} | custom-call | tf_op jit(solution)/shard_map/cond/branch_0_fun/place/pallas_call | solution.py:330
  17.8 1.0 %collective-permute-done.refs_0_ = bf16[128,128]{1,0:T(8,128)(2,1)S(1)} collective-permute-done((bf16[128,128]{1,0:T(8,128)(2,1)S(1)}, bf16[128,128]{1,0:T(8,128)(2,1)S(1)}, u32[]{:S(2)}, u32[]{:S(2)}) %collective-permute-start) | collective-permute-done | bytes 32800 | tf_op jit(solution)/shard_map/cond/branch_0_fun/ppermute | solution.py:352
  18.8 0.3 %collective-permute-done.1.refs_1_ = bf16[128,128]{1,0:T(8,128)(2,1)S(1)} collective-permute-done((bf16[128,128]{1,0:T(8,128)(2,1)S(1)}, bf16[128,128]{1,0:T(8,128)(2,1)S(1)}, u32[]{:S(2)}, u32[]{:S(2)}) %collective-permute-start.1) | collective-permute-done | bytes 32800 | tf_op jit(solution)/shard_map/cond/branch_0_fun/ppermute | solution.py:352
  19.1 0.7 %place.10 = bf16[1,1,2048,1024]{3,2,1,0:T(8,128)(2,1)} custom-call(s32[1,128]{1,0:T(1,128)S(1)} %get-tuple-element.101.plan, bf16[128,128]{1,0:T(8,128)(2,1)S(1)} %collective-permute-done.refs_0_, bf16[128,128]{1,0:T(8,128)(2,1)S(1)} %collective-permute-done.1.refs_1_, bf16[1,1,2048,1024]{3,2,1,0:T(8,128)(2,1)} %place.9.refs_2_), custom_call_target="tpu_custom_call", output_to_operand_aliasing={{}: (3, {})} | custom-call | tf_op jit(solution)/shard_map/cond/branch_0_fun/place/pallas_call | solution.py:330
Async XLA Ops:
  0.0 10.2 %collective-permute-start.25 = (bf16[1,2,128,512]{3,2,1,0:T(8,128)(2,1)}, bf16[1,2,128,512]{3,2,1,0:T(8,128)(2,1)S(1)}, u32[]{:S(2)}, u32[]{:S(2)}) collective-permute-start(bf16[1,2,128,512]{3,2,1,0:T(8,128)(2,1)} %param.14), channel_id=1, source_target_pairs={{9,0},{8,1},{17,8},{16,9},{25,16},{24,17},{1,24},{0,25},{11,2},{10... | collective-permute-start | bytes 786440 | tf_op jit(solution)/shard_map/ppermute | solution.py:263
  3.3 7.5 %collective-permute-start.24 = (bf16[1,2,128,512]{3,2,1,0:T(8,128)(2,1)}, bf16[1,2,128,512]{3,2,1,0:T(8,128)(2,1)S(1)}, u32[]{:S(2)}, u32[]{:S(2)}) collective-permute-start(bf16[1,2,128,512]{3,2,1,0:T(8,128)(2,1)} %param.14), channel_id=1, source_target_pairs={{8,0},{9,1},{16,8},{17,9},{24,16},{25,17},{0,24},{1,25},{10,2},{11... | collective-permute-start | bytes 786440 | tf_op jit(solution)/shard_map/ppermute | solution.py:263
  4.2 6.6 %copy-start = (bf16[1,1,1,2,1,128,128]{6,5,4,3,2,1,0:T(8,128)(2,1)S(1)}, bf16[1,1,1,2,1,128,128]{6,5,4,3,2,1,0:T(8,128)(2,1)}, u32[]{:S(2)}) copy-start(bf16[1,1,1,2,1,128,128]{6,5,4,3,2,1,0:T(8,128)(2,1)} %error.1) | copy-start | bytes 196612
  6.0 4.1 %collective-permute-start.26 = (bf16[1,128,128]{2,1,0:T(8,128)(2,1)S(1)}, bf16[1,128,128]{2,1,0:T(8,128)(2,1)S(1)}, u32[]{:S(2)}, u32[]{:S(2)}) collective-permute-start(bf16[1,128,128]{2,1,0:T(8,128)(2,1)S(1)} %get-tuple-element.171), channel_id=1, source_target_pairs={{1,0},{0,1},{3,2},{2,3},{5,4},{4,5},{7,6},{6,7},{9,8},{8,9},{11,10... | collective-permute-start | bytes 98312 | tf_op jit(solution)/shard_map/ppermute | solution.py:285
  11.2 5.9 %collective-permute-start.2 = (bf16[128,128]{1,0:T(8,128)(2,1)S(1)}, bf16[128,128]{1,0:T(8,128)(2,1)S(1)}, u32[]{:S(2)}, u32[]{:S(2)}) collective-permute-start(bf16[128,128]{1,0:T(8,128)(2,1)S(1)} %get-tuple-element.112), channel_id=1, source_target_pairs={{0,4},{2,6},{4,2},{6,0},{8,10},{10,12},{12,14},{14,8},{16,20},{18,... | collective-permute-start | bytes 98312 | tf_op jit(solution)/shard_map/cond/branch_0_fun/ppermute | solution.py:352
  14.0 4.8 %collective-permute-start = (bf16[128,128]{1,0:T(8,128)(2,1)S(1)}, bf16[128,128]{1,0:T(8,128)(2,1)S(1)}, u32[]{:S(2)}, u32[]{:S(2)}) collective-permute-start(bf16[128,128]{1,0:T(8,128)(2,1)S(1)} %get-tuple-element.102), channel_id=1, source_target_pairs={{0,6},{2,4},{4,0},{6,2},{8,12},{10,14},{12,8},{14,10},{16,22},{18,... | collective-permute-start | bytes 98312 | tf_op jit(solution)/shard_map/cond/branch_0_fun/ppermute | solution.py:352
  15.1 4.1 %collective-permute-start.1 = (bf16[128,128]{1,0:T(8,128)(2,1)S(1)}, bf16[128,128]{1,0:T(8,128)(2,1)S(1)}, u32[]{:S(2)}, u32[]{:S(2)}) collective-permute-start(bf16[128,128]{1,0:T(8,128)(2,1)S(1)} %get-tuple-element.103), channel_id=1, source_target_pairs={{0,2},{2,0},{4,6},{6,4},{8,14},{10,8},{12,10},{14,12},{16,18},{18,... | collective-permute-start | bytes 98312 | tf_op jit(solution)/shard_map/cond/branch_0_fun/ppermute | solution.py:352

commit v6 on v4

--- a/solution.py
+++ b/solution.py
@@ -11,7 +11,7 @@
 SMEM = pl.BlockSpec(memory_space=pltpu.SMEM)
 ANY = pl.BlockSpec(memory_space=pl.ANY)
 MOST_STEPS = 8
-ROUNDS = {4: [(2, 3, 1, 0), (3, 2, 0, 1), (1, 0, 3, 2)]}
+ROUNDS = {4: [(1, 3, 0, 2), (3, 2, 1, 0), (2, 0, 3, 1)]}
 SMALL = pltpu.CompilerParams(vmem_limit_bytes=4 << 20)
 
 

time: 20.1 us -> 20.3 us (level)
  waiting for transfers between devices: 5.45 us -> 3.59 us
  starting transfers between devices: 9.19 us -> 10.6 us
  Pallas kernels: 5.16 us -> 5.76 us
    ppermute x3, waiting for transfers between devices: 3.45 us -> 1.59 us  [exchanged(): lax.ppermute(block, 'dp', list(enumerate(targets)))]
    ppermute x3, starting transfers between devices: 4.41 us -> 5.87 us  [exchanged(): lax.ppermute(block, 'dp', list(enumerate(targets)))]
    pallas_call x2, Pallas kernels: 0.88 us -> 1.48 us  [placed(): pl.pallas_call(functools.partial(place, len(incoming), alone, to_row + fi...]
  transfers between devices with their start and end apart: 6 -> 6, of which waited for: 5 -> 4; matrix products, arithmetic and copies ran while one was open for 0% -> 0% of each run, Pallas kernels for 21% -> 23%
where the time goes in v6:
time: 20.3 us; the launch traced here: 20.1 us
  starting transfers between devices  10.6 us (52%)
  Pallas kernels  5.76 us (28%)
  waiting for transfers between devices  3.59 us (18%)
    ppermute x3, starting transfers between devices, exchanged(): lax.ppermute(block, 'dp', list(enumerate(targets)))  5.87 us
    ppermute x2, starting transfers between devices, body(): returned.append(lax.ppermute(cotangent, ('pipe', 'tensor'), pairs))  4.18 us
    pallas_call x1, Pallas kernels, body(): pl.pallas_call(clear, out_shape=pltpu.HBM(strip_shape, jnp.bfloat16), in_...  2.1 us
    pallas_call x1, Pallas kernels, body(): pl.pallas_call(functools.partial(pick, shifts, apart, width // edge), out...  1.86 us
    ppermute x3, waiting for transfers between devices, exchanged(): lax.ppermute(block, 'dp', list(enumerate(targets)))  1.59 us
    pallas_call x2, Pallas kernels, placed(): pl.pallas_call(functools.partial(place, len(incoming), alone, to_row + fi...  1.48 us
    ppermute x1, waiting for transfers between devices, body(): lax.ppermute(error, 'tensor', [((group + shift + 1) % groups, group) for...  1.36 us
    ppermute x2, waiting for transfers between devices, body(): returned.append(lax.ppermute(cotangent, ('pipe', 'tensor'), pairs))  0.64 us
  transfers between devices with their start and end apart: 6, of which 4 were waited for; matrix products, arithmetic and copies ran while one was open for 0% of the time, Pallas kernels for 23%

profile of v6, /device:TPU:0, one launch (start us, length us, event | category | flops | bytes accessed | tf_op | source)
XLA Modules:
  0.0 20.1 jit_solution(10151487588220793576)
XLA Ops:
  0.0 3.3 %collective-permute-start.25 = (bf16[1,2,128,512]{3,2,1,0:T(8,128)(2,1)}, bf16[1,2,128,512]{3,2,1,0:T(8,128)(2,1)S(1)}, u32[]{:S(2)}, u32[]{:S(2)}) collective-permute-start(bf16[1,2,128,512]{3,2,1,0:T(8,128)(2,1)} %param.14), channel_id=1, source_target_pairs={{9,0},{8,1},{17,8},{16,9},{25,16},{24,17},{1,24},{0,25},{11,2},{10... | collective-permute-start | bytes 786440 | tf_op jit(solution)/shard_map/ppermute | solution.py:259
  3.3 0.8 %collective-permute-start.24 = (bf16[1,2,128,512]{3,2,1,0:T(8,128)(2,1)}, bf16[1,2,128,512]{3,2,1,0:T(8,128)(2,1)S(1)}, u32[]{:S(2)}, u32[]{:S(2)}) collective-permute-start(bf16[1,2,128,512]{3,2,1,0:T(8,128)(2,1)} %param.14), channel_id=1, source_target_pairs={{8,0},{9,1},{16,8},{17,9},{24,16},{25,17},{0,24},{1,25},{10,2},{11... | collective-permute-start | bytes 786440 | tf_op jit(solution)/shard_map/ppermute | solution.py:259
  4.2 0.0 copy-start
  4.2 1.9 %pick.1 = (bf16[2,128,256]{2,1,0:T(8,128)(2,1)S(1)}, s32[1,128]{1,0:T(1,128)S(1)}, bf16[1,128,128]{2,1,0:T(8,128)(2,1)S(1)}) custom-call(s32[1,1,2,1,2,4]{5,4,3,2,1,0:T(2,128)} %bitcast.4, s32[1,1,64]{2,1,0:T(1,128)} %owners.1, bf16[1,2,128,8192]{3,2,1,0:T(8,128)(2,1)} %activations.1, bf16[1,1,1,2,1,128,128]{6,5,4,3,2,1,0:T(8,128)(2,1)} %error.1), custom_call_target="tpu_custom_call" | custom-call | tf_op jit(solution)/shard_map/pick/pallas_call | solution.py:263
  6.0 0.6 %collective-permute-start.26 = (bf16[1,128,128]{2,1,0:T(8,128)(2,1)S(1)}, bf16[1,128,128]{2,1,0:T(8,128)(2,1)S(1)}, u32[]{:S(2)}, u32[]{:S(2)}) collective-permute-start(bf16[1,128,128]{2,1,0:T(8,128)(2,1)S(1)} %get-tuple-element.171), channel_id=1, source_target_pairs={{1,0},{0,1},{3,2},{2,3},{5,4},{4,5},{7,6},{6,7},{9,8},{8,9},{11,10... | collective-permute-start | bytes 98312 | tf_op jit(solution)/shard_map/ppermute | solution.py:281
  6.6 2.1 %clear.1 = bf16[1,1,2048,1024]{3,2,1,0:T(8,128)(2,1)} custom-call(bf16[2,128,256]{2,1,0:T(8,128)(2,1)S(1)} %get-tuple-element.170.picked.after), custom_call_target="tpu_custom_call" | custom-call | bytes 4194304 | tf_op jit(solution)/shard_map/clear/pallas_call | solution.py:289
  8.8 1.4 %collective-permute-done.26.refs_2_ = bf16[1,128,128]{2,1,0:T(8,128)(2,1)S(1)} collective-permute-done((bf16[1,128,128]{2,1,0:T(8,128)(2,1)S(1)}, bf16[1,128,128]{2,1,0:T(8,128)(2,1)S(1)}, u32[]{:S(2)}, u32[]{:S(2)}) %collective-permute-start.26) | collective-permute-done | bytes 32800 | tf_op jit(solution)/shard_map/ppermute | solution.py:281
  10.2 0.0 collective-permute-done.25.refs_1_
  10.2 0.6 %collective-permute-done.24.refs_0_ = bf16[1,2,128,512]{3,2,1,0:T(8,128)(2,1)S(1)} collective-permute-done((bf16[1,2,128,512]{3,2,1,0:T(8,128)(2,1)}, bf16[1,2,128,512]{3,2,1,0:T(8,128)(2,1)S(1)}, u32[]{:S(2)}, u32[]{:S(2)}) %collective-permute-start.24) | collective-permute-done | bytes 262176 | tf_op jit(solution)/shard_map/ppermute | solution.py:259
  10.8 0.0 copy-done
  10.8 0.3 %multiply.1 = (f32[128,128]{1,0:T(8,128)S(1)}, f32[128,128]{1,0:T(8,128)S(1)}, f32[128,128]{1,0:T(8,128)S(1)}, f32[128,128]{1,0:T(8,128)S(1)}, bf16[128,128]{1,0...) custom-call(s32[1,128]{1,0:T(1,128)S(1)} %get-tuple-element.169.plan, ...), custom_call_target="tpu_custom_call" | custom-call | tf_op jit(solution)/shard_map/multiply/pallas_call | solution.py:315
  11.1 9.0 %conditional.1 = (bf16[1,1,2048,1024]{3,2,1,0:T(8,128)(2,1)}) conditional(s32[]{:T(128)} %bitcast.1, (bf16[128,128]{1,0:T(8,128)(2,1)S(1)}, bf16[128,128]{1,0:T(8,128)(2,1)S(1)}, bf16[128,128]{1,0:T(8,128)(2,1)S(1)}, s32[1,128]{1,0:T(1,128)S(1)}, bf16[128,128]{1,0:T(8,128)(2,1)S(1)}, ...), branch_computations={%region_0.0_spmd, %region_1.0_spmd, %region_2.0_spmd, %region_3.0_... | conditional | bytes 786560 | solution.py:364
  11.2 1.8 %collective-permute-start.2 = (bf16[128,128]{1,0:T(8,128)(2,1)S(1)}, bf16[128,128]{1,0:T(8,128)(2,1)S(1)}, u32[]{:S(2)}, u32[]{:S(2)}) collective-permute-start(bf16[128,128]{1,0:T(8,128)(2,1)S(1)} %get-tuple-element.112), channel_id=1, source_target_pairs={{0,2},{2,6},{4,0},{6,4},{1,3},{3,7},{5,1},{7,5},{8,10},{10,14},{12... | collective-permute-start | bytes 98312 | tf_op jit(solution)/shard_map/cond/branch_0_fun/ppermute | solution.py:342
  13.0 2.5 %collective-permute-start = (bf16[128,128]{1,0:T(8,128)(2,1)S(1)}, bf16[128,128]{1,0:T(8,128)(2,1)S(1)}, u32[]{:S(2)}, u32[]{:S(2)}) collective-permute-start(bf16[128,128]{1,0:T(8,128)(2,1)S(1)} %get-tuple-element.102), channel_id=1, source_target_pairs={{0,6},{2,4},{4,2},{6,0},{1,7},{3,5},{5,3},{7,1},{8,14},{10,12},{12... | collective-permute-start | bytes 98312 | tf_op jit(solution)/shard_map/cond/branch_0_fun/ppermute | solution.py:342
  15.4 1.6 %collective-permute-start.1 = (bf16[128,128]{1,0:T(8,128)(2,1)S(1)}, bf16[128,128]{1,0:T(8,128)(2,1)S(1)}, u32[]{:S(2)}, u32[]{:S(2)}) collective-permute-start(bf16[128,128]{1,0:T(8,128)(2,1)S(1)} %get-tuple-element.103), channel_id=1, source_target_pairs={{0,4},{2,0},{4,6},{6,2},{1,5},{3,1},{5,7},{7,3},{8,12},{10,8},{12,... | collective-permute-start | bytes 98312 | tf_op jit(solution)/shard_map/cond/branch_0_fun/ppermute | solution.py:342
  17.0 0.0 collective-permute-done.2.refs_1_
  17.0 0.7 %place.9.refs_2_ = bf16[1,1,2048,1024]{3,2,1,0:T(8,128)(2,1)} custom-call(s32[1,128]{1,0:T(1,128)S(1)} %get-tuple-element.101.plan, bf16[128,128]{1,0:T(8,128)(2,1)S(1)} %get-tuple-element.104.refs_0_, bf16[128,128]{1,0:T(8,128)(2,1)S(1)} %collective-permute-done.2.refs_1_, ...), custom_call_target="tpu_custom_call", output_to_operand_aliasing={{}: (3, {})} | custom-call | tf_op jit(solution)/shard_map/cond/branch_0_fun/place/pallas_call | solution.py:326
  17.8 0.9 %collective-permute-done.refs_0_ = bf16[128,128]{1,0:T(8,128)(2,1)S(1)} collective-permute-done((bf16[128,128]{1,0:T(8,128)(2,1)S(1)}, bf16[128,128]{1,0:T(8,128)(2,1)S(1)}, u32[]{:S(2)}, u32[]{:S(2)}) %collective-permute-start) | collective-permute-done | bytes 32800 | tf_op jit(solution)/shard_map/cond/branch_0_fun/ppermute | solution.py:342
  18.7 0.7 %collective-permute-done.1.refs_1_ = bf16[128,128]{1,0:T(8,128)(2,1)S(1)} collective-permute-done((bf16[128,128]{1,0:T(8,128)(2,1)S(1)}, bf16[128,128]{1,0:T(8,128)(2,1)S(1)}, u32[]{:S(2)}, u32[]{:S(2)}) %collective-permute-start.1) | collective-permute-done | bytes 32800 | tf_op jit(solution)/shard_map/cond/branch_0_fun/ppermute | solution.py:342
  19.4 0.7 %place.10 = bf16[1,1,2048,1024]{3,2,1,0:T(8,128)(2,1)} custom-call(s32[1,128]{1,0:T(1,128)S(1)} %get-tuple-element.101.plan, bf16[128,128]{1,0:T(8,128)(2,1)S(1)} %collective-permute-done.refs_0_, bf16[128,128]{1,0:T(8,128)(2,1)S(1)} %collective-permute-done.1.refs_1_, bf16[1,1,2048,1024]{3,2,1,0:T(8,128)(2,1)} %place.9.refs_2_), custom_call_target="tpu_custom_call", output_to_operand_aliasing={{}: (3, {})} | custom-call | tf_op jit(solution)/shard_map/cond/branch_0_fun/place/pallas_call | solution.py:326
Async XLA Ops:
  0.0 10.2 %collective-permute-start.25 = (bf16[1,2,128,512]{3,2,1,0:T(8,128)(2,1)}, bf16[1,2,128,512]{3,2,1,0:T(8,128)(2,1)S(1)}, u32[]{:S(2)}, u32[]{:S(2)}) collective-permute-start(bf16[1,2,128,512]{3,2,1,0:T(8,128)(2,1)} %param.14), channel_id=1, source_target_pairs={{9,0},{8,1},{17,8},{16,9},{25,16},{24,17},{1,24},{0,25},{11,2},{10... | collective-permute-start | bytes 786440 | tf_op jit(solution)/shard_map/ppermute | solution.py:259
  3.3 7.5 %collective-permute-start.24 = (bf16[1,2,128,512]{3,2,1,0:T(8,128)(2,1)}, bf16[1,2,128,512]{3,2,1,0:T(8,128)(2,1)S(1)}, u32[]{:S(2)}, u32[]{:S(2)}) collective-permute-start(bf16[1,2,128,512]{3,2,1,0:T(8,128)(2,1)} %param.14), channel_id=1, source_target_pairs={{8,0},{9,1},{16,8},{17,9},{24,16},{25,17},{0,24},{1,25},{10,2},{11... | collective-permute-start | bytes 786440 | tf_op jit(solution)/shard_map/ppermute | solution.py:259
  4.2 6.6 %copy-start = (bf16[1,1,1,2,1,128,128]{6,5,4,3,2,1,0:T(8,128)(2,1)S(1)}, bf16[1,1,1,2,1,128,128]{6,5,4,3,2,1,0:T(8,128)(2,1)}, u32[]{:S(2)}) copy-start(bf16[1,1,1,2,1,128,128]{6,5,4,3,2,1,0:T(8,128)(2,1)} %error.1) | copy-start | bytes 196612
  6.0 4.1 %collective-permute-start.26 = (bf16[1,128,128]{2,1,0:T(8,128)(2,1)S(1)}, bf16[1,128,128]{2,1,0:T(8,128)(2,1)S(1)}, u32[]{:S(2)}, u32[]{:S(2)}) collective-permute-start(bf16[1,128,128]{2,1,0:T(8,128)(2,1)S(1)} %get-tuple-element.171), channel_id=1, source_target_pairs={{1,0},{0,1},{3,2},{2,3},{5,4},{4,5},{7,6},{6,7},{9,8},{8,9},{11,10... | collective-permute-start | bytes 98312 | tf_op jit(solution)/shard_map/ppermute | solution.py:281
  11.2 5.9 %collective-permute-start.2 = (bf16[128,128]{1,0:T(8,128)(2,1)S(1)}, bf16[128,128]{1,0:T(8,128)(2,1)S(1)}, u32[]{:S(2)}, u32[]{:S(2)}) collective-permute-start(bf16[128,128]{1,0:T(8,128)(2,1)S(1)} %get-tuple-element.112), channel_id=1, source_target_pairs={{0,2},{2,6},{4,0},{6,4},{1,3},{3,7},{5,1},{7,5},{8,10},{10,14},{12... | collective-permute-start | bytes 98312 | tf_op jit(solution)/shard_map/cond/branch_0_fun/ppermute | solution.py:342
  13.0 5.7 %collective-permute-start = (bf16[128,128]{1,0:T(8,128)(2,1)S(1)}, bf16[128,128]{1,0:T(8,128)(2,1)S(1)}, u32[]{:S(2)}, u32[]{:S(2)}) collective-permute-start(bf16[128,128]{1,0:T(8,128)(2,1)S(1)} %get-tuple-element.102), channel_id=1, source_target_pairs={{0,6},{2,4},{4,2},{6,0},{1,7},{3,5},{5,3},{7,1},{8,14},{10,12},{12... | collective-permute-start | bytes 98312 | tf_op jit(solution)/shard_map/cond/branch_0_fun/ppermute | solution.py:342
  15.4 3.9 %collective-permute-start.1 = (bf16[128,128]{1,0:T(8,128)(2,1)S(1)}, bf16[128,128]{1,0:T(8,128)(2,1)S(1)}, u32[]{:S(2)}, u32[]{:S(2)}) collective-permute-start(bf16[128,128]{1,0:T(8,128)(2,1)S(1)} %get-tuple-element.103), channel_id=1, source_target_pairs={{0,4},{2,0},{4,6},{6,2},{1,5},{3,1},{5,7},{7,3},{8,12},{10,8},{12,... | collective-permute-start | bytes 98312 | tf_op jit(solution)/shard_map/cond/branch_0_fun/ppermute | solution.py:342

commit v7 on v4

--- a/solution.py
+++ b/solution.py
@@ -48,8 +48,7 @@
     return 1, 1 + tiles, 1 + 2 * tiles, 1 + 2 * tiles + steps, 1 + 2 * tiles + 2 * steps
 
 
-def pick(shifts, apart, columns, picks, owners, activations, errors, picked, plan, *refs):
-    cuts, (read, seen, copied) = refs[:shifts], refs[shifts:]
+def pick(apart, columns, picks, owners, activations, picked, plan, read, seen, copied):
     replica, group_at = lax.axis_index("dp"), lax.axis_index("tensor")
     groups, slots, replicas = picks.shape[2], picks.shape[3], picks.shape[-1]
     edge = picked.shape[1]
@@ -64,11 +63,6 @@
                 activations.at[0, :, :, column(block, edge)], read.at[at], copied.at[at]
             )
         )
-    for shift, cut in enumerate(cuts):
-        other = lax.rem(group_at + groups - shift - 1, groups)
-        reads.append(
-            pltpu.make_async_copy(errors.at[0, 0, 0, other], cut, copied.at[len(tiles) + shift])
-        )
     for copy in reads:
         copy.start()
 
@@ -132,8 +126,7 @@
 
     for at, copy in enumerate(reads):
         copy.wait()
-        if at < len(tiles):
-            picked[at] = read[at].reshape(-1, edge).T
+        picked[at] = read[at].reshape(-1, edge).T
 
 
 def clear(after, strip, zeros, cleared):
@@ -162,7 +155,7 @@
         for slot in range(slots):
             at = shift * slots + slot
             right = returned[shift][0, :, :, column(columns[at], edge)].reshape(tokens, edge)
-            extra = error[0, 0, 0, mine, slot] if shift == 0 else carried[shift - 1][slot]
+            extra = error[0, 0, 0, mine, slot] if shift == 0 else carried[shift - 1][0, 0, 0, 0, slot]
             tile = jnp.dot(picked[at], right, preferred_element_type=jnp.float32)
             tiles.append(tile + extra.astype(jnp.float32))
     if not apart:
@@ -258,31 +251,33 @@
         ]
         returned.append(lax.ppermute(cotangent, ("pipe", "tensor"), pairs))
     apart = replicas <= MOST_STEPS
-    tiles, shifts = groups * slots, groups - 1
+    tiles = groups * slots
     steps = len(rounds(replicas)) + 1 if apart else replicas
-    picked, plan, *errors = pl.pallas_call(
-        functools.partial(pick, shifts, apart, width // edge),
+    mine = lax.axis_index("tensor")
+    carried = [
+        lax.ppermute(
+            lax.dynamic_index_in_dim(error_tiles, (mine - shift + groups) % groups, axis=3),
+            "tensor",
+            [((group + shift) % groups, group) for group in range(groups)],
+        )
+        for shift in range(1, groups)
+    ]
+    picked, plan = pl.pallas_call(
+        functools.partial(pick, apart, width // edge),
         out_shape=[
             pltpu.VMEM((tiles, edge, micro * tokens), activations.dtype),
             pltpu.VMEM((1, -(-plan_sizes(tiles, steps)[-1] // 128) * 128), jnp.int32),
-        ]
-        + [pltpu.VMEM((slots, edge, edge), error_tiles.dtype)] * shifts,
-        in_specs=[SMEM, SMEM, ANY, ANY],
-        out_specs=[VMEM] * (2 + shifts),
+        ],
+        in_specs=[SMEM, SMEM, ANY],
+        out_specs=[VMEM] * 2,
         scratch_shapes=[
             pltpu.VMEM((tiles, micro, tokens, edge), activations.dtype),
             pltpu.SMEM((row_owners.shape[-1] * (width // edge),), jnp.int32),
-            pltpu.SemaphoreType.DMA((tiles + shifts,)),
+            pltpu.SemaphoreType.DMA((tiles,)),
         ],
         compiler_params=SMALL,
         name="pick",
-    )(in_hbm(picks), in_hbm(row_owners), in_hbm(activations), in_hbm(error_tiles))
-    carried = [
-        lax.ppermute(
-            error, "tensor", [((group + shift + 1) % groups, group) for group in range(groups)]
-        )
-        for shift, error in enumerate(errors)
-    ]
+    )(in_hbm(picks), in_hbm(row_owners), in_hbm(activations))
 
     zero_rows = min(strip_rows, 256)
     strip_shape = (1, 1, strip_rows, width)

time: 20.1 us -> 20.2 us (level)
  waiting for transfers between devices: 5.45 us -> 4.14 us
  local copies, waits for them, and re-layouts: 0.01 us -> 0.76 us
  Pallas kernels: 5.16 us -> 5.77 us
    dynamic_slice x0 -> x1, local copies, waits for them, and re-layouts: none -> 0.76 us  [body(): lax.dynamic_index_in_dim(error_tiles, (mine - shift + groups) % groups, a...]
    ppermute x1, waiting for transfers between devices: 1.36 us -> 0.72 us  [body(): lax.ppermute(lax.dynamic_index_in_dim(error_tiles, (mine - shift + groups...]
    ppermute x3, waiting for transfers between devices: 3.45 us -> 2.83 us  [exchanged(): lax.ppermute(block, 'dp', list(enumerate(targets)))]
    pallas_call x2, Pallas kernels: 0.88 us -> 1.5 us  [placed(): pl.pallas_call(functools.partial(place, len(incoming), alone, to_row + fi...]
  transfers between devices with their start and end apart: 6 -> 6, of which waited for: 5 -> 5; matrix products, arithmetic and copies ran while one was open for 0% -> 4% of each run, Pallas kernels for 21% -> 24%
where the time goes in v7:
time: 20.2 us; the launch traced here: 19.9 us
  starting transfers between devices  9.12 us (45%)
  Pallas kernels  5.77 us (29%)
  waiting for transfers between devices  4.14 us (20%)
  local copies, waits for them, and re-layouts  0.76 us (4%)
    ppermute x3, starting transfers between devices, exchanged(): lax.ppermute(block, 'dp', list(enumerate(targets)))  4.41 us
    ppermute x2, starting transfers between devices, body(): returned.append(lax.ppermute(cotangent, ('pipe', 'tensor'), pairs))  4.18 us
    ppermute x3, waiting for transfers between devices, exchanged(): lax.ppermute(block, 'dp', list(enumerate(targets)))  2.83 us
    pallas_call x1, Pallas kernels, body(): pl.pallas_call(clear, out_shape=pltpu.HBM(strip_shape, jnp.bfloat16), in_...  2.1 us
    pallas_call x1, Pallas kernels, body(): pl.pallas_call(functools.partial(pick, apart, width // edge), out_shape=[...  1.84 us
    pallas_call x2, Pallas kernels, placed(): pl.pallas_call(functools.partial(place, len(incoming), alone, to_row + fi...  1.5 us
    dynamic_slice x1, local copies, waits for them, and re-layouts, body(): lax.dynamic_index_in_dim(error_tiles, (mine - shift + groups) % groups, a...  0.76 us
    ppermute x1, waiting for transfers between devices, body(): lax.ppermute(lax.dynamic_index_in_dim(error_tiles, (mine - shift + groups...  0.72 us
  transfers between devices with their start and end apart: 6, of which 5 were waited for; matrix products, arithmetic and copies ran while one was open for 4% of the time, Pallas kernels for 24%

profile of v7, /device:TPU:0, one launch (start us, length us, event | category | flops | bytes accessed | tf_op | source)
XLA Modules:
  0.0 19.9 jit_solution(12874107265233947386)
XLA Ops:
  0.0 3.3 %collective-permute-start.25 = (bf16[1,2,128,512]{3,2,1,0:T(8,128)(2,1)}, bf16[1,2,128,512]{3,2,1,0:T(8,128)(2,1)S(1)}, u32[]{:S(2)}, u32[]{:S(2)}) collective-permute-start(bf16[1,2,128,512]{3,2,1,0:T(8,128)(2,1)} %param.14), channel_id=1, source_target_pairs={{9,0},{8,1},{17,8},{16,9},{25,16},{24,17},{1,24},{0,25},{11,2},{10... | collective-permute-start | bytes 786440 | tf_op jit(solution)/shard_map/ppermute | solution.py:252
  3.3 0.8 %collective-permute-start.24 = (bf16[1,2,128,512]{3,2,1,0:T(8,128)(2,1)}, bf16[1,2,128,512]{3,2,1,0:T(8,128)(2,1)S(1)}, u32[]{:S(2)}, u32[]{:S(2)}) collective-permute-start(bf16[1,2,128,512]{3,2,1,0:T(8,128)(2,1)} %param.14), channel_id=1, source_target_pairs={{8,0},{9,1},{16,8},{17,9},{24,16},{25,17},{0,24},{1,25},{10,2},{11... | collective-permute-start | bytes 786440 | tf_op jit(solution)/shard_map/ppermute | solution.py:252
  4.2 0.8 %constant_dynamic-slice_fusion = bf16[1,1,1,1,1,128,128]{6,5,4,3,2,1,0:T(8,128)(2,1)S(1)} fusion(bf16[1,1,1,2,1,128,128]{6,5,4,3,2,1,0:T(8,128)(2,1)} %error.1, s32[]{:T(128)S(6)} %select_n.12), kind=kLoop, calls=%fused_computation | loop fusion | bytes 65540 | tf_op jit(solution)/shard_map/jit(dynamic_index_in_dim)/dynamic_slice | solution.py:259
  4.9 0.5 %collective-permute-start.26 = (bf16[1,1,1,1,1,128,128]{6,5,4,3,2,1,0:T(8,128)(2,1)S(1)}, bf16[1,1,1,1,1,128,128]{6,5,4,3,2,1,0:T(8,128)(2,1)S(1)}, u32[]{:S(2)}, u32[]{:S(2)}) collective-permute-start(bf16[1,1,1,1,1,128,128]{6,5,4,3,2,1,0:T(8,128)(2,1)S(1)} %constant_dynamic-slice_fusion), channel_id=1, source_target_pairs={{1,0},{0,1},{3,2},{2,3},{5,4},{4,5},{7,6},{6,7},{9,8},{8,9},{11,10... | collective-permute-start | bytes 98312 | tf_op jit(solution)/shard_map/ppermute | solution.py:258
  5.5 0.0 copy-start
  5.5 1.8 %pick.1 = (bf16[2,128,256]{2,1,0:T(8,128)(2,1)S(1)}, s32[1,128]{1,0:T(1,128)S(1)}) custom-call(s32[1,1,2,1,2,4]{5,4,3,2,1,0:T(2,128)} %bitcast.4, s32[1,1,64]{2,1,0:T(1,128)} %owners.1, bf16[1,2,128,8192]{3,2,1,0:T(8,128)(2,1)} %activations.1), custom_call_target="tpu_custom_call" | custom-call | tf_op jit(solution)/shard_map/pick/pallas_call | solution.py:265
  7.3 2.1 %clear.1 = bf16[1,1,2048,1024]{3,2,1,0:T(8,128)(2,1)} custom-call(bf16[2,128,256]{2,1,0:T(8,128)(2,1)S(1)} %get-tuple-element.169.picked.after), custom_call_target="tpu_custom_call" | custom-call | bytes 4194304 | tf_op jit(solution)/shard_map/clear/pallas_call | solution.py:284
  9.5 0.7 %collective-permute-done.26.refs_2_ = bf16[1,1,1,1,1,128,128]{6,5,4,3,2,1,0:T(8,128)(2,1)S(1)} collective-permute-done((bf16[1,1,1,1,1,128,128]{6,5,4,3,2,1,0:T(8,128)(2,1)S(1)}, bf16[1,1,1,1,1,128,128]{6,5,4,3,2,1,0:T(8,128)(2,1)S(1)}, u32[]{:S(2)}, u32[]{:S(2)}) %collective-permute-start.26) | collective-permute-done | bytes 32800 | tf_op jit(solution)/shard_map/ppermute | solution.py:258
  10.2 0.0 collective-permute-done.25.refs_1_
  10.2 0.6 %collective-permute-done.24.refs_0_ = bf16[1,2,128,512]{3,2,1,0:T(8,128)(2,1)S(1)} collective-permute-done((bf16[1,2,128,512]{3,2,1,0:T(8,128)(2,1)}, bf16[1,2,128,512]{3,2,1,0:T(8,128)(2,1)S(1)}, u32[]{:S(2)}, u32[]{:S(2)}) %collective-permute-start.24) | collective-permute-done | bytes 262176 | tf_op jit(solution)/shard_map/ppermute | solution.py:252
  10.8 0.0 copy-done
  10.8 0.3 %multiply.1 = (f32[128,128]{1,0:T(8,128)S(1)}, f32[128,128]{1,0:T(8,128)S(1)}, f32[128,128]{1,0:T(8,128)S(1)}, f32[128,128]{1,0:T(8,128)S(1)}, bf16[128,128]{1,0...) custom-call(s32[1,128]{1,0:T(1,128)S(1)} %get-tuple-element.168.plan, ...), custom_call_target="tpu_custom_call" | custom-call | tf_op jit(solution)/shard_map/multiply/pallas_call | solution.py:310
  11.1 8.8 %conditional.1 = (bf16[1,1,2048,1024]{3,2,1,0:T(8,128)(2,1)}) conditional(s32[]{:T(128)} %bitcast.1, (bf16[128,128]{1,0:T(8,128)(2,1)S(1)}, bf16[128,128]{1,0:T(8,128)(2,1)S(1)}, bf16[128,128]{1,0:T(8,128)(2,1)S(1)}, s32[1,128]{1,0:T(1,128)S(1)}, bf16[128,128]{1,0:T(8,128)(2,1)S(1)}, ...), branch_computations={%region_0.1_spmd, %region_1.2_spmd, %region_2.3_spmd, %region_3.4_... | conditional | bytes 786560 | solution.py:359
  11.2 2.8 %collective-permute-start.2 = (bf16[128,128]{1,0:T(8,128)(2,1)S(1)}, bf16[128,128]{1,0:T(8,128)(2,1)S(1)}, u32[]{:S(2)}, u32[]{:S(2)}) collective-permute-start(bf16[128,128]{1,0:T(8,128)(2,1)S(1)} %get-tuple-element.112), channel_id=1, source_target_pairs={{0,4},{2,6},{4,2},{6,0},{1,5},{3,7},{5,3},{7,1},{8,12},{10,14},{12... | collective-permute-start | bytes 98312 | tf_op jit(solution)/shard_map/cond/branch_0_fun/ppermute | solution.py:337
  14.0 1.1 %collective-permute-start = (bf16[128,128]{1,0:T(8,128)(2,1)S(1)}, bf16[128,128]{1,0:T(8,128)(2,1)S(1)}, u32[]{:S(2)}, u32[]{:S(2)}) collective-permute-start(bf16[128,128]{1,0:T(8,128)(2,1)S(1)} %get-tuple-element.102), channel_id=1, source_target_pairs={{0,6},{2,4},{4,0},{6,2},{1,7},{3,5},{5,1},{7,3},{8,14},{10,12},{12... | collective-permute-start | bytes 98312 | tf_op jit(solution)/shard_map/cond/branch_0_fun/ppermute | solution.py:337
  15.1 0.5 %collective-permute-start.1 = (bf16[128,128]{1,0:T(8,128)(2,1)S(1)}, bf16[128,128]{1,0:T(8,128)(2,1)S(1)}, u32[]{:S(2)}, u32[]{:S(2)}) collective-permute-start(bf16[128,128]{1,0:T(8,128)(2,1)S(1)} %get-tuple-element.103), channel_id=1, source_target_pairs={{0,2},{2,0},{4,6},{6,4},{1,3},{3,1},{5,7},{7,5},{8,10},{10,8},{12,... | collective-permute-start | bytes 98312 | tf_op jit(solution)/shard_map/cond/branch_0_fun/ppermute | solution.py:337
  15.6 1.5 %collective-permute-done.2.refs_1_ = bf16[128,128]{1,0:T(8,128)(2,1)S(1)} collective-permute-done((bf16[128,128]{1,0:T(8,128)(2,1)S(1)}, bf16[128,128]{1,0:T(8,128)(2,1)S(1)}, u32[]{:S(2)}, u32[]{:S(2)}) %collective-permute-start.2) | collective-permute-done | bytes 32800 | tf_op jit(solution)/shard_map/cond/branch_0_fun/ppermute | solution.py:337
  17.0 0.7 %place.9.refs_2_ = bf16[1,1,2048,1024]{3,2,1,0:T(8,128)(2,1)} custom-call(s32[1,128]{1,0:T(1,128)S(1)} %get-tuple-element.101.plan, bf16[128,128]{1,0:T(8,128)(2,1)S(1)} %get-tuple-element.104.refs_0_, bf16[128,128]{1,0:T(8,128)(2,1)S(1)} %collective-permute-done.2.refs_1_, ...), custom_call_target="tpu_custom_call", output_to_operand_aliasing={{}: (3, {})} | custom-call | tf_op jit(solution)/shard_map/cond/branch_0_fun/place/pallas_call | solution.py:321
  17.8 1.0 %collective-permute-done.refs_0_ = bf16[128,128]{1,0:T(8,128)(2,1)S(1)} collective-permute-done((bf16[128,128]{1,0:T(8,128)(2,1)S(1)}, bf16[128,128]{1,0:T(8,128)(2,1)S(1)}, u32[]{:S(2)}, u32[]{:S(2)}) %collective-permute-start) | collective-permute-done | bytes 32800 | tf_op jit(solution)/shard_map/cond/branch_0_fun/ppermute | solution.py:337
  18.8 0.3 %collective-permute-done.1.refs_1_ = bf16[128,128]{1,0:T(8,128)(2,1)S(1)} collective-permute-done((bf16[128,128]{1,0:T(8,128)(2,1)S(1)}, bf16[128,128]{1,0:T(8,128)(2,1)S(1)}, u32[]{:S(2)}, u32[]{:S(2)}) %collective-permute-start.1) | collective-permute-done | bytes 32800 | tf_op jit(solution)/shard_map/cond/branch_0_fun/ppermute | solution.py:337
  19.1 0.7 %place.10 = bf16[1,1,2048,1024]{3,2,1,0:T(8,128)(2,1)} custom-call(s32[1,128]{1,0:T(1,128)S(1)} %get-tuple-element.101.plan, bf16[128,128]{1,0:T(8,128)(2,1)S(1)} %collective-permute-done.refs_0_, bf16[128,128]{1,0:T(8,128)(2,1)S(1)} %collective-permute-done.1.refs_1_, bf16[1,1,2048,1024]{3,2,1,0:T(8,128)(2,1)} %place.9.refs_2_), custom_call_target="tpu_custom_call", output_to_operand_aliasing={{}: (3, {})} | custom-call | tf_op jit(solution)/shard_map/cond/branch_0_fun/place/pallas_call | solution.py:321
Async XLA Ops:
  0.0 10.2 %collective-permute-start.25 = (bf16[1,2,128,512]{3,2,1,0:T(8,128)(2,1)}, bf16[1,2,128,512]{3,2,1,0:T(8,128)(2,1)S(1)}, u32[]{:S(2)}, u32[]{:S(2)}) collective-permute-start(bf16[1,2,128,512]{3,2,1,0:T(8,128)(2,1)} %param.14), channel_id=1, source_target_pairs={{9,0},{8,1},{17,8},{16,9},{25,16},{24,17},{1,24},{0,25},{11,2},{10... | collective-permute-start | bytes 786440 | tf_op jit(solution)/shard_map/ppermute | solution.py:252
  3.3 7.5 %collective-permute-start.24 = (bf16[1,2,128,512]{3,2,1,0:T(8,128)(2,1)}, bf16[1,2,128,512]{3,2,1,0:T(8,128)(2,1)S(1)}, u32[]{:S(2)}, u32[]{:S(2)}) collective-permute-start(bf16[1,2,128,512]{3,2,1,0:T(8,128)(2,1)} %param.14), channel_id=1, source_target_pairs={{8,0},{9,1},{16,8},{17,9},{24,16},{25,17},{0,24},{1,25},{10,2},{11... | collective-permute-start | bytes 786440 | tf_op jit(solution)/shard_map/ppermute | solution.py:252
  4.9 5.3 %collective-permute-start.26 = (bf16[1,1,1,1,1,128,128]{6,5,4,3,2,1,0:T(8,128)(2,1)S(1)}, bf16[1,1,1,1,1,128,128]{6,5,4,3,2,1,0:T(8,128)(2,1)S(1)}, u32[]{:S(2)}, u32[]{:S(2)}) collective-permute-start(bf16[1,1,1,1,1,128,128]{6,5,4,3,2,1,0:T(8,128)(2,1)S(1)} %constant_dynamic-slice_fusion), channel_id=1, source_target_pairs={{1,0},{0,1},{3,2},{2,3},{5,4},{4,5},{7,6},{6,7},{9,8},{8,9},{11,10... | collective-permute-start | bytes 98312 | tf_op jit(solution)/shard_map/ppermute | solution.py:258
  5.5 5.3 %copy-start = (bf16[1,1,1,2,1,128,128]{6,5,4,3,2,1,0:T(8,128)(2,1)S(1)}, bf16[1,1,1,2,1,128,128]{6,5,4,3,2,1,0:T(8,128)(2,1)}, u32[]{:S(2)}) copy-start(bf16[1,1,1,2,1,128,128]{6,5,4,3,2,1,0:T(8,128)(2,1)} %error.1) | copy-start | bytes 196612
  11.2 5.9 %collective-permute-start.2 = (bf16[128,128]{1,0:T(8,128)(2,1)S(1)}, bf16[128,128]{1,0:T(8,128)(2,1)S(1)}, u32[]{:S(2)}, u32[]{:S(2)}) collective-permute-start(bf16[128,128]{1,0:T(8,128)(2,1)S(1)} %get-tuple-element.112), channel_id=1, source_target_pairs={{0,4},{2,6},{4,2},{6,0},{1,5},{3,7},{5,3},{7,1},{8,12},{10,14},{12... | collective-permute-start | bytes 98312 | tf_op jit(solution)/shard_map/cond/branch_0_fun/ppermute | solution.py:337
  14.0 4.8 %collective-permute-start = (bf16[128,128]{1,0:T(8,128)(2,1)S(1)}, bf16[128,128]{1,0:T(8,128)(2,1)S(1)}, u32[]{:S(2)}, u32[]{:S(2)}) collective-permute-start(bf16[128,128]{1,0:T(8,128)(2,1)S(1)} %get-tuple-element.102), channel_id=1, source_target_pairs={{0,6},{2,4},{4,0},{6,2},{1,7},{3,5},{5,1},{7,3},{8,14},{10,12},{12... | collective-permute-start | bytes 98312 | tf_op jit(solution)/shard_map/cond/branch_0_fun/ppermute | solution.py:337
  15.1 4.1 %collective-permute-start.1 = (bf16[128,128]{1,0:T(8,128)(2,1)S(1)}, bf16[128,128]{1,0:T(8,128)(2,1)S(1)}, u32[]{:S(2)}, u32[]{:S(2)}) collective-permute-start(bf16[128,128]{1,0:T(8,128)(2,1)S(1)} %get-tuple-element.103), channel_id=1, source_target_pairs={{0,2},{2,0},{4,6},{6,4},{1,3},{3,1},{5,7},{7,5},{8,10},{10,8},{12,... | collective-permute-start | bytes 98312 | tf_op jit(solution)/shard_map/cond/branch_0_fun/ppermute | solution.py:337

commit v8 on v7

--- a/solution.py
+++ b/solution.py
@@ -221,7 +221,7 @@
                     block = block_of(later).astype(jnp.float32)
                     total = total + jnp.where(meets(step, later), block, 0.0)
                 staged[step] = total.astype(staged.dtype)
-            write_of(step).start()
+            write_of(step).start(priority=1)
 
     for step in range(steps):
 

time: 20.2 us -> 19.9 us (0.985); the launches traced: 19.9 us -> 19.9 us
  no operation moved by 1% of the time
where the time goes in v8:
time: 19.9 us
  starting transfers between devices  9.12 us (46%)
  Pallas kernels  5.76 us (29%)
  waiting for transfers between devices  4.14 us (21%)
  local copies, waits for them, and re-layouts  0.76 us (4%)
    ppermute x3, starting transfers between devices, exchanged(): lax.ppermute(block, 'dp', list(enumerate(targets)))  4.41 us
    ppermute x2, starting transfers between devices, body(): returned.append(lax.ppermute(cotangent, ('pipe', 'tensor'), pairs))  4.18 us
    ppermute x3, waiting for transfers between devices, exchanged(): lax.ppermute(block, 'dp', list(enumerate(targets)))  2.83 us
    pallas_call x1, Pallas kernels, body(): pl.pallas_call(clear, out_shape=pltpu.HBM(strip_shape, jnp.bfloat16), in_...  2.1 us
    pallas_call x1, Pallas kernels, body(): pl.pallas_call(functools.partial(pick, apart, width // edge), out_shape=[...  1.84 us
    pallas_call x2, Pallas kernels, placed(): pl.pallas_call(functools.partial(place, len(incoming), alone, to_row + fi...  1.49 us
    dynamic_slice x1, local copies, waits for them, and re-layouts, body(): lax.dynamic_index_in_dim(error_tiles, (mine - shift + groups) % groups, a...  0.76 us
    ppermute x1, waiting for transfers between devices, body(): lax.ppermute(lax.dynamic_index_in_dim(error_tiles, (mine - shift + groups...  0.72 us
  transfers between devices with their start and end apart: 6, of which 5 were waited for; matrix products, arithmetic and copies ran while one was open for 4% of the time, Pallas kernels for 24%

profile of v8, /device:TPU:0, one launch (start us, length us, event | category | flops | bytes accessed | tf_op | source)
XLA Modules:
  0.0 19.9 jit_solution(12205682002157920182)
XLA Ops:
  0.0 3.3 %collective-permute-start.25 = (bf16[1,2,128,512]{3,2,1,0:T(8,128)(2,1)}, bf16[1,2,128,512]{3,2,1,0:T(8,128)(2,1)S(1)}, u32[]{:S(2)}, u32[]{:S(2)}) collective-permute-start(bf16[1,2,128,512]{3,2,1,0:T(8,128)(2,1)} %param.14), channel_id=1, source_target_pairs={{9,0},{8,1},{17,8},{16,9},{25,16},{24,17},{1,24},{0,25},{11,2},{10... | collective-permute-start | bytes 786440 | tf_op jit(solution)/shard_map/ppermute | solution.py:252
  3.3 0.8 %collective-permute-start.24 = (bf16[1,2,128,512]{3,2,1,0:T(8,128)(2,1)}, bf16[1,2,128,512]{3,2,1,0:T(8,128)(2,1)S(1)}, u32[]{:S(2)}, u32[]{:S(2)}) collective-permute-start(bf16[1,2,128,512]{3,2,1,0:T(8,128)(2,1)} %param.14), channel_id=1, source_target_pairs={{8,0},{9,1},{16,8},{17,9},{24,16},{25,17},{0,24},{1,25},{10,2},{11... | collective-permute-start | bytes 786440 | tf_op jit(solution)/shard_map/ppermute | solution.py:252
  4.2 0.8 %constant_dynamic-slice_fusion = bf16[1,1,1,1,1,128,128]{6,5,4,3,2,1,0:T(8,128)(2,1)S(1)} fusion(bf16[1,1,1,2,1,128,128]{6,5,4,3,2,1,0:T(8,128)(2,1)} %error.1, s32[]{:T(128)S(6)} %select_n.12), kind=kLoop, calls=%fused_computation | loop fusion | bytes 65540 | tf_op jit(solution)/shard_map/jit(dynamic_index_in_dim)/dynamic_slice | solution.py:259
  4.9 0.5 %collective-permute-start.26 = (bf16[1,1,1,1,1,128,128]{6,5,4,3,2,1,0:T(8,128)(2,1)S(1)}, bf16[1,1,1,1,1,128,128]{6,5,4,3,2,1,0:T(8,128)(2,1)S(1)}, u32[]{:S(2)}, u32[]{:S(2)}) collective-permute-start(bf16[1,1,1,1,1,128,128]{6,5,4,3,2,1,0:T(8,128)(2,1)S(1)} %constant_dynamic-slice_fusion), channel_id=1, source_target_pairs={{1,0},{0,1},{3,2},{2,3},{5,4},{4,5},{7,6},{6,7},{9,8},{8,9},{11,10... | collective-permute-start | bytes 98312 | tf_op jit(solution)/shard_map/ppermute | solution.py:258
  5.5 0.0 copy-start
  5.5 1.8 %pick.1 = (bf16[2,128,256]{2,1,0:T(8,128)(2,1)S(1)}, s32[1,128]{1,0:T(1,128)S(1)}) custom-call(s32[1,1,2,1,2,4]{5,4,3,2,1,0:T(2,128)} %bitcast.4, s32[1,1,64]{2,1,0:T(1,128)} %owners.1, bf16[1,2,128,8192]{3,2,1,0:T(8,128)(2,1)} %activations.1), custom_call_target="tpu_custom_call" | custom-call | tf_op jit(solution)/shard_map/pick/pallas_call | solution.py:265
  7.3 2.1 %clear.1 = bf16[1,1,2048,1024]{3,2,1,0:T(8,128)(2,1)} custom-call(bf16[2,128,256]{2,1,0:T(8,128)(2,1)S(1)} %get-tuple-element.169.picked.after), custom_call_target="tpu_custom_call" | custom-call | bytes 4194304 | tf_op jit(solution)/shard_map/clear/pallas_call | solution.py:284
  9.5 0.7 %collective-permute-done.26.refs_2_ = bf16[1,1,1,1,1,128,128]{6,5,4,3,2,1,0:T(8,128)(2,1)S(1)} collective-permute-done((bf16[1,1,1,1,1,128,128]{6,5,4,3,2,1,0:T(8,128)(2,1)S(1)}, bf16[1,1,1,1,1,128,128]{6,5,4,3,2,1,0:T(8,128)(2,1)S(1)}, u32[]{:S(2)}, u32[]{:S(2)}) %collective-permute-start.26) | collective-permute-done | bytes 32800 | tf_op jit(solution)/shard_map/ppermute | solution.py:258
  10.2 0.0 collective-permute-done.25.refs_1_
  10.2 0.6 %collective-permute-done.24.refs_0_ = bf16[1,2,128,512]{3,2,1,0:T(8,128)(2,1)S(1)} collective-permute-done((bf16[1,2,128,512]{3,2,1,0:T(8,128)(2,1)}, bf16[1,2,128,512]{3,2,1,0:T(8,128)(2,1)S(1)}, u32[]{:S(2)}, u32[]{:S(2)}) %collective-permute-start.24) | collective-permute-done | bytes 262176 | tf_op jit(solution)/shard_map/ppermute | solution.py:252
  10.8 0.0 copy-done
  10.8 0.3 %multiply.1 = (f32[128,128]{1,0:T(8,128)S(1)}, f32[128,128]{1,0:T(8,128)S(1)}, f32[128,128]{1,0:T(8,128)S(1)}, f32[128,128]{1,0:T(8,128)S(1)}, bf16[128,128]{1,0...) custom-call(s32[1,128]{1,0:T(1,128)S(1)} %get-tuple-element.168.plan, ...), custom_call_target="tpu_custom_call" | custom-call | tf_op jit(solution)/shard_map/multiply/pallas_call | solution.py:310
  11.1 8.8 %conditional.1 = (bf16[1,1,2048,1024]{3,2,1,0:T(8,128)(2,1)}) conditional(s32[]{:T(128)} %bitcast.1, (bf16[128,128]{1,0:T(8,128)(2,1)S(1)}, bf16[128,128]{1,0:T(8,128)(2,1)S(1)}, bf16[128,128]{1,0:T(8,128)(2,1)S(1)}, s32[1,128]{1,0:T(1,128)S(1)}, bf16[128,128]{1,0:T(8,128)(2,1)S(1)}, ...), branch_computations={%region_0.1_spmd, %region_1.2_spmd, %region_2.3_spmd, %region_3.4_... | conditional | bytes 786560 | solution.py:359
  11.2 2.8 %collective-permute-start.2 = (bf16[128,128]{1,0:T(8,128)(2,1)S(1)}, bf16[128,128]{1,0:T(8,128)(2,1)S(1)}, u32[]{:S(2)}, u32[]{:S(2)}) collective-permute-start(bf16[128,128]{1,0:T(8,128)(2,1)S(1)} %get-tuple-element.112), channel_id=1, source_target_pairs={{0,4},{2,6},{4,2},{6,0},{1,5},{3,7},{5,3},{7,1},{8,12},{10,14},{12... | collective-permute-start | bytes 98312 | tf_op jit(solution)/shard_map/cond/branch_0_fun/ppermute | solution.py:337
  14.0 1.1 %collective-permute-start = (bf16[128,128]{1,0:T(8,128)(2,1)S(1)}, bf16[128,128]{1,0:T(8,128)(2,1)S(1)}, u32[]{:S(2)}, u32[]{:S(2)}) collective-permute-start(bf16[128,128]{1,0:T(8,128)(2,1)S(1)} %get-tuple-element.102), channel_id=1, source_target_pairs={{0,6},{2,4},{4,0},{6,2},{1,7},{3,5},{5,1},{7,3},{8,14},{10,12},{12... | collective-permute-start | bytes 98312 | tf_op jit(solution)/shard_map/cond/branch_0_fun/ppermute | solution.py:337
  15.1 0.5 %collective-permute-start.1 = (bf16[128,128]{1,0:T(8,128)(2,1)S(1)}, bf16[128,128]{1,0:T(8,128)(2,1)S(1)}, u32[]{:S(2)}, u32[]{:S(2)}) collective-permute-start(bf16[128,128]{1,0:T(8,128)(2,1)S(1)} %get-tuple-element.103), channel_id=1, source_target_pairs={{0,2},{2,0},{4,6},{6,4},{1,3},{3,1},{5,7},{7,5},{8,10},{10,8},{12,... | collective-permute-start | bytes 98312 | tf_op jit(solution)/shard_map/cond/branch_0_fun/ppermute | solution.py:337
  15.6 1.5 %collective-permute-done.2.refs_1_ = bf16[128,128]{1,0:T(8,128)(2,1)S(1)} collective-permute-done((bf16[128,128]{1,0:T(8,128)(2,1)S(1)}, bf16[128,128]{1,0:T(8,128)(2,1)S(1)}, u32[]{:S(2)}, u32[]{:S(2)}) %collective-permute-start.2) | collective-permute-done | bytes 32800 | tf_op jit(solution)/shard_map/cond/branch_0_fun/ppermute | solution.py:337
  17.0 0.7 %place.9.refs_2_ = bf16[1,1,2048,1024]{3,2,1,0:T(8,128)(2,1)} custom-call(s32[1,128]{1,0:T(1,128)S(1)} %get-tuple-element.101.plan, bf16[128,128]{1,0:T(8,128)(2,1)S(1)} %get-tuple-element.104.refs_0_, bf16[128,128]{1,0:T(8,128)(2,1)S(1)} %collective-permute-done.2.refs_1_, ...), custom_call_target="tpu_custom_call", output_to_operand_aliasing={{}: (3, {})} | custom-call | tf_op jit(solution)/shard_map/cond/branch_0_fun/place/pallas_call | solution.py:321
  17.8 1.0 %collective-permute-done.refs_0_ = bf16[128,128]{1,0:T(8,128)(2,1)S(1)} collective-permute-done((bf16[128,128]{1,0:T(8,128)(2,1)S(1)}, bf16[128,128]{1,0:T(8,128)(2,1)S(1)}, u32[]{:S(2)}, u32[]{:S(2)}) %collective-permute-start) | collective-permute-done | bytes 32800 | tf_op jit(solution)/shard_map/cond/branch_0_fun/ppermute | solution.py:337
  18.8 0.3 %collective-permute-done.1.refs_1_ = bf16[128,128]{1,0:T(8,128)(2,1)S(1)} collective-permute-done((bf16[128,128]{1,0:T(8,128)(2,1)S(1)}, bf16[128,128]{1,0:T(8,128)(2,1)S(1)}, u32[]{:S(2)}, u32[]{:S(2)}) %collective-permute-start.1) | collective-permute-done | bytes 32800 | tf_op jit(solution)/shard_map/cond/branch_0_fun/ppermute | solution.py:337
  19.1 0.7 %place.10 = bf16[1,1,2048,1024]{3,2,1,0:T(8,128)(2,1)} custom-call(s32[1,128]{1,0:T(1,128)S(1)} %get-tuple-element.101.plan, bf16[128,128]{1,0:T(8,128)(2,1)S(1)} %collective-permute-done.refs_0_, bf16[128,128]{1,0:T(8,128)(2,1)S(1)} %collective-permute-done.1.refs_1_, bf16[1,1,2048,1024]{3,2,1,0:T(8,128)(2,1)} %place.9.refs_2_), custom_call_target="tpu_custom_call", output_to_operand_aliasing={{}: (3, {})} | custom-call | tf_op jit(solution)/shard_map/cond/branch_0_fun/place/pallas_call | solution.py:321
Async XLA Ops:
  0.0 10.2 %collective-permute-start.25 = (bf16[1,2,128,512]{3,2,1,0:T(8,128)(2,1)}, bf16[1,2,128,512]{3,2,1,0:T(8,128)(2,1)S(1)}, u32[]{:S(2)}, u32[]{:S(2)}) collective-permute-start(bf16[1,2,128,512]{3,2,1,0:T(8,128)(2,1)} %param.14), channel_id=1, source_target_pairs={{9,0},{8,1},{17,8},{16,9},{25,16},{24,17},{1,24},{0,25},{11,2},{10... | collective-permute-start | bytes 786440 | tf_op jit(solution)/shard_map/ppermute | solution.py:252
  3.3 7.5 %collective-permute-start.24 = (bf16[1,2,128,512]{3,2,1,0:T(8,128)(2,1)}, bf16[1,2,128,512]{3,2,1,0:T(8,128)(2,1)S(1)}, u32[]{:S(2)}, u32[]{:S(2)}) collective-permute-start(bf16[1,2,128,512]{3,2,1,0:T(8,128)(2,1)} %param.14), channel_id=1, source_target_pairs={{8,0},{9,1},{16,8},{17,9},{24,16},{25,17},{0,24},{1,25},{10,2},{11... | collective-permute-start | bytes 786440 | tf_op jit(solution)/shard_map/ppermute | solution.py:252
  4.9 5.3 %collective-permute-start.26 = (bf16[1,1,1,1,1,128,128]{6,5,4,3,2,1,0:T(8,128)(2,1)S(1)}, bf16[1,1,1,1,1,128,128]{6,5,4,3,2,1,0:T(8,128)(2,1)S(1)}, u32[]{:S(2)}, u32[]{:S(2)}) collective-permute-start(bf16[1,1,1,1,1,128,128]{6,5,4,3,2,1,0:T(8,128)(2,1)S(1)} %constant_dynamic-slice_fusion), channel_id=1, source_target_pairs={{1,0},{0,1},{3,2},{2,3},{5,4},{4,5},{7,6},{6,7},{9,8},{8,9},{11,10... | collective-permute-start | bytes 98312 | tf_op jit(solution)/shard_map/ppermute | solution.py:258
  5.5 5.3 %copy-start = (bf16[1,1,1,2,1,128,128]{6,5,4,3,2,1,0:T(8,128)(2,1)S(1)}, bf16[1,1,1,2,1,128,128]{6,5,4,3,2,1,0:T(8,128)(2,1)}, u32[]{:S(2)}) copy-start(bf16[1,1,1,2,1,128,128]{6,5,4,3,2,1,0:T(8,128)(2,1)} %error.1) | copy-start | bytes 196612
  11.2 5.9 %collective-permute-start.2 = (bf16[128,128]{1,0:T(8,128)(2,1)S(1)}, bf16[128,128]{1,0:T(8,128)(2,1)S(1)}, u32[]{:S(2)}, u32[]{:S(2)}) collective-permute-start(bf16[128,128]{1,0:T(8,128)(2,1)S(1)} %get-tuple-element.112), channel_id=1, source_target_pairs={{0,4},{2,6},{4,2},{6,0},{1,5},{3,7},{5,3},{7,1},{8,12},{10,14},{12... | collective-permute-start | bytes 98312 | tf_op jit(solution)/shard_map/cond/branch_0_fun/ppermute | solution.py:337
  14.0 4.8 %collective-permute-start = (bf16[128,128]{1,0:T(8,128)(2,1)S(1)}, bf16[128,128]{1,0:T(8,128)(2,1)S(1)}, u32[]{:S(2)}, u32[]{:S(2)}) collective-permute-start(bf16[128,128]{1,0:T(8,128)(2,1)S(1)} %get-tuple-element.102), channel_id=1, source_target_pairs={{0,6},{2,4},{4,0},{6,2},{1,7},{3,5},{5,1},{7,3},{8,14},{10,12},{12... | collective-permute-start | bytes 98312 | tf_op jit(solution)/shard_map/cond/branch_0_fun/ppermute | solution.py:337
  15.1 4.1 %collective-permute-start.1 = (bf16[128,128]{1,0:T(8,128)(2,1)S(1)}, bf16[128,128]{1,0:T(8,128)(2,1)S(1)}, u32[]{:S(2)}, u32[]{:S(2)}) collective-permute-start(bf16[128,128]{1,0:T(8,128)(2,1)S(1)} %get-tuple-element.103), channel_id=1, source_target_pairs={{0,2},{2,0},{4,6},{6,4},{1,3},{3,1},{5,7},{7,5},{8,10},{10,8},{12,... | collective-permute-start | bytes 98312 | tf_op jit(solution)/shard_map/cond/branch_0_fun/ppermute | solution.py:337

commit v9 on v7

--- a/solution.py
+++ b/solution.py
@@ -23,18 +23,18 @@
     return pl.ds(pl.multiple_of(index * edge, edge), edge)
 
 
-def rounds(replicas):
+def rounds(replicas, odd=0):
     shifts = [
         tuple((one + step) % replicas for one in range(replicas)) for step in range(1, replicas)
     ]
-    return ROUNDS.get(replicas, shifts)
-
-
-def step_table(replicas):
+    return shifts if odd else ROUNDS.get(replicas, shifts)
+
+
+def step_table(replicas, odd):
     table = []
     for source in range(replicas):
         steps = [0] * replicas
-        for step, targets in reversed(list(enumerate(rounds(replicas), 1))):
+        for step, targets in reversed(list(enumerate(rounds(replicas, odd), 1))):
             steps[targets[source]] = step
         table.append(sum(step << 4 * target for target, step in enumerate(steps)))
     return table
@@ -77,7 +77,11 @@
             owner += (row >= one * owned).astype(jnp.int32)
         return owner
 
-    table = step_table(replicas) if apart else []
+    odd = lax.rem(lax.axis_index("pipe"), 2) > 0
+    table = [
+        jnp.where(odd, other, packed)
+        for packed, other in zip(step_table(replicas, 0), step_table(replicas, 1))
+    ] if apart else []
     mine = jnp.int32(0)
     for source, packed in enumerate(table):
         mine = jnp.where(replica == source, packed, mine)
@@ -99,7 +103,7 @@
             place_col = jnp.where(
                 here, picks[0, 0, group, slot, 1, origin] + group * per_group, place_col
             )
-        step = (jnp.int32(table[origin]) >> 4 * replica) & 15 if apart else origin
+        step = (table[origin] >> 4 * replica) & 15 if apart else origin
         planned = jnp.where(lane == to_row + step, place_row, planned)
         planned = jnp.where(lane == to_col + step, place_col, planned)
 
@@ -119,7 +123,7 @@
         for at, spot in enumerate(spots):
             origin, (group, slot) = at // len(tiles), tiles[at % len(tiles)]
             owner = owner_of(owners[0, 0, picks[0, 0, group, slot, 0, origin]])
-            step = (jnp.int32(table[origin]) >> 4 * owner) & 15
+            step = (table[origin] >> 4 * owner) & 15
             bit = jnp.int32(1) << wide_bit(jnp.maximum(step, 1), steps)
             wide = jnp.where((seen[spot] > 1) & (step > 0), wide | bit, wide)
     plan[...] = jnp.where(lane == 0, wide, planned)
@@ -333,10 +337,14 @@
         )(plan, *incoming, strip)
 
     def exchanged(blocks):
-        moved = [
-            lax.ppermute(block, "dp", list(enumerate(targets)))
-            for block, targets in zip(blocks[1:], rounds(replicas))
-        ]
+        moved = []
+        for at, block in enumerate(blocks[1:]):
+            pairs = [
+                (section * replicas + source, section * replicas + target)
+                for section in range(sections)
+                for source, target in enumerate(rounds(replicas, section % 2)[at])
+            ]
+            moved.append(lax.ppermute(block, ("pipe", "dp"), pairs))
         return [blocks[0], *moved]
 
     if not apart:

time: 20.2 us -> 19.9 us (0.985); the launches traced: 19.9 us -> 19.9 us
  no operation moved by 1% of the time
where the time goes in v9:
time: 19.9 us
  starting transfers between devices  9.12 us (46%)
  Pallas kernels  5.77 us (29%)
  waiting for transfers between devices  4.14 us (21%)
  local copies, waits for them, and re-layouts  0.76 us (4%)
    ppermute x3, starting transfers between devices, exchanged(): moved.append(lax.ppermute(block, ('pipe', 'dp'), pairs))  4.41 us
    ppermute x2, starting transfers between devices, body(): returned.append(lax.ppermute(cotangent, ('pipe', 'tensor'), pairs))  4.18 us
    ppermute x3, waiting for transfers between devices, exchanged(): moved.append(lax.ppermute(block, ('pipe', 'dp'), pairs))  2.83 us
    pallas_call x1, Pallas kernels, body(): pl.pallas_call(clear, out_shape=pltpu.HBM(strip_shape, jnp.bfloat16), in_...  2.1 us
    pallas_call x1, Pallas kernels, body(): pl.pallas_call(functools.partial(pick, apart, width // edge), out_shape=[...  1.84 us
    pallas_call x2, Pallas kernels, placed(): pl.pallas_call(functools.partial(place, len(incoming), alone, to_row + fi...  1.5 us
    dynamic_slice x1, local copies, waits for them, and re-layouts, body(): lax.dynamic_index_in_dim(error_tiles, (mine - shift + groups) % groups, a...  0.76 us
    ppermute x1, waiting for transfers between devices, body(): lax.ppermute(lax.dynamic_index_in_dim(error_tiles, (mine - shift + groups...  0.72 us
  transfers between devices with their start and end apart: 6, of which 5 were waited for; matrix products, arithmetic and copies ran while one was open for 4% of the time, Pallas kernels for 24%

profile of v9, /device:TPU:0, one launch (start us, length us, event | category | flops | bytes accessed | tf_op | source)
XLA Modules:
  0.0 19.9 jit_solution(7231596743154079882)
XLA Ops:
  0.0 3.3 %collective-permute-start.25 = (bf16[1,2,128,512]{3,2,1,0:T(8,128)(2,1)}, bf16[1,2,128,512]{3,2,1,0:T(8,128)(2,1)S(1)}, u32[]{:S(2)}, u32[]{:S(2)}) collective-permute-start(bf16[1,2,128,512]{3,2,1,0:T(8,128)(2,1)} %param.14), channel_id=1, source_target_pairs={{9,0},{8,1},{17,8},{16,9},{25,16},{24,17},{1,24},{0,25},{11,2},{10... | collective-permute-start | bytes 786440 | tf_op jit(solution)/shard_map/ppermute | solution.py:256
  3.3 0.8 %collective-permute-start.24 = (bf16[1,2,128,512]{3,2,1,0:T(8,128)(2,1)}, bf16[1,2,128,512]{3,2,1,0:T(8,128)(2,1)S(1)}, u32[]{:S(2)}, u32[]{:S(2)}) collective-permute-start(bf16[1,2,128,512]{3,2,1,0:T(8,128)(2,1)} %param.14), channel_id=1, source_target_pairs={{8,0},{9,1},{16,8},{17,9},{24,16},{25,17},{0,24},{1,25},{10,2},{11... | collective-permute-start | bytes 786440 | tf_op jit(solution)/shard_map/ppermute | solution.py:256
  4.2 0.8 %constant_dynamic-slice_fusion = bf16[1,1,1,1,1,128,128]{6,5,4,3,2,1,0:T(8,128)(2,1)S(1)} fusion(bf16[1,1,1,2,1,128,128]{6,5,4,3,2,1,0:T(8,128)(2,1)} %error.1, s32[]{:T(128)S(6)} %select_n.12), kind=kLoop, calls=%fused_computation | loop fusion | bytes 65540 | tf_op jit(solution)/shard_map/jit(dynamic_index_in_dim)/dynamic_slice | solution.py:263
  4.9 0.5 %collective-permute-start.26 = (bf16[1,1,1,1,1,128,128]{6,5,4,3,2,1,0:T(8,128)(2,1)S(1)}, bf16[1,1,1,1,1,128,128]{6,5,4,3,2,1,0:T(8,128)(2,1)S(1)}, u32[]{:S(2)}, u32[]{:S(2)}) collective-permute-start(bf16[1,1,1,1,1,128,128]{6,5,4,3,2,1,0:T(8,128)(2,1)S(1)} %constant_dynamic-slice_fusion), channel_id=1, source_target_pairs={{1,0},{0,1},{3,2},{2,3},{5,4},{4,5},{7,6},{6,7},{9,8},{8,9},{11,10... | collective-permute-start | bytes 98312 | tf_op jit(solution)/shard_map/ppermute | solution.py:262
  5.5 0.0 copy-start
  5.5 1.8 %pick.1 = (bf16[2,128,256]{2,1,0:T(8,128)(2,1)S(1)}, s32[1,128]{1,0:T(1,128)S(1)}) custom-call(s32[1,1,2,1,2,4]{5,4,3,2,1,0:T(2,128)} %bitcast.4, s32[1,1,64]{2,1,0:T(1,128)} %owners.1, bf16[1,2,128,8192]{3,2,1,0:T(8,128)(2,1)} %activations.1), custom_call_target="tpu_custom_call" | custom-call | tf_op jit(solution)/shard_map/pick/pallas_call | solution.py:269
  7.3 2.1 %clear.1 = bf16[1,1,2048,1024]{3,2,1,0:T(8,128)(2,1)} custom-call(bf16[2,128,256]{2,1,0:T(8,128)(2,1)S(1)} %get-tuple-element.169.picked.after), custom_call_target="tpu_custom_call" | custom-call | bytes 4194304 | tf_op jit(solution)/shard_map/clear/pallas_call | solution.py:288
  9.5 0.7 %collective-permute-done.26.refs_2_ = bf16[1,1,1,1,1,128,128]{6,5,4,3,2,1,0:T(8,128)(2,1)S(1)} collective-permute-done((bf16[1,1,1,1,1,128,128]{6,5,4,3,2,1,0:T(8,128)(2,1)S(1)}, bf16[1,1,1,1,1,128,128]{6,5,4,3,2,1,0:T(8,128)(2,1)S(1)}, u32[]{:S(2)}, u32[]{:S(2)}) %collective-permute-start.26) | collective-permute-done | bytes 32800 | tf_op jit(solution)/shard_map/ppermute | solution.py:262
  10.2 0.0 collective-permute-done.25.refs_1_
  10.2 0.6 %collective-permute-done.24.refs_0_ = bf16[1,2,128,512]{3,2,1,0:T(8,128)(2,1)S(1)} collective-permute-done((bf16[1,2,128,512]{3,2,1,0:T(8,128)(2,1)}, bf16[1,2,128,512]{3,2,1,0:T(8,128)(2,1)S(1)}, u32[]{:S(2)}, u32[]{:S(2)}) %collective-permute-start.24) | collective-permute-done | bytes 262176 | tf_op jit(solution)/shard_map/ppermute | solution.py:256
  10.8 0.0 copy-done
  10.8 0.3 %multiply.1 = (f32[128,128]{1,0:T(8,128)S(1)}, f32[128,128]{1,0:T(8,128)S(1)}, f32[128,128]{1,0:T(8,128)S(1)}, f32[128,128]{1,0:T(8,128)S(1)}, bf16[128,128]{1,0...) custom-call(s32[1,128]{1,0:T(1,128)S(1)} %get-tuple-element.168.plan, ...), custom_call_target="tpu_custom_call" | custom-call | tf_op jit(solution)/shard_map/multiply/pallas_call | solution.py:314
  11.1 8.8 %conditional.1 = (bf16[1,1,2048,1024]{3,2,1,0:T(8,128)(2,1)}) conditional(s32[]{:T(128)} %bitcast.1, (bf16[128,128]{1,0:T(8,128)(2,1)S(1)}, bf16[128,128]{1,0:T(8,128)(2,1)S(1)}, bf16[128,128]{1,0:T(8,128)(2,1)S(1)}, s32[1,128]{1,0:T(1,128)S(1)}, bf16[128,128]{1,0:T(8,128)(2,1)S(1)}, ...), branch_computations={%region_0.1_spmd, %region_1.2_spmd, %region_2.3_spmd, %region_3.4_... | conditional | bytes 786560 | solution.py:367
  11.2 2.8 %collective-permute-start.2 = (bf16[128,128]{1,0:T(8,128)(2,1)S(1)}, bf16[128,128]{1,0:T(8,128)(2,1)S(1)}, u32[]{:S(2)}, u32[]{:S(2)}) collective-permute-start(bf16[128,128]{1,0:T(8,128)(2,1)S(1)} %get-tuple-element.112), channel_id=1, source_target_pairs={{0,4},{2,6},{4,2},{6,0},{8,10},{10,12},{12,14},{14,8},{16,20},{18,... | collective-permute-start | bytes 98312 | tf_op jit(solution)/shard_map/cond/branch_0_fun/ppermute | solution.py:347
  14.0 1.1 %collective-permute-start = (bf16[128,128]{1,0:T(8,128)(2,1)S(1)}, bf16[128,128]{1,0:T(8,128)(2,1)S(1)}, u32[]{:S(2)}, u32[]{:S(2)}) collective-permute-start(bf16[128,128]{1,0:T(8,128)(2,1)S(1)} %get-tuple-element.102), channel_id=1, source_target_pairs={{0,6},{2,4},{4,0},{6,2},{8,12},{10,14},{12,8},{14,10},{16,22},{18,... | collective-permute-start | bytes 98312 | tf_op jit(solution)/shard_map/cond/branch_0_fun/ppermute | solution.py:347
  15.1 0.5 %collective-permute-start.1 = (bf16[128,128]{1,0:T(8,128)(2,1)S(1)}, bf16[128,128]{1,0:T(8,128)(2,1)S(1)}, u32[]{:S(2)}, u32[]{:S(2)}) collective-permute-start(bf16[128,128]{1,0:T(8,128)(2,1)S(1)} %get-tuple-element.103), channel_id=1, source_target_pairs={{0,2},{2,0},{4,6},{6,4},{8,14},{10,8},{12,10},{14,12},{16,18},{18,... | collective-permute-start | bytes 98312 | tf_op jit(solution)/shard_map/cond/branch_0_fun/ppermute | solution.py:347
  15.6 1.5 %collective-permute-done.2.refs_1_ = bf16[128,128]{1,0:T(8,128)(2,1)S(1)} collective-permute-done((bf16[128,128]{1,0:T(8,128)(2,1)S(1)}, bf16[128,128]{1,0:T(8,128)(2,1)S(1)}, u32[]{:S(2)}, u32[]{:S(2)}) %collective-permute-start.2) | collective-permute-done | bytes 32800 | tf_op jit(solution)/shard_map/cond/branch_0_fun/ppermute | solution.py:347
  17.1 0.7 %place.9.refs_2_ = bf16[1,1,2048,1024]{3,2,1,0:T(8,128)(2,1)} custom-call(s32[1,128]{1,0:T(1,128)S(1)} %get-tuple-element.101.plan, bf16[128,128]{1,0:T(8,128)(2,1)S(1)} %get-tuple-element.104.refs_0_, bf16[128,128]{1,0:T(8,128)(2,1)S(1)} %collective-permute-done.2.refs_1_, ...), custom_call_target="tpu_custom_call", output_to_operand_aliasing={{}: (3, {})} | custom-call | tf_op jit(solution)/shard_map/cond/branch_0_fun/place/pallas_call | solution.py:325
  17.8 1.0 %collective-permute-done.refs_0_ = bf16[128,128]{1,0:T(8,128)(2,1)S(1)} collective-permute-done((bf16[128,128]{1,0:T(8,128)(2,1)S(1)}, bf16[128,128]{1,0:T(8,128)(2,1)S(1)}, u32[]{:S(2)}, u32[]{:S(2)}) %collective-permute-start) | collective-permute-done | bytes 32800 | tf_op jit(solution)/shard_map/cond/branch_0_fun/ppermute | solution.py:347
  18.8 0.3 %collective-permute-done.1.refs_1_ = bf16[128,128]{1,0:T(8,128)(2,1)S(1)} collective-permute-done((bf16[128,128]{1,0:T(8,128)(2,1)S(1)}, bf16[128,128]{1,0:T(8,128)(2,1)S(1)}, u32[]{:S(2)}, u32[]{:S(2)}) %collective-permute-start.1) | collective-permute-done | bytes 32800 | tf_op jit(solution)/shard_map/cond/branch_0_fun/ppermute | solution.py:347
  19.1 0.7 %place.10 = bf16[1,1,2048,1024]{3,2,1,0:T(8,128)(2,1)} custom-call(s32[1,128]{1,0:T(1,128)S(1)} %get-tuple-element.101.plan, bf16[128,128]{1,0:T(8,128)(2,1)S(1)} %collective-permute-done.refs_0_, bf16[128,128]{1,0:T(8,128)(2,1)S(1)} %collective-permute-done.1.refs_1_, bf16[1,1,2048,1024]{3,2,1,0:T(8,128)(2,1)} %place.9.refs_2_), custom_call_target="tpu_custom_call", output_to_operand_aliasing={{}: (3, {})} | custom-call | tf_op jit(solution)/shard_map/cond/branch_0_fun/place/pallas_call | solution.py:325
Async XLA Ops:
  0.0 10.2 %collective-permute-start.25 = (bf16[1,2,128,512]{3,2,1,0:T(8,128)(2,1)}, bf16[1,2,128,512]{3,2,1,0:T(8,128)(2,1)S(1)}, u32[]{:S(2)}, u32[]{:S(2)}) collective-permute-start(bf16[1,2,128,512]{3,2,1,0:T(8,128)(2,1)} %param.14), channel_id=1, source_target_pairs={{9,0},{8,1},{17,8},{16,9},{25,16},{24,17},{1,24},{0,25},{11,2},{10... | collective-permute-start | bytes 786440 | tf_op jit(solution)/shard_map/ppermute | solution.py:256
  3.3 7.5 %collective-permute-start.24 = (bf16[1,2,128,512]{3,2,1,0:T(8,128)(2,1)}, bf16[1,2,128,512]{3,2,1,0:T(8,128)(2,1)S(1)}, u32[]{:S(2)}, u32[]{:S(2)}) collective-permute-start(bf16[1,2,128,512]{3,2,1,0:T(8,128)(2,1)} %param.14), channel_id=1, source_target_pairs={{8,0},{9,1},{16,8},{17,9},{24,16},{25,17},{0,24},{1,25},{10,2},{11... | collective-permute-start | bytes 786440 | tf_op jit(solution)/shard_map/ppermute | solution.py:256
  4.9 5.3 %collective-permute-start.26 = (bf16[1,1,1,1,1,128,128]{6,5,4,3,2,1,0:T(8,128)(2,1)S(1)}, bf16[1,1,1,1,1,128,128]{6,5,4,3,2,1,0:T(8,128)(2,1)S(1)}, u32[]{:S(2)}, u32[]{:S(2)}) collective-permute-start(bf16[1,1,1,1,1,128,128]{6,5,4,3,2,1,0:T(8,128)(2,1)S(1)} %constant_dynamic-slice_fusion), channel_id=1, source_target_pairs={{1,0},{0,1},{3,2},{2,3},{5,4},{4,5},{7,6},{6,7},{9,8},{8,9},{11,10... | collective-permute-start | bytes 98312 | tf_op jit(solution)/shard_map/ppermute | solution.py:262
  5.5 5.3 %copy-start = (bf16[1,1,1,2,1,128,128]{6,5,4,3,2,1,0:T(8,128)(2,1)S(1)}, bf16[1,1,1,2,1,128,128]{6,5,4,3,2,1,0:T(8,128)(2,1)}, u32[]{:S(2)}) copy-start(bf16[1,1,1,2,1,128,128]{6,5,4,3,2,1,0:T(8,128)(2,1)} %error.1) | copy-start | bytes 196612
  11.2 5.9 %collective-permute-start.2 = (bf16[128,128]{1,0:T(8,128)(2,1)S(1)}, bf16[128,128]{1,0:T(8,128)(2,1)S(1)}, u32[]{:S(2)}, u32[]{:S(2)}) collective-permute-start(bf16[128,128]{1,0:T(8,128)(2,1)S(1)} %get-tuple-element.112), channel_id=1, source_target_pairs={{0,4},{2,6},{4,2},{6,0},{8,10},{10,12},{12,14},{14,8},{16,20},{18,... | collective-permute-start | bytes 98312 | tf_op jit(solution)/shard_map/cond/branch_0_fun/ppermute | solution.py:347
  14.0 4.8 %collective-permute-start = (bf16[128,128]{1,0:T(8,128)(2,1)S(1)}, bf16[128,128]{1,0:T(8,128)(2,1)S(1)}, u32[]{:S(2)}, u32[]{:S(2)}) collective-permute-start(bf16[128,128]{1,0:T(8,128)(2,1)S(1)} %get-tuple-element.102), channel_id=1, source_target_pairs={{0,6},{2,4},{4,0},{6,2},{8,12},{10,14},{12,8},{14,10},{16,22},{18,... | collective-permute-start | bytes 98312 | tf_op jit(solution)/shard_map/cond/branch_0_fun/ppermute | solution.py:347
  15.1 4.1 %collective-permute-start.1 = (bf16[128,128]{1,0:T(8,128)(2,1)S(1)}, bf16[128,128]{1,0:T(8,128)(2,1)S(1)}, u32[]{:S(2)}, u32[]{:S(2)}) collective-permute-start(bf16[128,128]{1,0:T(8,128)(2,1)S(1)} %get-tuple-element.103), channel_id=1, source_target_pairs={{0,2},{2,0},{4,6},{6,4},{8,14},{10,8},{12,10},{14,12},{16,18},{18,... | collective-permute-start | bytes 98312 | tf_op jit(solution)/shard_map/cond/branch_0_fun/ppermute | solution.py:347
